TPU v7x, 512 devices: a whole 4x8x8 slice. The times are simulated.
512 devices in a mesh: seq: 64 (over y, z_lo, x), wt: 8 (over z_hi, core).
Axes of the slice: x: 4, y: 8, z: 8 (z_hi: 4, z_lo: 2; z = z_hi * 2 + z_lo), core: 2. Of those that a mesh axis runs over, the one named last changes fastest.
Arguments:
- normed_input_rows: bfloat16 [2, 8, 4096, 4096], P(None, 'wt', 'seq'), may hold values from -6 to 6
- queries: bfloat16 [2, 8, 4096, 4096], P(None, 'wt', 'seq'), may hold values from -150 to 150
- rotated_key_rows: bfloat16 [2, 8, 4096, 512], P(None, 'wt', 'seq'), may hold values from -6 to 6
- frozen_value_matrix: bfloat16 [4096, 512], P('wt'), may hold values from -0.09375 to 0.09375
- adapter_down_weight: bfloat16 [4096, 8], replicated, may hold values from -0.09375 to 0.09375
- adapter_up_weight: bfloat16 [8, 512], replicated, may hold values from -1.1953125 to 1.1953125
- output_gradient: bfloat16 [2, 8, 4096, 4096], P(None, 'wt', 'seq'), may hold values from -6 to 6
- shifted_head_mask: int32 [32], replicated, may hold values from 0 to 1, as said below
Outputs:
- query_grad: bfloat16 [2, 8, 4096, 4096], P(None, 'wt', 'seq')
- key_grad: bfloat16 [2, 8, 4096, 512], P(None, 'wt', 'seq')
- down_grad: float32 [4096, 8], replicated
- up_grad: float32 [8, 512], replicated
Inputs may be any that keep to these rules, and one draw needn't show every extreme that they name: `shifted_head_mask`: exactly half of the 32 query heads are 1; which ones varies.
All inputs are finite; a program needn't handle non-finite values.
Results may differ from a plain program's by a relative error of at most 0.028.
Values may be sent and summed in bfloat16 or wider, within the bound.
No kernel may reach another device: no remote copies, remote signals or barrier semaphores. Data moves between devices by JAX's collectives and lax.ppermute only.
A program may use at most 64 MiB of HBM per device.

v0:
```python
import math

import jax
import jax.numpy as jnp
from jax import lax
from jax.sharding import PartitionSpec as P

HEAD_WIDTH = 128
GROUP = 1024


adapter_scale = 2.0


def passed_along(block, axis, distance):
    devices = range(lax.axis_size(axis))
    route = [((i - distance) % len(devices), i) for i in devices]
    return lax.ppermute(block, axis, route)


def attend_block(query_rows, key_rows, value_rows, grad_rows, offset):
    scale_factor = 1.0 / math.sqrt(query_rows.shape[1])
    scores = jnp.dot(query_rows, key_rows.T, preferred_element_type=jnp.float32) * scale_factor
    query_place = offset + jnp.arange(query_rows.shape[0], dtype=jnp.int32)[:, None]
    key_place = jnp.arange(key_rows.shape[0], dtype=jnp.int32)[None, :]
    scores = jnp.where(key_place <= query_place, scores, -jnp.inf)
    row_max = jnp.max(scores, axis=1, keepdims=True)
    raised = jnp.exp(scores - row_max)
    weights = raised / jnp.sum(raised, axis=1, keepdims=True)
    rounded = weights.astype(jnp.bfloat16)
    output = jnp.dot(rounded, value_rows, preferred_element_type=jnp.float32)
    deltas = jnp.sum(grad_rows.astype(jnp.float32) * output, axis=1, keepdims=True)
    value_grad = jnp.dot(rounded.T, grad_rows, preferred_element_type=jnp.float32)
    weight_grad = jnp.dot(grad_rows, value_rows.T, preferred_element_type=jnp.float32)
    score_grad = (weights * (weight_grad - deltas)).astype(jnp.bfloat16)
    query_grad = jnp.dot(score_grad, key_rows, preferred_element_type=jnp.float32) * scale_factor
    key_grad = jnp.dot(score_grad.T, query_rows, preferred_element_type=jnp.float32) * scale_factor
    return (query_grad, key_grad, value_grad)


def group_grads(stacked):
    middle = stacked.shape[1] // 2
    early_grads = attend_block(
        stacked[0, :middle], stacked[1, :middle], stacked[2, :middle], stacked[3, :middle], 0
    )
    later_grads = attend_block(
        stacked[0, middle:], stacked[1], stacked[2], stacked[3, middle:], middle
    )
    filler = jnp.zeros((middle, stacked.shape[2]), jnp.float32)
    query_part = jnp.concatenate([early_grads[0], later_grads[0]], axis=0)
    key_part = later_grads[1] + jnp.concatenate([early_grads[1], filler], axis=0)
    value_part = later_grads[2] + jnp.concatenate([early_grads[2], filler], axis=0)
    return jnp.stack([query_part, key_part, value_part]).astype(jnp.bfloat16)


def regroup_rows(stacked):
    return lax.all_to_all(stacked, "seq", split_axis=1, concat_axis=1, tiled=True)


def body(
    normed_input_rows,
    queries,
    rotated_key_rows,
    frozen_value_matrix,
    adapter_down_weight,
    adapter_up_weight,
    output_gradient,
    shifted_head_mask,
):
    seq_devices = lax.axis_size("seq")
    weight_devices = lax.axis_size("wt")
    sequences = normed_input_rows.shape[0]
    local_rows = normed_input_rows.shape[2]
    model_width = normed_input_rows.shape[3]
    head_size = HEAD_WIDTH
    query_heads = queries.shape[3] // head_size
    value_heads = rotated_key_rows.shape[3] // head_size
    group_ratio = query_heads // value_heads
    local_tokens = sequences * local_rows
    span_rows = local_rows * seq_devices
    half_group = GROUP // 2
    token_positions = normed_input_rows.reshape(local_tokens, model_width)
    frozen_value_term = jnp.dot(
        token_positions,
        lax.all_gather(frozen_value_matrix, "wt", axis=0, tiled=True),
        preferred_element_type=jnp.float32,
    )
    low_rank_rows = jnp.dot(
        token_positions, adapter_down_weight, preferred_element_type=jnp.float32
    )
    adapter_up_matrix = adapter_up_weight.astype(jnp.float32)
    adapter_value_term = jnp.dot(low_rank_rows, adapter_up_matrix, precision=lax.Precision.HIGHEST)
    value_states = (frozen_value_term + adapter_scale * adapter_value_term).astype(jnp.bfloat16)

    def arranged(source, head_count):
        reordered = jnp.transpose(
            source.reshape(sequences, local_rows, head_count, head_size), (2, 0, 1, 3)
        )
        if head_count < query_heads:
            reordered = jnp.repeat(reordered, group_ratio, axis=0)
        return reordered.reshape(seq_devices, local_rows, head_size)

    outgoing = jnp.stack(
        [
            arranged(queries, query_heads),
            arranged(rotated_key_rows, value_heads),
            arranged(value_states, value_heads),
            arranged(output_gradient, query_heads),
        ]
    )
    incoming = regroup_rows(outgoing)
    local_part = incoming.reshape(4, span_rows, head_size)
    query_head = lax.axis_index("seq") // sequences
    shifted = lax.dynamic_index_in_dim(shifted_head_mask, query_head, 0, keepdims=False)
    group_count = span_rows // GROUP
    leading = local_part[:, :half_group]
    fetched = passed_along(leading, "wt", -1)
    rolled = jnp.concatenate([local_part[:, half_group:], fetched], axis=1)
    working = jnp.where(shifted > 0, rolled, local_part)
    blocks = jnp.transpose(working.reshape(4, group_count, GROUP, head_size), (1, 0, 2, 3))
    gradients = lax.map(group_grads, blocks)
    gradients = jnp.transpose(gradients, (1, 0, 2, 3)).reshape(3, group_count * GROUP, head_size)
    trailing = gradients[:, span_rows - half_group :]
    arrived = passed_along(trailing, "wt", 1)
    unrolled = jnp.concatenate([arrived, gradients[:, : span_rows - half_group]], axis=1)
    result = jnp.where(shifted > 0, unrolled, gradients)
    returned = regroup_rows(result.reshape(3, seq_devices, local_rows, head_size))
    by_head = returned.reshape(3, query_heads, sequences, local_rows, head_size)
    query_grad = jnp.transpose(by_head[0], (1, 2, 0, 3)).reshape(
        sequences, 1, local_rows, query_heads * head_size
    )
    summed = (
        by_head[1:]
        .astype(jnp.float32)
        .reshape(2, value_heads, group_ratio, sequences, local_rows, head_size)
    )
    summed = jnp.transpose(jnp.sum(summed, axis=2), (0, 2, 3, 1, 4))
    key_grad = (
        summed[0].astype(jnp.bfloat16).reshape(sequences, 1, local_rows, value_heads * head_size)
    )
    value_grad = summed[1].reshape(local_tokens, value_heads * head_size)
    pulled = jnp.dot(value_grad, adapter_up_matrix.T, precision=lax.Precision.HIGHEST).astype(
        jnp.bfloat16
    )
    local_down = jnp.dot(token_positions.T, pulled, preferred_element_type=jnp.float32)
    local_up = jnp.dot(low_rank_rows.T, value_grad, precision=lax.Precision.HIGHEST)
    summed_down, summed_up = lax.psum((local_down, local_up), ("seq", "wt"))
    token_total = local_tokens * seq_devices * weight_devices
    scale_factor = adapter_scale / math.sqrt(token_total)
    return (query_grad, key_grad, summed_down * scale_factor, summed_up * scale_factor)


def solution(mesh):
    return jax.shard_map(
        body,
        mesh=mesh,
        in_specs=(
            P(None, "wt", "seq", None),
            P(None, "wt", "seq", None),
            P(None, "wt", "seq", None),
            P("wt", None),
            P(),
            P(),
            P(None, "wt", "seq", None),
            P(),
        ),
        out_specs=(P(None, "wt", "seq", None), P(None, "wt", "seq", None), P(), P()),
        check_vma=False,
    )
```

profile of v0, /device:TPU:1, one launch (start us, length us, event | category | flops | bytes accessed | tf_op | source)
XLA Modules:
  0.0 606.2 jit_solution(17848895670040987514)
XLA Ops:
  8.0 1.5 copy.68
  11.4 61.0 %all-gather.2.cloned.1.call-done = bf16[4096,512]{1,0:T(8,128)(2,1)} async-done(((bf16[512,512]{1,0:T(8,128)(2,1)}), bf16[4096,512]{1,0:T(8,128)(2,1)}) %all-gather.2.cloned.1.call-update) | async-done | bytes 4194320 | tf_op jit(solution)/shard_map/all_gather | solution.py:85
  72.4 2.9 fusion.31
  76.8 1.4 copy.49
  78.2 103.6 %all_to_all.10 = bf16[4,64,64,128]{3,2,0,1:T(8,128)(2,1)S(1)} all-to-all(bf16[4,64,64,128]{3,2,0,1:T(8,128)(2,1)S(1)} %copy.49), channel_id=1, replica_groups=mesh['seq'=64,'wt'=8] {'seq'}, dimensions={1} | all-to-all | bytes 8388608 | tf_op jit(solution)/shard_map/all_to_all | solution.py:57
  181.8 1.3 copy.50
  183.1 1.9 copy-done.1
  185.0 4.7 collective-permute-start
  191.0 2.3 slice.69
  193.3 6.5 %collective-permute-done = bf16[4,512,128]{2,1,0:T(8,128)(2,1)S(1)} collective-permute-done((bf16[4,512,128]{2,1,0:T(8,128)(2,1)S(1)}, bf16[4,512,128]{2,1,0:T(8,128)(2,1)S(1)}, u32[]{:S(2)}, u32[]{:S(2)}) %collective-permute-start) | collective-permute-done | bytes 524320 | tf_op jit(solution)/shard_map/ppermute | solution.py:18
  200.2 2.4 fusion.21
  202.5 37.1 %while.10 = (s32[]{:T(128)}, bf16[4,3,1024,128]{3,2,0,1:T(8,128)(2,1)}, bf16[4,4,1024,128]{3,2,0,1:T(8,128)(2,1)}, s32[]{:T(128)}) while((s32[]{:T(128)}, bf16[4,3,1024,128]{3,2,0,1:T(8,128)(2,1)}, bf16[4,4,1024,128]{3,2,0,1:T(8,128)(2,1)}, s32[]{:T(128)}) %tuple.35), condition=%wide.region_7.8_spmd, body=%wide.region_0.7_spmd.sunk | while | flops 1222702592 | bytes 36213304 | solution.py:121
  202.5 1.3 constant_dynamic-slice_fusion.2
  210.8 1.0 fusion.94
  211.8 1.3 constant_dynamic-slice_fusion.2
  220.0 1.1 fusion.94
  221.1 1.3 constant_dynamic-slice_fusion.2
  229.3 1.0 fusion.94
  230.3 1.3 constant_dynamic-slice_fusion.2
  238.6 1.1 fusion.94
  239.6 1.0 slice.71
  240.7 1.9 collective-permute-start.1
  242.6 2.0 slice.72
  244.6 2.7 collective-permute-done.1
  247.5 2.3 broadcast_select_fusion
  250.5 79.0 %all_to_all.11 = bf16[3,64,64,128]{3,2,0,1:T(8,128)(2,1)S(1)} all-to-all(bf16[3,64,64,128]{3,2,0,1:T(8,128)(2,1)S(1)} %copy.54), channel_id=1, replica_groups=mesh['seq'=64,'wt'=8] {'seq'}, dimensions={1} | all-to-all | bytes 6291456 | tf_op jit(solution)/shard_map/all_to_all | solution.py:57
  330.1 1.0 copy-done.3
  332.0 0.9 convolution_bitcast_fusion
  332.9 105.1 %psum.15 = f32[8,512]{1,0:T(8,128)S(1)} all-reduce(f32[8,512]{1,0:T(8,128)S(1)} %fusion.24), channel_id=1, replica_groups=mesh['seq'=64,'wt'=8] {'seq','wt'}, use_global_device_ids=true, to_apply=%region_10.11 | all-reduce | flops 4096 | bytes 32768 | tf_op jit(solution)/shard_map/psum | solution.py:147
  440.2 1.3 reshape.136
  441.4 156.4 %all-reduce.4.cloned.1.call-done = f32[4096,8]{0,1:T(8,128)} async-done(((f32[4096,8]{0,1:T(8,128)}), f32[4096,8]{0,1:T(8,128)}) %all-reduce.4.cloned.1.call-update) | async-done | bytes 131088 | tf_op jit(solution)/shard_map/psum | solution.py:147
  597.8 1.6 broadcast_multiply_fusion
  (130 shorter events, 36.6 us)
Async XLA Ops:
  7.2 3.8 copy-start
  7.2 65.2 %all-gather.2.cloned.1.call-start = ((), (), s32[]{:S(2)}) async-start(), calls=%async_computation.2 | async-start | bytes 4718592 | tf_op jit(solution)/shard_map/all_gather | solution.py:85
  7.9 589.9 %all-reduce.4.cloned.1.call-start = ((), (), s32[]{:S(2)}) async-start(), calls=%async_computation.3 | async-start | bytes 262144 | tf_op jit(solution)/shard_map/psum | solution.py:147
  8.0 2.0 copy-start.4
  10.0 0.9 copy-start.5
  10.0 1.0 copy-start.6
  11.0 64.3 %copy-start.7 = (bf16[8,512]{1,0:T(8,128)(2,1)S(1)}, bf16[8,512]{1,0:T(8,128)(2,1)}, u32[]{:S(2)}) copy-start(bf16[8,512]{1,0:T(8,128)(2,1)} %param.15) | copy-start | bytes 24580
  181.8 8.0 %copy-start.8 = (s32[32]{0:T(128)S(1)}, s32[32]{0:T(128)}, u32[]{:S(2)}) copy-start(s32[32]{0:T(128)} %param.17) | copy-start | bytes 388
  183.1 1.9 copy-start.1
  185.0 14.9 %collective-permute-start = (bf16[4,512,128]{2,1,0:T(8,128)(2,1)S(1)}, bf16[4,512,128]{2,1,0:T(8,128)(2,1)S(1)}, u32[]{:S(2)}, u32[]{:S(2)}) collective-permute-start(bf16[4,512,128]{2,1,0:T(8,128)(2,1)S(1)} %slice.70), channel_id=1, source_target_pairs={{1,0},{2,1},{3,2},{4,3},{5,4},{6,5},{7,6},{0,7},{9,8},{10,9},{11,1... | collective-permute-start | bytes 1572872 | tf_op jit(solution)/shard_map/ppermute | solution.py:18
  193.3 6.8 %copy-start.2 = (bf16[4,64,64,128]{3,2,1,0:T(8,128)(2,1)S(1)}, bf16[4,64,64,128]{3,2,1,0:T(8,128)(2,1)}, u32[]{:S(2)}) copy-start(bf16[4,64,64,128]{3,2,1,0:T(8,128)(2,1)} %copy-done.1) | copy-start | bytes 12582916
  240.7 6.6 %collective-permute-start.1 = (bf16[3,512,128]{2,1,0:T(8,128)(2,1)S(1)}, bf16[3,512,128]{2,1,0:T(8,128)(2,1)S(1)}, u32[]{:S(2)}, u32[]{:S(2)}) collective-permute-start(bf16[3,512,128]{2,1,0:T(8,128)(2,1)S(1)} %slice.71), channel_id=1, source_target_pairs={{7,0},{0,1},{1,2},{2,3},{3,4},{4,5},{5,6},{6,7},{15,8},{8,9},{9,10... | collective-permute-start | bytes 1179656 | tf_op jit(solution)/shard_map/ppermute | solution.py:18
  329.5 1.7 copy-start.3
  331.2 108.3 %slice-start = ((bf16[3,64,64,128]{3,2,0,1:T(8,128)(2,1)}), bf16[1,64,64,128]{3,2,0,1:T(8,128)(2,1)S(1)}, s32[]{:S(2)}) async-start(bf16[3,64,64,128]{3,2,0,1:T(8,128)(2,1)} %copy-done.3), calls=%async_computation.4 | async-start | bytes 2097152 | tf_op jit(solution)/shard_map/slice | solution.py:129
Sparse Core Ops, SparseCore 0:
  10.2 62.1 all-gather.1
  333.0 264.7 all-reduce.3
where the time goes:
time: 606 us
  blocking collectives  288 us (48%)
  waiting for transfers between devices  227 us (37%)
  local copies, waits for them, and re-layouts  26.3 us (4%)
  matrix products  24.7 us (4%)
  other arithmetic  18 us (3%)
  between operations  15.1 us (2%)
  starting transfers between devices  6.71 us (1%)
    all_to_all x2, blocking collectives, regroup_rows(): lax.all_to_all(stacked, 'seq', split_axis=1, concat_axis=1, tiled=True)  183 us
    psum x1, waiting for transfers between devices, body(): summed_down, summed_up = lax.psum((local_down, local_up), ('seq', 'wt'))  156 us
    psum x1, blocking collectives, body(): summed_down, summed_up = lax.psum((local_down, local_up), ('seq', 'wt'))  105 us
    all_gather x1, waiting for transfers between devices, body(): lax.all_gather(frozen_value_matrix, 'wt', axis=0, tiled=True)  61 us
  transfers between devices with their start and end apart: 4, of which 4 were waited for; matrix products, arithmetic and copies ran while one was open for 2% of the time, Pallas kernels for 0%

commit v1 on v0

v1 whole, which is shorter than its diff:
```python
import math

import jax
import jax.numpy as jnp
from jax import lax
from jax.experimental import pallas as pl
from jax.experimental.pallas import tpu as pltpu
from jax.sharding import PartitionSpec as P

HEAD = 128
HALF = 512
TILE = 256
RATIO = 8
KV = 4
RANK = 8
UNITS = 8
SCALE = 1.0 / math.sqrt(HEAD)
ADAPTER_SCALE = 2.0
VMEM = 48 * 1024 * 1024
F32 = jnp.float32
BF16 = jnp.bfloat16


def dot_nt(a, b):
    return lax.dot_general(a, b, (((1,), (1,)), ((), ())), preferred_element_type=F32)


def dot_nn(a, b):
    return lax.dot_general(a, b, (((1,), (0,)), ((), ())), preferred_element_type=F32)


def weights_kernel(flags, q_ref, k_ref, kp_ref, p_ref):
    head = pl.program_id(0)
    factor = SCALE * math.log2(math.e)

    def tiles(full):
        for r in range(HALF // TILE):
            cols = pl.ds(r * TILE, TILE)
            keys = (r + 1) * TILE
            q = q_ref[cols, :]
            own = dot_nt(k_ref[pl.ds(0, keys), :], q)
            key_place = lax.broadcasted_iota(jnp.int32, (keys, TILE), 0)
            query_place = lax.broadcasted_iota(jnp.int32, (keys, TILE), 1) + r * TILE
            own = jnp.where(key_place <= query_place, own, -jnp.inf)
            top = jnp.max(own, axis=0, keepdims=True)
            if full:
                prev = dot_nt(kp_ref[...], q)
                top = jnp.maximum(top, jnp.max(prev, axis=0, keepdims=True))
            own = jnp.exp2((own - top) * factor)
            total = jnp.sum(own, axis=0, keepdims=True)
            if full:
                prev = jnp.exp2((prev - top) * factor)
                total = total + jnp.sum(prev, axis=0, keepdims=True)
            inverse = 1.0 / total
            p_ref[0, pl.ds(HALF, keys), cols] = (own * inverse).astype(BF16)
            if full:
                p_ref[0, pl.ds(0, HALF), cols] = (prev * inverse).astype(BF16)

    @pl.when(flags[head] > 0)
    def _():
        tiles(True)

    @pl.when(flags[head] == 0)
    def _():
        tiles(False)


def value_grad_kernel(flags, p_ref, do_ref, out_ref, acc):
    head = pl.program_id(0)

    @pl.when(head == 0)
    def _():
        acc[...] = jnp.zeros_like(acc)

    acc[pl.ds(HALF, TILE), :] += dot_nn(p_ref[0, pl.ds(HALF, TILE), :], do_ref[...])
    acc[pl.ds(HALF + TILE, TILE), :] += dot_nn(
        p_ref[0, pl.ds(HALF + TILE, TILE), pl.ds(TILE, TILE)], do_ref[pl.ds(TILE, TILE), :]
    )

    @pl.when(flags[head] > 0)
    def _():
        acc[pl.ds(0, HALF), :] += dot_nn(p_ref[0, pl.ds(0, HALF), :], do_ref[...])

    @pl.when(head == RATIO - 1)
    def _():
        out_ref[:, pl.ds(0, HEAD)] = acc[pl.ds(HALF, HALF), :].astype(BF16)
        out_ref[:, pl.ds(HEAD, HEAD)] = acc[pl.ds(0, HALF), :].astype(BF16)


def score_grad_kernel(flags, p_ref, q_ref, k_ref, kp_ref, do_ref, v_ref, out_ref, acc, kt):
    head = pl.program_id(0)

    @pl.when(head == 0)
    def _():
        acc[...] = jnp.zeros_like(acc)
        kt[:, pl.ds(0, HALF)] = kp_ref[...].astype(F32).T.astype(BF16)
        kt[:, pl.ds(HALF, HALF)] = k_ref[...].astype(F32).T.astype(BF16)

    def tiles(full):
        for r in range(HALF // TILE):
            cols = pl.ds(r * TILE, TILE)
            keys = (r + 1) * TILE
            q = q_ref[cols, :]
            do = do_ref[cols, :]
            p_own = p_ref[0, pl.ds(HALF, keys), cols].astype(F32)
            d_own = dot_nt(v_ref[pl.ds(0, keys), pl.ds(0, HEAD)], do)
            delta = jnp.sum(p_own * d_own, axis=0, keepdims=True)
            if full:
                p_prev = p_ref[0, pl.ds(0, HALF), cols].astype(F32)
                d_prev = dot_nt(v_ref[:, pl.ds(HEAD, HEAD)], do)
                delta = delta + jnp.sum(p_prev * d_prev, axis=0, keepdims=True)
            s_own = (p_own * (d_own - delta)).astype(BF16)
            dq = dot_nn(kt[:, pl.ds(HALF, keys)], s_own)
            acc[pl.ds(HALF, keys), :] += dot_nn(s_own, q)
            if full:
                s_prev = (p_prev * (d_prev - delta)).astype(BF16)
                dq = dq + dot_nn(kt[:, pl.ds(0, HALF)], s_prev)
                acc[pl.ds(0, HALF), :] += dot_nn(s_prev, q)
            place = pl.ds(pl.multiple_of(head * HEAD, HEAD), HEAD)
            out_ref[cols, place] = (dq * SCALE).T.astype(BF16)

    @pl.when(flags[head] > 0)
    def _():
        tiles(True)

    @pl.when(flags[head] == 0)
    def _():
        tiles(False)

    @pl.when(head == RATIO - 1)
    def _():
        out_ref[:, pl.ds(RATIO * HEAD, HEAD)] = (acc[pl.ds(HALF, HALF), :] * SCALE).astype(BF16)
        out_ref[:, pl.ds((RATIO + 1) * HEAD, HEAD)] = (acc[pl.ds(0, HALF), :] * SCALE).astype(BF16)


def values_kernel(x_ref, xh_ref, w_ref, low_ref, up_ref, out_ref, acc):
    step = pl.program_id(0)
    rows = x_ref.shape[0]

    @pl.when(step == 0)
    def _():
        up = up_ref[...].astype(F32)
        acc[...] = ADAPTER_SCALE * lax.dot_general(
            low_ref[...],
            up,
            (((1,), (0,)), ((), ())),
            preferred_element_type=F32,
            precision=lax.Precision.HIGHEST,
        )

    acc[pl.ds(0, rows), :] += dot_nn(x_ref[...], w_ref[...])
    acc[pl.ds(rows, rows), :] += dot_nn(xh_ref[...], w_ref[...])

    @pl.when(step == pl.num_programs(0) - 1)
    def _():
        part = rows // 2
        for s in range(2):
            for g in range(KV):
                for o in range(2):
                    out_ref[s * KV + g, :, pl.ds(o * HEAD, HEAD)] = acc[
                        pl.ds(o * rows + s * part, part), pl.ds(g * HEAD, HEAD)
                    ].astype(BF16)


def adapter_kernel(dv_ref, x_ref, xh_ref, low_ref, up_ref, out_ref):
    rows = x_ref.shape[0]
    width = x_ref.shape[1]
    part = rows // 2
    down = jnp.zeros((RANK, width), F32)
    for o, source in enumerate((x_ref, xh_ref)):
        for s in range(2):
            pulled = jnp.zeros((RANK, part), F32)
            for g in range(KV):
                block = dv_ref[s * KV + g, :, pl.ds(o * HEAD, HEAD)]
                pulled = pulled + dot_nt(up_ref[:, pl.ds(g * HEAD, HEAD)], block)
            down = down + dot_nn(pulled.astype(BF16), source[pl.ds(s * part, part), :])
    for c in range(width // HEAD):
        out_ref[pl.ds(c * RANK, RANK), :] = down[:, c * HEAD : (c + 1) * HEAD]
    base = width // HEAD
    for g in range(KV):
        up = jnp.zeros((RANK, HEAD), F32)
        for o in range(2):
            for s in range(2):
                block = dv_ref[s * KV + g, :, pl.ds(o * HEAD, HEAD)].astype(F32)
                up = up + lax.dot_general(
                    low_ref[o * 2 + s],
                    block,
                    (((1,), (0,)), ((), ())),
                    preferred_element_type=F32,
                    precision=lax.Precision.HIGHEST,
                )
        out_ref[pl.ds((base + g) * RANK, RANK), :] = up
    used = (base + KV) * RANK
    if out_ref.shape[0] > used:
        out_ref[pl.ds(used, out_ref.shape[0] - used), :] = jnp.zeros(
            (out_ref.shape[0] - used, HEAD), F32
        )


def call(kernel, flops, nbytes, **keywords):
    return pl.pallas_call(
        kernel,
        compiler_params=pltpu.CompilerParams(vmem_limit_bytes=VMEM),
        cost_estimate=pl.CostEstimate(flops=flops, bytes_accessed=nbytes, transcendentals=0),
        **keywords,
    )


def body(x, queries, keys, frozen, down_weight, up_weight, grads, mask):
    seq_devices = lax.axis_size("seq")
    weight_devices = lax.axis_size("wt")
    devices = seq_devices * weight_devices
    sequences, _, rows, width = x.shape
    tokens = sequences * rows
    y_planes = seq_devices // UNITS
    both = ("seq", "wt")
    groups = [[UNITS * y + j for j in range(UNITS)] for y in range(y_planes)]
    smem = pl.BlockSpec(memory_space=pltpu.SMEM)

    from_before = []
    for y in range(y_planes):
        for j in range(UNITS):
            for w in range(weight_devices):
                source = (y * UNITS + j) * weight_devices + w
                ny, nw = (y + 1, w) if y + 1 < y_planes else (0, (w + 1) % weight_devices)
                from_before.append((source, (ny * UNITS + j) * weight_devices + nw))
    to_before = [(b, a) for a, b in from_before]

    def swap(block):
        return lax.all_to_all(
            block, "seq", split_axis=0, concat_axis=0, axis_index_groups=groups, tiled=True
        )

    def by_unit(source, columns):
        split = source.reshape(sequences, rows, KV, columns)
        return jnp.transpose(split, (0, 2, 1, 3)).reshape(UNITS, rows, columns)

    place = lax.axis_index("seq")
    parity = (place // UNITS) % 2
    kv_head = place % KV
    my_mask = lax.dynamic_slice_in_dim(mask, kv_head * RATIO, RATIO, 0)
    flags = jnp.where(parity == 1, 1 - my_mask, my_mask).astype(jnp.int32)

    x_rows = x.reshape(tokens, width)
    wide = RATIO * HEAD

    first = swap(jnp.concatenate([by_unit(queries, wide), by_unit(keys, HEAD)], axis=2))
    second_in = by_unit(grads, wide)
    second_in, first = lax.optimization_barrier((second_in, first))
    second = swap(second_in)
    first = first.reshape(HALF, wide + HEAD)
    do_unit = second.reshape(HALF, wide)
    k_prev = lax.ppermute(first[:, wide:], both, from_before)
    x_before = lax.ppermute(x_rows, both, from_before)
    frozen_all = lax.all_gather(frozen, "wt", axis=0, tiled=True)

    head_block = pl.BlockSpec((HALF, HEAD), lambda h: (0, h))
    key_block = pl.BlockSpec((HALF, HEAD), lambda h: (0, RATIO))
    prev_block = pl.BlockSpec((HALF, HEAD), lambda h: (0, 0))
    p_block = pl.BlockSpec((1, 2 * HALF, HALF), lambda h: (h, 0, 0))

    product = 2 * RATIO * HALF * HALF * 3 // 2 * HEAD
    weights = call(
        weights_kernel,
        product,
        10 << 20,
        grid=(RATIO,),
        in_specs=[smem, head_block, key_block, prev_block],
        out_specs=p_block,
        out_shape=jax.ShapeDtypeStruct((RATIO, 2 * HALF, HALF), BF16),
        name="weights",
    )(flags, first, first, k_prev)

    dv_unit = call(
        value_grad_kernel,
        product,
        10 << 20,
        grid=(RATIO,),
        in_specs=[smem, p_block, head_block],
        out_specs=pl.BlockSpec((HALF, 2 * HEAD), lambda h: (0, 0)),
        out_shape=jax.ShapeDtypeStruct((HALF, 2 * HEAD), BF16),
        scratch_shapes=[pltpu.VMEM((2 * HALF, HEAD), F32)],
        name="value_grad",
    )(flags, weights, do_unit)
    dv_tokens = swap(dv_unit.reshape(UNITS, rows, 2 * HEAD))

    low = jnp.concatenate(
        [
            jnp.dot(x_rows, down_weight, preferred_element_type=F32),
            jnp.dot(x_before, down_weight, preferred_element_type=F32),
        ],
        axis=0,
    )
    low_parts = jnp.transpose(low.reshape(4, rows, RANK), (0, 2, 1))

    chunks = (width // HEAD + KV) * RANK
    share = -(-chunks // devices)
    whole = share * devices
    sums = call(
        adapter_kernel,
        4 * tokens * width * RANK,
        3 << 20,
        out_shape=jax.ShapeDtypeStruct((whole, HEAD), F32),
        name="adapter",
    )(dv_tokens, x_rows, x_before, low_parts, up_weight)
    scattered = lax.all_to_all(sums, both, split_axis=0, concat_axis=0, tiled=True)
    mine = jnp.sum(scattered.reshape(devices, share, HEAD), axis=0)
    mine = mine * (ADAPTER_SCALE / math.sqrt(tokens * devices))
    spread = jnp.broadcast_to(mine[None], (devices, share, HEAD)).reshape(whole, HEAD)
    gathered = lax.all_to_all(spread, both, split_axis=0, concat_axis=0, tiled=True)
    down_rows = gathered[: width // HEAD * RANK].reshape(width // HEAD, RANK, HEAD)
    down_grad = jnp.transpose(down_rows, (0, 2, 1)).reshape(width, RANK)
    up_rows = gathered[width // HEAD * RANK : chunks].reshape(KV, RANK, HEAD)
    up_grad = jnp.transpose(up_rows, (1, 0, 2)).reshape(RANK, KV * HEAD)

    steps = 4
    values = call(
        values_kernel,
        4 * tokens * width * KV * HEAD,
        6 << 20,
        grid=(steps,),
        in_specs=[
            pl.BlockSpec((tokens, width // steps), lambda i: (0, i)),
            pl.BlockSpec((tokens, width // steps), lambda i: (0, i)),
            pl.BlockSpec((width // steps, KV * HEAD), lambda i: (i, 0)),
            pl.BlockSpec((2 * tokens, RANK), lambda i: (0, 0)),
            pl.BlockSpec((RANK, KV * HEAD), lambda i: (0, 0)),
        ],
        out_specs=pl.BlockSpec((UNITS, rows, 2 * HEAD), lambda i: (0, 0, 0)),
        out_shape=jax.ShapeDtypeStruct((UNITS, rows, 2 * HEAD), BF16),
        scratch_shapes=[pltpu.VMEM((2 * tokens, KV * HEAD), F32)],
        name="values",
    )(x_rows, x_before, frozen_all, low, up_weight)
    v_unit = swap(values).reshape(HALF, 2 * HEAD)

    total = (RATIO + 2) * HEAD
    unit_grads = call(
        score_grad_kernel,
        3 * product,
        12 << 20,
        grid=(RATIO,),
        in_specs=[
            smem,
            p_block,
            head_block,
            key_block,
            prev_block,
            head_block,
            pl.BlockSpec((HALF, 2 * HEAD), lambda h: (0, 0)),
        ],
        out_specs=pl.BlockSpec((HALF, total), lambda h: (0, 0)),
        out_shape=jax.ShapeDtypeStruct((HALF, total), BF16),
        scratch_shapes=[pltpu.VMEM((2 * HALF, HEAD), F32), pltpu.VMEM((HEAD, 2 * HALF), BF16)],
        name="score_grad",
    )(flags, weights, first, first, k_prev, do_unit, v_unit)
    returned = swap(unit_grads.reshape(UNITS, rows, total))

    def by_token(part, columns):
        split = jnp.transpose(part.reshape(sequences, KV, rows, columns), (0, 2, 1, 3))
        return split.reshape(sequences, 1, rows, KV * columns)

    query_grad = by_token(returned[:, :, :wide], wide)
    key_own = by_token(returned[:, :, wide : wide + HEAD], HEAD)
    key_before = lax.ppermute(by_token(returned[:, :, wide + HEAD :], HEAD), both, to_before)
    key_grad = (key_own.astype(F32) + key_before.astype(F32)).astype(BF16)
    return (query_grad, key_grad, down_grad, up_grad)


def solution(mesh):
    tokens = P(None, "wt", "seq", None)
    return jax.shard_map(
        body,
        mesh=mesh,
        in_specs=(tokens, tokens, tokens, P("wt", None), P(), P(), tokens, P()),
        out_specs=(tokens, tokens, P(), P()),
        check_vma=False,
    )
```

time: 606 us -> 236 us (0.39)
  blocking collectives: 288 us -> 0 us
  waiting for transfers between devices: 227 us -> 89.6 us
  starting transfers between devices: 6.71 us -> 79.2 us
  Pallas kernels: 0 us -> 35.2 us
  matrix products: 24.7 us -> 0.74 us
  other arithmetic: 18 us -> 2.5 us
  local copies, waits for them, and re-layouts: 26.3 us -> 13.9 us
    all_to_all x2 -> x0, blocking collectives: 183 us -> none  [regroup_rows(): lax.all_to_all(stacked, 'seq', split_axis=1, concat_axis=1, tiled=True)]
    psum x1 -> x0, waiting for transfers between devices: 156 us -> none  [body(): summed_down, summed_up = lax.psum((local_down, local_up), ('seq', 'wt'))]
    psum x1 -> x0, blocking collectives: 105 us -> none  [body(): summed_down, summed_up = lax.psum((local_down, local_up), ('seq', 'wt'))]
    all_to_all x0 -> x7, waiting for transfers between devices: none -> 68.8 us  [the longest x5 53.2 us: swap(): lax.all_to_all(block, 'seq', split_axis=0, concat_axis=0, axis_index_grou...]
    all_to_all x0 -> x7, starting transfers between devices: none -> 66.3 us  [the longest x5 30.5 us: swap(): lax.all_to_all(block, 'seq', split_axis=0, concat_axis=0, axis_index_grou...]
    all_gather x1, waiting for transfers between devices: 61 us -> 0.01 us  [body(): frozen_all = lax.all_gather(frozen, 'wt', axis=0, tiled=True)]
    pallas_call x0 -> x5, Pallas kernels: none -> 35.2 us  [the longest x1 12.9 us: body(): call(score_grad_kernel, 3 * product, 12 << 20, grid=(RATIO,), in_specs=[s...]
    dot_general x54 -> x2, matrix products: 24.7 us -> 0.74 us  [the longest x1 0.37 us: body(): jnp.dot(x_rows, down_weight, preferred_element_type=F32)]
  transfers between devices with their start and end apart: 4 -> 11, of which waited for: 4 -> 7; matrix products, arithmetic and copies ran while one was open for 2% -> 5% of each run, Pallas kernels for 0% -> 15%
where the time goes in v1:
time: 236 us; the launch traced here: 235 us
  waiting for transfers between devices  89.6 us (38%)
  starting transfers between devices  79.2 us (34%)
  Pallas kernels  35.2 us (15%)
  between operations  14.3 us (6%)
  local copies, waits for them, and re-layouts  13.9 us (6%)
  other arithmetic  2.5 us (1%)
    all_to_all x5, waiting for transfers between devices, swap(): lax.all_to_all(block, 'seq', split_axis=0, concat_axis=0, axis_index_grou...  53.2 us
    all_to_all x5, starting transfers between devices, swap(): lax.all_to_all(block, 'seq', split_axis=0, concat_axis=0, axis_index_grou...  30.5 us
    ppermute x1, waiting for transfers between devices, body(): k_prev = lax.ppermute(first[:, wide:], both, from_before)  20.2 us
    all_to_all x1, starting transfers between devices, body(): lax.all_to_all(sums, both, split_axis=0, concat_axis=0, tiled=True)  19.5 us
    all_to_all x1, starting transfers between devices, body(): lax.all_to_all(spread, both, split_axis=0, concat_axis=0, tiled=True)  16.3 us
    pallas_call x1, Pallas kernels, body(): call(score_grad_kernel, 3 * product, 12 << 20, grid=(RATIO,), in_specs=[s...  12.9 us
    all_to_all x1, waiting for transfers between devices, body(): lax.all_to_all(spread, both, split_axis=0, concat_axis=0, tiled=True)  11.5 us
    pallas_call x1, Pallas kernels, body(): call(weights_kernel, product, 10 << 20, grid=(RATIO,), in_specs=[smem, he...  8.07 us
  transfers between devices with their start and end apart: 11, of which 7 were waited for; matrix products, arithmetic and copies ran while one was open for 5% of the time, Pallas kernels for 15%

profile of v1, /device:TPU:1, one launch (start us, length us, event | category | flops | bytes accessed | tf_op | source)
XLA Modules:
  0.0 235.4 jit_solution(6981457168188212436)
XLA Ops:
  7.9 0.9 reshape.118
  8.9 0.8 reshape.116
  10.0 1.2 pad_maximum_fusion
  11.2 6.8 %all-to-all-start = ((bf16[8,64,1152]{2,1,0:T(8,128)(2,1)}), bf16[8,64,1152]{2,1,0:T(8,128)(2,1)S(1)}, u32[]{:S(2)}, u32[]{:S(2)}) async-start(bf16[8,64,1152]{2,1,0:T(8,128)(2,1)} %pad_maximum_fusion), calls=%async_computation | async-start | bytes 2359296 | tf_op jit(solution)/shard_map/all_to_all | solution.py:230
  18.0 0.8 reshape.114
  18.8 1.3 copy.30
  20.1 9.4 %all-to-all-done = bf16[8,64,1152]{2,1,0:T(8,128)(2,1)S(1)} async-done(((bf16[8,64,1152]{2,1,0:T(8,128)(2,1)}), bf16[8,64,1152]{2,1,0:T(8,128)(2,1)S(1)}, u32[]{:S(2)}, u32[]{:S(2)}) %all-to-all-start) | async-done | bytes 1179680 | tf_op jit(solution)/shard_map/all_to_all | solution.py:230
  29.5 7.9 %all-to-all-start.1 = ((bf16[8,64,1024]{2,1,0:T(8,128)(2,1)}), bf16[8,64,1024]{2,1,0:T(8,128)(2,1)}, u32[]{:S(2)}, u32[]{:S(2)}) async-start(bf16[8,64,1024]{2,1,0:T(8,128)(2,1)} %bitcast.1), calls=%async_computation.1 | async-start | bytes 2097152 | tf_op jit(solution)/shard_map/all_to_all | solution.py:230
  37.4 4.5 %collective-permute-start.1 = (bf16[128,4096]{1,0:T(8,128)(2,1)S(1)}, bf16[128,4096]{1,0:T(8,128)(2,1)S(1)}, u32[]{:S(2)}, u32[]{:S(2)}) collective-permute-start(bf16[128,4096]{1,0:T(8,128)(2,1)S(1)} %bitcast.58), channel_id=1, source_target_pairs={{0,64},{1,65},{2,66},{3,67},{4,68},{5,69},{6,70},{7,71},{8,72},{9,... | collective-permute-start | bytes 3145736 | tf_op jit(solution)/shard_map/ppermute | solution.py:254
  42.6 3.2 %collective-permute-start = (bf16[512,128]{1,0:T(8,128)(2,1)}, bf16[512,128]{1,0:T(8,128)(2,1)S(1)}, u32[]{:S(2)}, u32[]{:S(2)}) collective-permute-start(bf16[512,128]{1,0:T(8,128)(2,1)} %slice.26), channel_id=1, source_target_pairs={{0,64},{1,65},{2,66},{3,67},{4,68},{5,69},{6,70},{7,71},{8,72},{9,... | collective-permute-start | bytes 393224 | tf_op jit(solution)/shard_map/ppermute | solution.py:253
  46.3 20.2 %collective-permute-done.kp_ref = bf16[512,128]{1,0:T(8,128)(2,1)S(1)} collective-permute-done((bf16[512,128]{1,0:T(8,128)(2,1)}, bf16[512,128]{1,0:T(8,128)(2,1)S(1)}, u32[]{:S(2)}, u32[]{:S(2)}) %collective-permute-start) | collective-permute-done | bytes 131104 | tf_op jit(solution)/shard_map/ppermute | solution.py:253
  66.5 8.1 %weights.1.p_ref = bf16[8,1024,512]{2,1,0:T(8,128)(2,1)} custom-call(s32[8]{0:T(128)S(1)} %broadcast_select_fusion.flags, bf16[512,1152]{1,0:T(8,128)(2,1)S(1)} %bitcast.54, bf16[512,1152]{1,0:T(8,128)(2,1)S(1)} %bitcast.55, bf16[512,128]{1,0:T(8,128)(2,1)S(1)} %collective-permute-done.kp_ref), custom_call_target="tpu_custom_call" | custom-call | flops 805306368 | bytes 10485760 | tf_op jit(solution)/shard_map/weights/pallas_call | solution.py:263
  74.5 23.7 %all-to-all-done.1 = bf16[8,64,1024]{2,1,0:T(8,128)(2,1)} async-done(((bf16[8,64,1024]{2,1,0:T(8,128)(2,1)}), bf16[8,64,1024]{2,1,0:T(8,128)(2,1)}, u32[]{:S(2)}, u32[]{:S(2)}) %all-to-all-start.1) | async-done | bytes 1048608 | tf_op jit(solution)/shard_map/all_to_all | solution.py:230
  98.2 7.4 %value_grad.1 = bf16[512,256]{1,0:T(8,128)(2,1)S(1)} custom-call(s32[8]{0:T(128)S(1)} %broadcast_select_fusion.flags, bf16[8,1024,512]{2,1,0:T(8,128)(2,1)} %weights.1.p_ref, bf16[512,1024]{1,0:T(8,128)(2,1)} %bitcast.7.do_ref), custom_call_target="tpu_custom_call" | custom-call | flops 805306368 | bytes 10485760 | tf_op jit(solution)/shard_map/value_grad/pallas_call | solution.py:274
  106.3 7.1 %all-to-all-start.4 = ((bf16[8,64,256]{2,1,0:T(8,128)(2,1)}), bf16[8,64,256]{2,1,0:T(8,128)(2,1)}, u32[]{:S(2)}, u32[]{:S(2)}) async-start(bf16[8,64,256]{2,1,0:T(8,128)(2,1)} %bitcast.63), calls=%async_computation.4 | async-start | bytes 524288 | tf_op jit(solution)/shard_map/all_to_all | solution.py:230
  113.8 0.8 copy.33.low_ref
  114.6 0.9 copy-done.5
  115.5 4.6 %values.1 = bf16[8,64,256]{2,1,0:T(8,128)(2,1)S(1)} custom-call(bf16[128,4096]{1,0:T(8,128)(2,1)S(1)} %bitcast.60, bf16[128,4096]{1,0:T(8,128)(2,1)S(1)} %collective-permute-done.1.xh_ref, bf16[4096,512]{1,0:T(8,128)(2,1)} %all-gather.2.cloned.1.call-done.w_ref, f32[256,8]{1,0:T(8,128)S(1)} %copy-done.5, bf16[8,512]{1,0:T(8,128)(2,1)S(1)} %copy-done.6), custom_call_target="tpu_custom_call" | custom-call | flops 1073741824 | bytes 6291456 | tf_op jit(solution)/shard_map/values/pallas_call | solution.py:317
  120.9 5.1 %all-to-all-start.2 = ((bf16[8,64,256]{2,1,0:T(8,128)(2,1)}), bf16[8,64,256]{2,1,0:T(8,128)(2,1)}, u32[]{:S(2)}, u32[]{:S(2)}) async-start(bf16[8,64,256]{2,1,0:T(8,128)(2,1)} %copy-done.2), calls=%async_computation.2 | async-start | bytes 524288 | tf_op jit(solution)/shard_map/all_to_all | solution.py:230
  126.1 2.3 adapter.1
  129.1 3.1 %all-to-all-done.2 = bf16[8,64,256]{2,1,0:T(8,128)(2,1)} async-done(((bf16[8,64,256]{2,1,0:T(8,128)(2,1)}), bf16[8,64,256]{2,1,0:T(8,128)(2,1)}, u32[]{:S(2)}, u32[]{:S(2)}) %all-to-all-start.2) | async-done | bytes 262176 | tf_op jit(solution)/shard_map/all_to_all | solution.py:230
  132.2 19.5 %all-to-all-start.5 = ((f32[512,1,128]{2,1,0:T(1,128)}), f32[512,1,128]{2,1,0:T(1,128)S(1)}, u32[]{:S(2)}, u32[]{:S(2)}) async-start(f32[512,1,128]{2,1,0:T(1,128)} %bitcast.62), calls=%async_computation.5 | async-start | bytes 524288 | tf_op jit(solution)/shard_map/all_to_all | solution.py:306
  151.7 12.9 %score_grad.1 = bf16[512,1280]{1,0:T(8,128)(2,1)} custom-call(s32[8]{0:T(128)S(1)} %broadcast_select_fusion.flags, bf16[8,1024,512]{2,1,0:T(8,128)(2,1)} %weights.1.p_ref, bf16[512,1152]{1,0:T(8,128)(2,1)S(1)} %bitcast.56, bf16[512,1152]{1,0:T(8,128)(2,1)S(1)} %bitcast.57, bf16[512,128]{1,0:T(8,128)(2,1)S(1)} %collective-permute-done.kp_ref, ...), custom_call_target="tpu_custom_call" | custom-call | flops 2415919104 | bytes 12582912 | tf_op jit(solution)/shard_map/score_grad/pallas_call | solution.py:337
  164.6 4.0 %all-to-all-done.5 = f32[512,1,128]{2,1,0:T(1,128)S(1)} async-done(((f32[512,1,128]{2,1,0:T(1,128)}), f32[512,1,128]{2,1,0:T(1,128)S(1)}, u32[]{:S(2)}, u32[]{:S(2)}) %all-to-all-start.5) | async-done | bytes 262176 | tf_op jit(solution)/shard_map/all_to_all | solution.py:306
  168.6 3.6 %all-to-all-start.3 = ((bf16[8,64,1280]{2,1,0:T(8,128)(2,1)}), bf16[8,64,1280]{2,1,0:T(8,128)(2,1)S(1)}, u32[]{:S(2)}, u32[]{:S(2)}) async-start(bf16[8,64,1280]{2,1,0:T(8,128)(2,1)} %bitcast.10), calls=%async_computation.3 | async-start | bytes 2621440 | tf_op jit(solution)/shard_map/all_to_all | solution.py:230
  172.7 17.1 %all-to-all-done.3 = bf16[8,64,1280]{2,1,0:T(8,128)(2,1)S(1)} async-done(((bf16[8,64,1280]{2,1,0:T(8,128)(2,1)}), bf16[8,64,1280]{2,1,0:T(8,128)(2,1)S(1)}, u32[]{:S(2)}, u32[]{:S(2)}) %all-to-all-start.3) | async-done | bytes 1310752 | tf_op jit(solution)/shard_map/all_to_all | solution.py:230
  189.8 0.8 reshape.131
  190.6 16.3 %all-to-all-start.6 = ((f32[512,1,128]{2,1,0:T(1,128)}), f32[512,1,128]{2,1,0:T(1,128)S(1)}, u32[]{:S(2)}, u32[]{:S(2)}) async-start(f32[512,1,128]{2,1,0:T(1,128)} %reshape.131), calls=%async_computation.6 | async-start | bytes 524288 | tf_op jit(solution)/shard_map/all_to_all | solution.py:310
  207.2 5.1 %collective-permute-start.2 = (bf16[2,1,64,512]{3,2,1,0:T(8,128)(2,1)S(1)}, bf16[2,1,64,512]{3,2,1,0:T(8,128)(2,1)S(1)}, u32[]{:S(2)}, u32[]{:S(2)}) collective-permute-start(bf16[2,1,64,512]{3,2,1,0:T(8,128)(2,1)S(1)} %reshape.128), channel_id=1, source_target_pairs={{64,0},{65,1},{66,2},{67,3},{68,4},{69,5},{70,6},{71,7},{72,8},{73... | collective-permute-start | bytes 393224 | tf_op jit(solution)/shard_map/ppermute | solution.py:364
  212.3 11.5 %all-to-all-done.6 = f32[512,1,128]{2,1,0:T(1,128)S(1)} async-done(((f32[512,1,128]{2,1,0:T(1,128)}), f32[512,1,128]{2,1,0:T(1,128)S(1)}, u32[]{:S(2)}, u32[]{:S(2)}) %all-to-all-start.6) | async-done | bytes 262176 | tf_op jit(solution)/shard_map/all_to_all | solution.py:310
  225.2 0.8 copy.43
  226.0 1.6 reshape.126
  (45 shorter events, 7.9 us)
Async XLA Ops:
  7.2 38.6 %copy-start = (bf16[4096,8]{0,1:T(8,128)(2,1)S(1)}, bf16[4096,8]{0,1:T(8,128)(2,1)}, u32[]{:S(2)}) copy-start(bf16[4096,8]{0,1:T(8,128)(2,1)} %param.12) | copy-start | bytes 196612
  7.2 1.7 copy-start.7
  7.2 107.4 %all-gather.2.cloned.1.call-start = ((), (), s32[]{:S(2)}) async-start(), calls=%async_computation.7 | async-start | bytes 4718592 | tf_op jit(solution)/shard_map/all_gather | solution.py:255
  11.2 6.8 %copy-start.8 = (bf16[2,1,64,4096]{3,2,1,0:T(8,128)(2,1)S(1)}, bf16[2,1,64,4096]{3,2,1,0:T(8,128)(2,1)}, u32[]{:S(2)}) copy-start(bf16[2,1,64,4096]{3,2,1,0:T(8,128)(2,1)} %param.14) | copy-start | bytes 3145732
  11.2 18.3 %all-to-all-start = ((bf16[8,64,1152]{2,1,0:T(8,128)(2,1)}), bf16[8,64,1152]{2,1,0:T(8,128)(2,1)S(1)}, u32[]{:S(2)}, u32[]{:S(2)}) async-start(bf16[8,64,1152]{2,1,0:T(8,128)(2,1)} %pad_maximum_fusion), calls=%async_computation | async-start | bytes 2359296 | tf_op jit(solution)/shard_map/all_to_all | solution.py:230
  20.1 17.3 %copy-start.1 = (bf16[2,1,64,4096]{3,2,1,0:T(8,128)(2,1)S(1)}, bf16[2,1,64,4096]{3,2,1,0:T(8,128)(2,1)}, u32[]{:S(2)}) copy-start(bf16[2,1,64,4096]{3,2,1,0:T(8,128)(2,1)} %param.8) | copy-start | bytes 3145732
  29.5 16.7 %copy-start.9 = (s32[32]{0:T(128)S(1)}, s32[32]{0:T(128)}, u32[]{:S(2)}) copy-start(s32[32]{0:T(128)} %param.15) | copy-start | bytes 388
  29.5 68.7 %all-to-all-start.1 = ((bf16[8,64,1024]{2,1,0:T(8,128)(2,1)}), bf16[8,64,1024]{2,1,0:T(8,128)(2,1)}, u32[]{:S(2)}, u32[]{:S(2)}) async-start(bf16[8,64,1024]{2,1,0:T(8,128)(2,1)} %bitcast.1), calls=%async_computation.1 | async-start | bytes 2097152 | tf_op jit(solution)/shard_map/all_to_all | solution.py:230
  37.4 76.1 %collective-permute-start.1 = (bf16[128,4096]{1,0:T(8,128)(2,1)S(1)}, bf16[128,4096]{1,0:T(8,128)(2,1)S(1)}, u32[]{:S(2)}, u32[]{:S(2)}) collective-permute-start(bf16[128,4096]{1,0:T(8,128)(2,1)S(1)} %bitcast.58), channel_id=1, source_target_pairs={{0,64},{1,65},{2,66},{3,67},{4,68},{5,69},{6,70},{7,71},{8,72},{9,... | collective-permute-start | bytes 3145736 | tf_op jit(solution)/shard_map/ppermute | solution.py:254
  42.6 23.9 %collective-permute-start = (bf16[512,128]{1,0:T(8,128)(2,1)}, bf16[512,128]{1,0:T(8,128)(2,1)S(1)}, u32[]{:S(2)}, u32[]{:S(2)}) collective-permute-start(bf16[512,128]{1,0:T(8,128)(2,1)} %slice.26), channel_id=1, source_target_pairs={{0,64},{1,65},{2,66},{3,67},{4,68},{5,69},{6,70},{7,71},{8,72},{9,... | collective-permute-start | bytes 393224 | tf_op jit(solution)/shard_map/ppermute | solution.py:253
  105.6 0.7 copy-start.4
  106.3 8.3 %copy-start.6 = (bf16[8,512]{1,0:T(8,128)(2,1)S(1)}, bf16[8,512]{1,0:T(8,128)(2,1)}, u32[]{:S(2)}) copy-start(bf16[8,512]{1,0:T(8,128)(2,1)} %up_ref.3) | copy-start | bytes 24580
  106.3 14.6 %all-to-all-start.4 = ((bf16[8,64,256]{2,1,0:T(8,128)(2,1)}), bf16[8,64,256]{2,1,0:T(8,128)(2,1)}, u32[]{:S(2)}, u32[]{:S(2)}) async-start(bf16[8,64,256]{2,1,0:T(8,128)(2,1)} %bitcast.63), calls=%async_computation.4 | async-start | bytes 524288 | tf_op jit(solution)/shard_map/all_to_all | solution.py:230
  114.6 0.9 copy-start.5
  120.2 0.7 copy-start.2
  120.9 11.3 %all-to-all-start.2 = ((bf16[8,64,256]{2,1,0:T(8,128)(2,1)}), bf16[8,64,256]{2,1,0:T(8,128)(2,1)}, u32[]{:S(2)}, u32[]{:S(2)}) async-start(bf16[8,64,256]{2,1,0:T(8,128)(2,1)} %copy-done.2), calls=%async_computation.2 | async-start | bytes 524288 | tf_op jit(solution)/shard_map/all_to_all | solution.py:230
  128.4 0.7 copy-start.3
  132.2 36.4 %all-to-all-start.5 = ((f32[512,1,128]{2,1,0:T(1,128)}), f32[512,1,128]{2,1,0:T(1,128)S(1)}, u32[]{:S(2)}, u32[]{:S(2)}) async-start(f32[512,1,128]{2,1,0:T(1,128)} %bitcast.62), calls=%async_computation.5 | async-start | bytes 524288 | tf_op jit(solution)/shard_map/all_to_all | solution.py:306
  168.6 21.2 %all-to-all-start.3 = ((bf16[8,64,1280]{2,1,0:T(8,128)(2,1)}), bf16[8,64,1280]{2,1,0:T(8,128)(2,1)S(1)}, u32[]{:S(2)}, u32[]{:S(2)}) async-start(bf16[8,64,1280]{2,1,0:T(8,128)(2,1)} %bitcast.10), calls=%async_computation.3 | async-start | bytes 2621440 | tf_op jit(solution)/shard_map/all_to_all | solution.py:230
  190.6 33.2 %all-to-all-start.6 = ((f32[512,1,128]{2,1,0:T(1,128)}), f32[512,1,128]{2,1,0:T(1,128)S(1)}, u32[]{:S(2)}, u32[]{:S(2)}) async-start(f32[512,1,128]{2,1,0:T(1,128)} %reshape.131), calls=%async_computation.6 | async-start | bytes 524288 | tf_op jit(solution)/shard_map/all_to_all | solution.py:310
  207.2 20.6 %collective-permute-start.2 = (bf16[2,1,64,512]{3,2,1,0:T(8,128)(2,1)S(1)}, bf16[2,1,64,512]{3,2,1,0:T(8,128)(2,1)S(1)}, u32[]{:S(2)}, u32[]{:S(2)}) collective-permute-start(bf16[2,1,64,512]{3,2,1,0:T(8,128)(2,1)S(1)} %reshape.128), channel_id=1, source_target_pairs={{64,0},{65,1},{66,2},{67,3},{68,4},{69,5},{70,6},{71,7},{72,8},{73... | collective-permute-start | bytes 393224 | tf_op jit(solution)/shard_map/ppermute | solution.py:364
Sparse Core Ops, SparseCore 0:
  10.2 103.8 all-gather.1

commit v2 on v1

v2 whole, which is shorter than its diff:
```python
import functools
import math

import jax
import jax.numpy as jnp
from jax import lax
from jax.experimental import pallas as pl
from jax.experimental.pallas import tpu as pltpu
from jax.sharding import PartitionSpec as P

HEAD = 128
HALF = 512
TILE = 256
RATIO = 8
KV = 4
RANK = 8
UNITS = 8
SCALE = 1.0 / math.sqrt(HEAD)
ADAPTER_SCALE = 2.0
VMEM = 48 * 1024 * 1024
F32 = jnp.float32
BF16 = jnp.bfloat16


def dot_nt(a, b):
    return lax.dot_general(a, b, (((1,), (1,)), ((), ())), preferred_element_type=F32)


def dot_nn(a, b):
    return lax.dot_general(a, b, (((1,), (0,)), ((), ())), preferred_element_type=F32)


def weights_kernel(flags, q_ref, k_ref, kp_ref, own_ref, prev_ref):
    head = pl.program_id(0)
    factor = SCALE * math.log2(math.e)

    def tiles(full):
        for r in range(HALF // TILE):
            cols = pl.ds(r * TILE, TILE)
            q = q_ref[cols, :]
            key_place = lax.broadcasted_iota(jnp.int32, (TILE, TILE), 0)
            query_place = lax.broadcasted_iota(jnp.int32, (TILE, TILE), 1)
            scores = dot_nt(k_ref[cols, :], q)
            scores = jnp.where(key_place <= query_place, scores, -jnp.inf)
            parts = [(own_ref, r * TILE, scores)]
            sources = [(own_ref, k_ref, t) for t in range(r)]
            if full:
                sources += [(prev_ref, kp_ref, t) for t in range(HALF // TILE)]
            for place, keys, t in sources:
                parts.append((place, t * TILE, dot_nt(keys[pl.ds(t * TILE, TILE), :], q)))
            top = functools.reduce(
                jnp.maximum, [jnp.max(scores, axis=0, keepdims=True) for _, _, scores in parts]
            )
            raised = [
                (place, at, jnp.exp2((scores - top) * factor)) for place, at, scores in parts
            ]
            total = sum(jnp.sum(e, axis=0, keepdims=True) for _, _, e in raised)
            inverse = 1.0 / total
            for place, at, e in raised:
                place[0, pl.ds(at, TILE), cols] = (e * inverse).astype(BF16)

    @pl.when(flags[head] > 0)
    def _():
        tiles(True)

    @pl.when(flags[head] == 0)
    def _():
        tiles(False)


def value_grad_kernel(flags, own_ref, prev_ref, do_ref, dv_ref, dvp_ref, acc):
    head = pl.program_id(0)

    @pl.when(head == 0)
    def _():
        acc[...] = jnp.zeros_like(acc)

    acc[pl.ds(HALF, TILE), :] += dot_nn(own_ref[0, pl.ds(0, TILE), :], do_ref[...])
    acc[pl.ds(HALF + TILE, TILE), :] += dot_nn(
        own_ref[0, pl.ds(TILE, TILE), pl.ds(TILE, TILE)], do_ref[pl.ds(TILE, TILE), :]
    )

    @pl.when(flags[head] > 0)
    def _():
        acc[pl.ds(0, HALF), :] += dot_nn(prev_ref[0], do_ref[...])

    @pl.when(head == RATIO - 1)
    def _():
        dv_ref[...] = acc[pl.ds(HALF, HALF), :]
        dvp_ref[...] = acc[pl.ds(0, HALF), :].astype(BF16)


def score_grad_kernel(
    flags, own_ref, prev_ref, q_ref, k_ref, kp_ref, do_ref, v_ref, vp_ref, out_ref, acc, kt
):
    head = pl.program_id(0)

    @pl.when(head == 0)
    def _():
        acc[...] = jnp.zeros_like(acc)
        kt[:, pl.ds(0, HALF)] = kp_ref[...].astype(F32).T.astype(BF16)
        kt[:, pl.ds(HALF, HALF)] = k_ref[...].astype(F32).T.astype(BF16)

    def tiles(full):
        for r in range(HALF // TILE):
            cols = pl.ds(r * TILE, TILE)
            q = q_ref[cols, :]
            do = do_ref[cols, :]
            sources = [(own_ref, v_ref, t * TILE, HALF) for t in range(r + 1)]
            if full:
                sources += [(prev_ref, vp_ref, t * TILE, 0) for t in range(HALF // TILE)]
            parts = []
            for place, values, at, base in sources:
                p = place[0, pl.ds(at, TILE), cols].astype(F32)
                parts.append((p, dot_nt(values[pl.ds(at, TILE), :], do), at + base))
            delta = sum(jnp.sum(p * d, axis=0, keepdims=True) for p, d, _ in parts)
            dq = jnp.zeros((HEAD, TILE), F32)
            for p, d, at in parts:
                score_grad = (p * (d - delta)).astype(BF16)
                dq = dq + dot_nn(kt[:, pl.ds(at, TILE)], score_grad)
                acc[pl.ds(at, TILE), :] += dot_nn(score_grad, q)
            place = pl.ds(pl.multiple_of(head * HEAD, HEAD), HEAD)
            out_ref[cols, place] = (dq * SCALE).T.astype(BF16)

    @pl.when(flags[head] > 0)
    def _():
        tiles(True)

    @pl.when(flags[head] == 0)
    def _():
        tiles(False)

    @pl.when(head == RATIO - 1)
    def _():
        out_ref[:, pl.ds(RATIO * HEAD, HEAD)] = (acc[pl.ds(HALF, HALF), :] * SCALE).astype(BF16)
        out_ref[:, pl.ds((RATIO + 1) * HEAD, HEAD)] = (acc[pl.ds(0, HALF), :] * SCALE).astype(BF16)


def values_kernel(x_ref, xo_ref, w_ref, low_ref, up_ref, own_ref, other_ref, acc):
    step = pl.program_id(0)
    rows = x_ref.shape[0]

    @pl.when(step == 0)
    def _():
        acc[...] = ADAPTER_SCALE * lax.dot_general(
            low_ref[...],
            up_ref[...].astype(F32),
            (((1,), (0,)), ((), ())),
            preferred_element_type=F32,
            precision=lax.Precision.HIGHEST,
        )

    acc[pl.ds(0, rows), :] += dot_nn(x_ref[...], w_ref[...])
    acc[pl.ds(rows, rows), :] += dot_nn(xo_ref[...], w_ref[...])

    @pl.when(step == pl.num_programs(0) - 1)
    def _():
        own_ref[...] = acc[pl.ds(0, rows), :].astype(BF16)
        other_ref[...] = acc[pl.ds(rows, rows), :].astype(BF16)


def adapter_kernel(dv_ref, x_ref, low_ref, up_ref, out_ref):
    width = x_ref.shape[1]
    part = x_ref.shape[0] // 2
    down = jnp.zeros((RANK, width), F32)
    for s in range(2):
        pulled = jnp.zeros((RANK, part), F32)
        for g in range(KV):
            pulled = pulled + dot_nt(up_ref[:, pl.ds(g * HEAD, HEAD)], dv_ref[s * KV + g])
        down = down + dot_nn(pulled.astype(BF16), x_ref[pl.ds(s * part, part), :])
    for c in range(width // HEAD):
        out_ref[pl.ds(c * RANK, RANK), :] = down[:, c * HEAD : (c + 1) * HEAD]
    base = width // HEAD
    for g in range(KV):
        up = jnp.zeros((RANK, HEAD), F32)
        for s in range(2):
            up = up + lax.dot_general(
                low_ref[s],
                dv_ref[s * KV + g].astype(F32),
                (((1,), (0,)), ((), ())),
                preferred_element_type=F32,
                precision=lax.Precision.HIGHEST,
            )
        out_ref[pl.ds((base + g) * RANK, RANK), :] = up
    used = (base + KV) * RANK
    if out_ref.shape[0] > used:
        out_ref[pl.ds(used, out_ref.shape[0] - used), :] = jnp.zeros(
            (out_ref.shape[0] - used, HEAD), F32
        )


def call(kernel, flops, nbytes, **keywords):
    return pl.pallas_call(
        kernel,
        compiler_params=pltpu.CompilerParams(vmem_limit_bytes=VMEM),
        cost_estimate=pl.CostEstimate(flops=flops, bytes_accessed=nbytes, transcendentals=0),
        **keywords,
    )


def body(x, queries, keys, frozen, down_weight, up_weight, grads, mask):
    seq_devices = lax.axis_size("seq")
    weight_devices = lax.axis_size("wt")
    devices = seq_devices * weight_devices
    sequences, _, rows, width = x.shape
    tokens = sequences * rows
    y_planes = seq_devices // UNITS
    both = ("seq", "wt")
    groups = [[UNITS * y + j for j in range(UNITS)] for y in range(y_planes)]
    smem = pl.BlockSpec(memory_space=pltpu.SMEM)

    def flat(y, j, w):
        return (y * UNITS + j) * weight_devices + w

    everywhere = [
        (y, j, w) for y in range(y_planes) for j in range(UNITS) for w in range(weight_devices)
    ]
    from_before = [
        (
            flat(y, j, w),
            flat(y + 1, j, w) if y + 1 < y_planes else flat(0, j, (w + 1) % weight_devices),
        )
        for y, j, w in everywhere
    ]
    to_before = [(b, a) for a, b in from_before]
    turned = [(flat(w, j, y), flat(y, j, w)) for y, j, w in everywhere]
    other_core = [(w, w ^ 1) for w in range(weight_devices)]
    columns_of_y = [[UNITS * y + j for y in range(y_planes)] for j in range(UNITS)]

    def swap(block):
        return lax.all_to_all(
            block, "seq", split_axis=0, concat_axis=0, axis_index_groups=groups, tiled=True
        )

    def by_unit(source, columns):
        split = source.reshape(sequences, rows, KV, columns)
        return jnp.transpose(split, (0, 2, 1, 3)).reshape(UNITS, rows, columns)

    place = lax.axis_index("seq")
    parity = (place // UNITS) % 2
    kv_head = place % KV
    my_mask = lax.dynamic_slice_in_dim(mask, kv_head * RATIO, RATIO, 0)
    flags = jnp.where(parity == 1, 1 - my_mask, my_mask).astype(jnp.int32)

    x_rows = x.reshape(tokens, width)
    wide = RATIO * HEAD
    core = lax.axis_index("wt") % 2
    half_columns = KV * HEAD // 2

    shard = lax.dynamic_slice_in_dim(frozen, (place // UNITS) % 2 * half_columns, half_columns, 1)
    shard = lax.ppermute(shard, both, turned)
    frozen_half = lax.all_gather(
        shard, "seq", axis=0, axis_index_groups=columns_of_y, tiled=True
    )
    x_other = lax.ppermute(x_rows, "wt", other_core)

    first = swap(jnp.concatenate([by_unit(queries, wide), by_unit(keys, HEAD)], axis=2))
    second_in = by_unit(grads, wide)
    second_in, first = lax.optimization_barrier((second_in, first))
    second = swap(second_in)
    first = first.reshape(HALF, wide + HEAD)
    do_unit = second.reshape(HALF, wide)
    k_prev = lax.ppermute(first[:, wide:], both, from_before)

    head_block = pl.BlockSpec((HALF, HEAD), lambda h: (0, h))
    key_block = pl.BlockSpec((HALF, HEAD), lambda h: (0, RATIO))
    prev_block = pl.BlockSpec((HALF, HEAD), lambda h: (0, 0))
    p_block = pl.BlockSpec((1, HALF, HALF), lambda h: (h, 0, 0))
    p_shape = pltpu.HBM((RATIO, HALF, HALF), BF16)

    product = 2 * RATIO * HALF * HALF * 3 // 2 * HEAD
    weights_own, weights_prev = call(
        weights_kernel,
        product,
        10 << 20,
        grid=(RATIO,),
        in_specs=[smem, head_block, key_block, prev_block],
        out_specs=(p_block, p_block),
        out_shape=(p_shape, p_shape),
        name="weights",
    )(flags, first, first, k_prev)
    weights_own = pltpu.with_memory_space_constraint(weights_own, pltpu.HBM)
    weights_prev = pltpu.with_memory_space_constraint(weights_prev, pltpu.HBM)

    dv_own, dv_prev = call(
        value_grad_kernel,
        product,
        10 << 20,
        grid=(RATIO,),
        in_specs=[smem, p_block, p_block, head_block],
        out_specs=(prev_block, prev_block),
        out_shape=(
            jax.ShapeDtypeStruct((HALF, HEAD), F32),
            jax.ShapeDtypeStruct((HALF, HEAD), BF16),
        ),
        scratch_shapes=[pltpu.VMEM((2 * HALF, HEAD), F32)],
        name="value_grad",
    )(flags, weights_own, weights_prev, do_unit)
    dv_next = lax.ppermute(dv_prev, both, to_before)
    dv_unit = (dv_own + dv_next.astype(F32)).astype(BF16).reshape(UNITS, rows, HEAD)

    low = jnp.dot(x_rows, down_weight, preferred_element_type=F32)
    low_other = jnp.dot(x_other, down_weight, preferred_element_type=F32)
    low_parts = jnp.transpose(low.reshape(sequences, rows, RANK), (0, 2, 1))
    up_half = lax.dynamic_slice_in_dim(up_weight, core * half_columns, half_columns, 1)

    steps = 4
    slab = pl.BlockSpec((tokens, width // steps), lambda i: (0, i))
    value_block = pl.BlockSpec((tokens, half_columns), lambda i: (0, 0))
    value_shape = jax.ShapeDtypeStruct((tokens, half_columns), BF16)
    values_mine, values_other = call(
        values_kernel,
        4 * tokens * width * half_columns,
        4 << 20,
        grid=(steps,),
        in_specs=[
            slab,
            slab,
            pl.BlockSpec((width // steps, half_columns), lambda i: (i, 0)),
            pl.BlockSpec((2 * tokens, RANK), lambda i: (0, 0)),
            pl.BlockSpec((RANK, half_columns), lambda i: (0, 0)),
        ],
        out_specs=(value_block, value_block),
        out_shape=(value_shape, value_shape),
        scratch_shapes=[pltpu.VMEM((2 * tokens, half_columns), F32)],
        name="values",
    )(x_rows, x_other, frozen_half, jnp.concatenate([low, low_other], axis=0), up_half)
    values_back = lax.ppermute(values_other, "wt", other_core)
    low_half = jnp.where(core == 0, values_mine, values_back)
    high_half = jnp.where(core == 0, values_back, values_mine)
    value_parts = by_unit(jnp.concatenate([low_half, high_half], axis=1), HEAD)

    third = swap(jnp.concatenate([dv_unit, value_parts], axis=2))
    third_rows = third.reshape(HALF, 2 * HEAD)
    v_prev = lax.ppermute(third_rows[:, HEAD:], both, from_before)

    chunks = (width // HEAD + KV) * RANK
    share = -(-chunks // devices)
    whole = share * devices
    sums = call(
        adapter_kernel,
        4 * tokens * width * RANK,
        3 << 20,
        grid=(1,),
        in_specs=[
            pl.BlockSpec((UNITS, rows, HEAD), lambda i: (0, 0, 0)),
            pl.BlockSpec((tokens, width), lambda i: (0, 0)),
            pl.BlockSpec((sequences, RANK, rows), lambda i: (0, 0, 0)),
            pl.BlockSpec((RANK, KV * HEAD), lambda i: (0, 0)),
        ],
        out_specs=pl.BlockSpec((whole, HEAD), lambda i: (0, 0)),
        out_shape=jax.ShapeDtypeStruct((whole, HEAD), F32),
        name="adapter",
    )(third, x_rows, low_parts, up_weight)
    scattered = lax.all_to_all(sums, both, split_axis=0, concat_axis=0, tiled=True)
    mine = jnp.sum(scattered.reshape(devices, share, HEAD), axis=0)
    mine = mine * (ADAPTER_SCALE / math.sqrt(tokens * devices))
    spread = jnp.broadcast_to(mine[None], (devices, share, HEAD)).reshape(whole, HEAD)
    gathered = lax.all_to_all(spread, both, split_axis=0, concat_axis=0, tiled=True)
    down_rows = gathered[: width // HEAD * RANK].reshape(width // HEAD, RANK, HEAD)
    down_grad = jnp.transpose(down_rows, (0, 2, 1)).reshape(width, RANK)
    up_rows = gathered[width // HEAD * RANK : chunks].reshape(KV, RANK, HEAD)
    up_grad = jnp.transpose(up_rows, (1, 0, 2)).reshape(RANK, KV * HEAD)

    total = (RATIO + 2) * HEAD
    unit_grads = call(
        score_grad_kernel,
        3 * product,
        12 << 20,
        grid=(RATIO,),
        in_specs=[
            smem,
            p_block,
            p_block,
            head_block,
            key_block,
            prev_block,
            head_block,
            pl.BlockSpec((HALF, HEAD), lambda h: (0, 1)),
            prev_block,
        ],
        out_specs=pl.BlockSpec((HALF, total), lambda h: (0, 0)),
        out_shape=jax.ShapeDtypeStruct((HALF, total), BF16),
        scratch_shapes=[pltpu.VMEM((2 * HALF, HEAD), F32), pltpu.VMEM((HEAD, 2 * HALF), BF16)],
        name="score_grad",
    )(
        flags,
        weights_own,
        weights_prev,
        first,
        first,
        k_prev,
        do_unit,
        third_rows,
        v_prev,
    )
    returned = swap(unit_grads.reshape(UNITS, rows, total))

    def by_token(part, columns):
        split = jnp.transpose(part.reshape(sequences, KV, rows, columns), (0, 2, 1, 3))
        return split.reshape(sequences, 1, rows, KV * columns)

    query_grad = by_token(returned[:, :, :wide], wide)
    key_own = by_token(returned[:, :, wide : wide + HEAD], HEAD)
    key_before = lax.ppermute(by_token(returned[:, :, wide + HEAD :], HEAD), both, to_before)
    key_grad = (key_own.astype(F32) + key_before.astype(F32)).astype(BF16)
    return (query_grad, key_grad, down_grad, up_grad)


def solution(mesh):
    tokens = P(None, "wt", "seq", None)
    return jax.shard_map(
        body,
        mesh=mesh,
        in_specs=(tokens, tokens, tokens, P("wt", None), P(), P(), tokens, P()),
        out_specs=(tokens, tokens, P(), P()),
        check_vma=False,
    )
```

time: 236 us -> 228 us (0.966)
  waiting for transfers between devices: 89.6 us -> 71 us
  starting transfers between devices: 79.2 us -> 88.2 us
  Pallas kernels: 35.2 us -> 31.5 us
    ppermute x1 -> x5, starting transfers between devices: 4.54 us -> 20.7 us  [the longest x1 5.97 us: body(): values_back = lax.ppermute(values_other, 'wt', other_core)]
    all_to_all x5 -> x4, waiting for transfers between devices: 53.2 us -> 38.7 us  [swap(): lax.all_to_all(block, 'seq', split_axis=0, concat_axis=0, axis_index_grou...]
    ppermute x1, waiting for transfers between devices: 20.2 us -> 8.21 us  [body(): k_prev = lax.ppermute(first[:, wide:], both, from_before)]
    all_to_all x5 -> x4, starting transfers between devices: 30.5 us -> 21.3 us  [swap(): lax.all_to_all(block, 'seq', split_axis=0, concat_axis=0, axis_index_grou...]
    all_to_all x1, starting transfers between devices: 16.3 us -> 24.1 us  [body(): lax.all_to_all(spread, both, split_axis=0, concat_axis=0, tiled=True)]
    ppermute x1 -> x5, waiting for transfers between devices: 0.01 us -> 6.29 us  [the longest x1 5.02 us: body(): v_prev = lax.ppermute(third_rows[:, HEAD:], both, from_before)]
    all_gather x1, waiting for transfers between devices: 0.01 us -> 6.23 us  [body(): lax.all_gather(shard, 'seq', axis=0, axis_index_groups=columns_of_y, tile...]
    all_to_all x1, starting transfers between devices: 19.5 us -> 15 us  [body(): lax.all_to_all(sums, both, split_axis=0, concat_axis=0, tiled=True)]
  transfers between devices with their start and end apart: 11 -> 14, of which waited for: 7 -> 8; matrix products, arithmetic and copies ran while one was open for 5% -> 7% of each run, Pallas kernels for 15% -> 13%
where the time goes in v2:
time: 228 us; the launch traced here: 227 us
  starting transfers between devices  88.2 us (39%)
  waiting for transfers between devices  71 us (31%)
  Pallas kernels  31.5 us (14%)
  local copies, waits for them, and re-layouts  15.5 us (7%)
  between operations  14.4 us (6%)
  other arithmetic  4.16 us (2%)
    all_to_all x4, waiting for transfers between devices, swap(): lax.all_to_all(block, 'seq', split_axis=0, concat_axis=0, axis_index_grou...  38.7 us
    all_to_all x1, starting transfers between devices, body(): lax.all_to_all(spread, both, split_axis=0, concat_axis=0, tiled=True)  24.1 us
    all_to_all x4, starting transfers between devices, swap(): lax.all_to_all(block, 'seq', split_axis=0, concat_axis=0, axis_index_grou...  21.3 us
    all_to_all x1, starting transfers between devices, body(): lax.all_to_all(sums, both, split_axis=0, concat_axis=0, tiled=True)  15 us
    pallas_call x1, Pallas kernels, body(): call(score_grad_kernel, 3 * product, 12 << 20, grid=(RATIO,), in_specs=[s...  12.2 us
    all_to_all x1, waiting for transfers between devices, body(): lax.all_to_all(spread, both, split_axis=0, concat_axis=0, tiled=True)  11.5 us
    ppermute x1, waiting for transfers between devices, body(): k_prev = lax.ppermute(first[:, wide:], both, from_before)  8.21 us
    pallas_call x1, Pallas kernels, body(): call(weights_kernel, product, 10 << 20, grid=(RATIO,), in_specs=[smem, he...  7.57 us
  transfers between devices with their start and end apart: 14, of which 8 were waited for; matrix products, arithmetic and copies ran while one was open for 7% of the time, Pallas kernels for 13%

profile of v2, /device:TPU:1, one launch (start us, length us, event | category | flops | bytes accessed | tf_op | source)
XLA Modules:
  0.0 226.7 jit_solution(11511119355125861357)
XLA Ops:
  8.2 4.6 %collective-permute-start.3 = (bf16[512,256]{1,0:T(8,128)(2,1)S(1)}, bf16[512,256]{1,0:T(8,128)(2,1)S(1)}, u32[]{:S(2)}, u32[]{:S(2)}) collective-permute-start(bf16[512,256]{1,0:T(8,128)(2,1)S(1)} %constant_dynamic-slice_fusion.1), channel_id=1, source_target_pairs={{0,0},{64,1},{128,2},{192,3},{256,4},{320,5},{384,6},{448,7},{8,8}... | collective-permute-start | bytes 786440 | tf_op jit(solution)/shard_map/ppermute | solution.py:251
  14.9 1.1 pad_maximum_fusion
  16.1 5.8 %all-to-all-start = ((bf16[8,64,1152]{2,1,0:T(8,128)(2,1)}), bf16[8,64,1152]{2,1,0:T(8,128)(2,1)S(1)}, u32[]{:S(2)}, u32[]{:S(2)}) async-start(bf16[8,64,1152]{2,1,0:T(8,128)(2,1)} %pad_maximum_fusion), calls=%async_computation | async-start | bytes 2359296 | tf_op jit(solution)/shard_map/all_to_all | solution.py:231
  22.7 1.9 reshape.120
  24.6 1.3 copy.31
  25.9 22.4 %all-to-all-done = bf16[8,64,1152]{2,1,0:T(8,128)(2,1)S(1)} async-done(((bf16[8,64,1152]{2,1,0:T(8,128)(2,1)}), bf16[8,64,1152]{2,1,0:T(8,128)(2,1)S(1)}, u32[]{:S(2)}, u32[]{:S(2)}) %all-to-all-start) | async-done | bytes 1179680 | tf_op jit(solution)/shard_map/all_to_all | solution.py:231
  48.3 4.2 %all-to-all-start.1 = ((bf16[8,64,1024]{2,1,0:T(8,128)(2,1)}), bf16[8,64,1024]{2,1,0:T(8,128)(2,1)}, u32[]{:S(2)}, u32[]{:S(2)}) async-start(bf16[8,64,1024]{2,1,0:T(8,128)(2,1)} %bitcast.68), calls=%async_computation.1 | async-start | bytes 2097152 | tf_op jit(solution)/shard_map/all_to_all | solution.py:231
  52.6 2.7 %collective-permute-start.2 = (bf16[128,4096]{1,0:T(8,128)(2,1)S(1)}, bf16[128,4096]{1,0:T(8,128)(2,1)}, u32[]{:S(2)}, u32[]{:S(2)}) collective-permute-start(bf16[128,4096]{1,0:T(8,128)(2,1)S(1)} %bitcast.61), channel_id=1, source_target_pairs={{0,1},{1,0},{2,3},{3,2},{4,5},{5,4},{6,7},{7,6},{8,9},{9,8},{10,11... | collective-permute-start | bytes 3145736 | tf_op jit(solution)/shard_map/ppermute | solution.py:255
  55.8 1.9 collective-permute-start
  57.7 1.6 fusion.2
  59.5 8.2 %collective-permute-done.kp_ref = bf16[512,128]{1,0:T(8,128)(2,1)S(1)} collective-permute-done((bf16[512,128]{1,0:T(8,128)(2,1)S(1)}, bf16[512,128]{1,0:T(8,128)(2,1)S(1)}, u32[]{:S(2)}, u32[]{:S(2)}) %collective-permute-start) | collective-permute-done | bytes 131104 | tf_op jit(solution)/shard_map/ppermute | solution.py:263
  67.7 7.6 %weights.1 = (bf16[8,512,512]{2,1,0:T(8,128)(2,1)}, bf16[8,512,512]{2,1,0:T(8,128)(2,1)}) custom-call(s32[8]{0:T(128)S(1)} %broadcast_select_fusion.2.flags, bf16[512,1152]{1,0:T(8,128)(2,1)S(1)} %bitcast.57, bf16[512,1152]{1,0:T(8,128)(2,1)S(1)} %bitcast.58, bf16[512,128]{1,0:T(8,128)(2,1)S(1)} %collective-permute-done.kp_ref), custom_call_target="tpu_custom_call" | custom-call | flops 805306368 | bytes 10485760 | tf_op jit(solution)/shard_map/weights/pallas_call | solution.py:272
  75.3 6.2 %all-gather.2.cloned.1.call-done.w_ref = bf16[4096,256]{1,0:T(8,128)(2,1)} async-done(((bf16[512,256]{1,0:T(8,128)(2,1)}), bf16[4096,256]{1,0:T(8,128)(2,1)}) %all-gather.2.cloned.1.call-update) | async-done | bytes 2097168 | tf_op jit(solution)/shard_map/all_gather | solution.py:252
  81.5 1.6 copy-done.2
  83.1 3.3 %values.1 = (bf16[128,256]{1,0:T(8,128)(2,1)S(1)}, bf16[128,256]{1,0:T(8,128)(2,1)S(1)}) custom-call(bf16[128,4096]{1,0:T(8,128)(2,1)S(1)} %bitcast.63, bf16[128,4096]{1,0:T(8,128)(2,1)} %collective-permute-done.2.xo_ref, bf16[4096,256]{1,0:T(8,128)(2,1)S(1)} %copy-done.2, f32[256,8]{1,0:T(8,128)S(1)} %copy.34.low_ref, ...), custom_call_target="tpu_custom_call" | custom-call | flops 536870912 | bytes 4194304 | tf_op jit(solution)/shard_map/values/pallas_call | solution.py:311
  86.4 6.0 %collective-permute-start.4 = (bf16[128,256]{1,0:T(8,128)(2,1)S(1)}, bf16[128,256]{1,0:T(8,128)(2,1)S(1)}, u32[]{:S(2)}, u32[]{:S(2)}) collective-permute-start(bf16[128,256]{1,0:T(8,128)(2,1)S(1)} %get-tuple-element.19), channel_id=1, source_target_pairs={{0,1},{1,0},{2,3},{3,2},{4,5},{5,4},{6,7},{7,6},{8,9},{9,8},{10,11... | collective-permute-start | bytes 196616 | tf_op jit(solution)/shard_map/ppermute | solution.py:328
  92.4 7.0 %value_grad.1 = (f32[512,128]{1,0:T(8,128)S(1)}, bf16[512,128]{1,0:T(8,128)(2,1)S(1)}) custom-call(s32[8]{0:T(128)S(1)} %broadcast_select_fusion.2.flags, bf16[8,512,512]{2,1,0:T(8,128)(2,1)} %get-tuple-element.13.own_ref, bf16[8,512,512]{2,1,0:T(8,128)(2,1)} %get-tuple-element.14.prev_ref, bf16[512,1024]{1,0:T(8,128)(2,1)} %bitcast.7.do_ref), custom_call_target="tpu_custom_call" | custom-call | flops 805306368 | bytes 10485760 | tf_op jit(solution)/shard_map/value_grad/pallas_call | solution.py:285
  99.5 4.2 %collective-permute-start.1 = (bf16[512,128]{1,0:T(8,128)(2,1)S(1)}, bf16[512,128]{1,0:T(8,128)(2,1)}, u32[]{:S(2)}, u32[]{:S(2)}) collective-permute-start(bf16[512,128]{1,0:T(8,128)(2,1)S(1)} %get-tuple-element.17), channel_id=1, source_target_pairs={{64,0},{65,1},{66,2},{67,3},{68,4},{69,5},{70,6},{71,7},{72,8},{73... | collective-permute-start | bytes 393224 | tf_op jit(solution)/shard_map/ppermute | solution.py:299
  105.3 1.3 collective-permute-done.1
  108.3 5.4 %all-to-all-start.2 = ((bf16[8,64,256]{2,1,0:T(8,128)(2,1)}), bf16[8,64,256]{2,1,0:T(8,128)(2,1)S(1)}, u32[]{:S(2)}, u32[]{:S(2)}) async-start(bf16[8,64,256]{2,1,0:T(8,128)(2,1)} %pad_maximum_fusion.1), calls=%async_computation.2 | async-start | bytes 524288 | tf_op jit(solution)/shard_map/all_to_all | solution.py:231
  113.7 6.0 %all-to-all-done.2.dv_ref = bf16[8,64,256]{2,1,0:T(8,128)(2,1)S(1)} async-done(((bf16[8,64,256]{2,1,0:T(8,128)(2,1)}), bf16[8,64,256]{2,1,0:T(8,128)(2,1)S(1)}, u32[]{:S(2)}, u32[]{:S(2)}) %all-to-all-start.2) | async-done | bytes 262176 | tf_op jit(solution)/shard_map/all_to_all | solution.py:231
  119.7 1.3 adapter.1
  121.1 15.0 %all-to-all-start.4 = ((f32[512,1,128]{2,1,0:T(1,128)}), f32[512,1,128]{2,1,0:T(1,128)S(1)}, u32[]{:S(2)}, u32[]{:S(2)}) async-start(f32[512,1,128]{2,1,0:T(1,128)} %bitcast.22), calls=%async_computation.4 | async-start | bytes 524288 | tf_op jit(solution)/shard_map/all_to_all | solution.py:355
  136.1 3.3 %collective-permute-start.5 = (bf16[512,128]{1,0:T(8,128)(2,1)S(1)}, bf16[512,128]{1,0:T(8,128)(2,1)S(1)}, u32[]{:S(2)}, u32[]{:S(2)}) collective-permute-start(bf16[512,128]{1,0:T(8,128)(2,1)S(1)} %slice.31), channel_id=1, source_target_pairs={{0,64},{1,65},{2,66},{3,67},{4,68},{5,69},{6,70},{7,71},{8,72},{9,... | collective-permute-start | bytes 393224 | tf_op jit(solution)/shard_map/ppermute | solution.py:335
  139.4 5.0 %collective-permute-done.5.vp_ref = bf16[512,128]{1,0:T(8,128)(2,1)S(1)} collective-permute-done((bf16[512,128]{1,0:T(8,128)(2,1)S(1)}, bf16[512,128]{1,0:T(8,128)(2,1)S(1)}, u32[]{:S(2)}, u32[]{:S(2)}) %collective-permute-start.5) | collective-permute-done | bytes 131104 | tf_op jit(solution)/shard_map/ppermute | solution.py:335
  144.4 12.2 %score_grad.1 = bf16[512,1280]{1,0:T(8,128)(2,1)} custom-call(s32[8]{0:T(128)S(1)} %broadcast_select_fusion.2.flags, bf16[8,512,512]{2,1,0:T(8,128)(2,1)} %get-tuple-element.13.own_ref, bf16[8,512,512]{2,1,0:T(8,128)(2,1)} %get-tuple-element.14.prev_ref, bf16[512,1152]{1,0:T(8,128)(2,1)S(1)} %bitcast.59, bf16[512,1152]{1,0:T(8,128)(2,1)S(1)} %bitcast.60, ...), custom_call_target="tpu_custom_call" | custom-call | flops 2415919104 | bytes 12582912 | tf_op jit(solution)/shard_map/score_grad/pallas_call | solution.py:366
  156.6 5.8 %all-to-all-start.3 = ((bf16[8,64,1280]{2,1,0:T(8,128)(2,1)}), bf16[8,64,1280]{2,1,0:T(8,128)(2,1)S(1)}, u32[]{:S(2)}, u32[]{:S(2)}) async-start(bf16[8,64,1280]{2,1,0:T(8,128)(2,1)} %bitcast.13), calls=%async_computation.3 | async-start | bytes 2621440 | tf_op jit(solution)/shard_map/all_to_all | solution.py:231
  163.0 10.3 %all-to-all-done.3 = bf16[8,64,1280]{2,1,0:T(8,128)(2,1)S(1)} async-done(((bf16[8,64,1280]{2,1,0:T(8,128)(2,1)}), bf16[8,64,1280]{2,1,0:T(8,128)(2,1)S(1)}, u32[]{:S(2)}, u32[]{:S(2)}) %all-to-all-start.3) | async-done | bytes 1310752 | tf_op jit(solution)/shard_map/all_to_all | solution.py:231
  174.1 24.1 %all-to-all-start.5 = ((f32[512,1,128]{2,1,0:T(1,128)}), f32[512,1,128]{2,1,0:T(1,128)S(1)}, u32[]{:S(2)}, u32[]{:S(2)}) async-start(f32[512,1,128]{2,1,0:T(1,128)} %reshape.139), calls=%async_computation.5 | async-start | bytes 524288 | tf_op jit(solution)/shard_map/all_to_all | solution.py:359
  198.5 5.1 %collective-permute-start.6 = (bf16[2,1,64,512]{3,2,1,0:T(8,128)(2,1)S(1)}, bf16[2,1,64,512]{3,2,1,0:T(8,128)(2,1)S(1)}, u32[]{:S(2)}, u32[]{:S(2)}) collective-permute-start(bf16[2,1,64,512]{3,2,1,0:T(8,128)(2,1)S(1)} %reshape.137), channel_id=1, source_target_pairs={{64,0},{65,1},{66,2},{67,3},{68,4},{69,5},{70,6},{71,7},{72,8},{73... | collective-permute-start | bytes 393224 | tf_op jit(solution)/shard_map/ppermute | solution.py:405
  203.6 11.5 %all-to-all-done.5 = f32[512,1,128]{2,1,0:T(1,128)S(1)} async-done(((f32[512,1,128]{2,1,0:T(1,128)}), f32[512,1,128]{2,1,0:T(1,128)S(1)}, u32[]{:S(2)}, u32[]{:S(2)}) %all-to-all-start.5) | async-done | bytes 262176 | tf_op jit(solution)/shard_map/all_to_all | solution.py:359
  217.3 1.6 reshape.135
  (56 shorter events, 12.6 us)
Async XLA Ops:
  7.2 1.0 copy-start
  7.2 6.6 %copy-start.4 = (bf16[2,1,64,4096]{3,2,1,0:T(8,128)(2,1)S(1)}, bf16[2,1,64,4096]{3,2,1,0:T(8,128)(2,1)}, u32[]{:S(2)}) copy-start(bf16[2,1,64,4096]{3,2,1,0:T(8,128)(2,1)} %param.9) | copy-start | bytes 3145732
  8.2 13.7 %collective-permute-start.3 = (bf16[512,256]{1,0:T(8,128)(2,1)S(1)}, bf16[512,256]{1,0:T(8,128)(2,1)S(1)}, u32[]{:S(2)}, u32[]{:S(2)}) collective-permute-start(bf16[512,256]{1,0:T(8,128)(2,1)S(1)} %constant_dynamic-slice_fusion.1), channel_id=1, source_target_pairs={{0,0},{64,1},{128,2},{192,3},{256,4},{320,5},{384,6},{448,7},{8,8}... | collective-permute-start | bytes 786440 | tf_op jit(solution)/shard_map/ppermute | solution.py:251
  16.1 32.2 %all-to-all-start = ((bf16[8,64,1152]{2,1,0:T(8,128)(2,1)}), bf16[8,64,1152]{2,1,0:T(8,128)(2,1)S(1)}, u32[]{:S(2)}, u32[]{:S(2)}) async-start(bf16[8,64,1152]{2,1,0:T(8,128)(2,1)} %pad_maximum_fusion), calls=%async_computation | async-start | bytes 2359296 | tf_op jit(solution)/shard_map/all_to_all | solution.py:231
  21.9 59.6 %all-gather.2.cloned.1.call-start = ((), (), s32[]{:S(2)}) async-start(), calls=%async_computation.6 | async-start | bytes 2359296 | tf_op jit(solution)/shard_map/all_gather | solution.py:252
  22.0 0.7 copy-start.6
  25.9 26.7 %copy-start.1 = (bf16[2,1,64,4096]{3,2,1,0:T(8,128)(2,1)S(1)}, bf16[2,1,64,4096]{3,2,1,0:T(8,128)(2,1)}, u32[]{:S(2)}) copy-start(bf16[2,1,64,4096]{3,2,1,0:T(8,128)(2,1)} %param.8) | copy-start | bytes 3145732
  25.9 29.5 %copy-start.7 = (s32[32]{0:T(128)S(1)}, s32[32]{0:T(128)}, u32[]{:S(2)}) copy-start(s32[32]{0:T(128)} %param.15) | copy-start | bytes 388
  25.9 29.5 %copy-start.3 = (bf16[8,512]{1,0:T(8,128)(2,1)S(1)}, bf16[8,512]{1,0:T(8,128)(2,1)}, u32[]{:S(2)}) copy-start(bf16[8,512]{1,0:T(8,128)(2,1)} %up_ref.1) | copy-start | bytes 24580
  25.9 29.5 %copy-start.5 = (bf16[4096,8]{0,1:T(8,128)(2,1)S(1)}, bf16[4096,8]{0,1:T(8,128)(2,1)}, u32[]{:S(2)}) copy-start(bf16[4096,8]{0,1:T(8,128)(2,1)} %param.12) | copy-start | bytes 196612
  48.3 44.1 %all-to-all-start.1 = ((bf16[8,64,1024]{2,1,0:T(8,128)(2,1)}), bf16[8,64,1024]{2,1,0:T(8,128)(2,1)}, u32[]{:S(2)}, u32[]{:S(2)}) async-start(bf16[8,64,1024]{2,1,0:T(8,128)(2,1)} %bitcast.68), calls=%async_computation.1 | async-start | bytes 2097152 | tf_op jit(solution)/shard_map/all_to_all | solution.py:231
  52.6 5.2 %collective-permute-start.2 = (bf16[128,4096]{1,0:T(8,128)(2,1)S(1)}, bf16[128,4096]{1,0:T(8,128)(2,1)}, u32[]{:S(2)}, u32[]{:S(2)}) collective-permute-start(bf16[128,4096]{1,0:T(8,128)(2,1)S(1)} %bitcast.61), channel_id=1, source_target_pairs={{0,1},{1,0},{2,3},{3,2},{4,5},{5,4},{6,7},{7,6},{8,9},{9,8},{10,11... | collective-permute-start | bytes 3145736 | tf_op jit(solution)/shard_map/ppermute | solution.py:255
  55.8 11.9 %collective-permute-start = (bf16[512,128]{1,0:T(8,128)(2,1)S(1)}, bf16[512,128]{1,0:T(8,128)(2,1)S(1)}, u32[]{:S(2)}, u32[]{:S(2)}) collective-permute-start(bf16[512,128]{1,0:T(8,128)(2,1)S(1)} %slice.30), channel_id=1, source_target_pairs={{0,64},{1,65},{2,66},{3,67},{4,68},{5,69},{6,70},{7,71},{8,72},{9,... | collective-permute-start | bytes 393224 | tf_op jit(solution)/shard_map/ppermute | solution.py:263
  81.5 1.6 copy-start.2
  86.4 17.2 %collective-permute-start.4 = (bf16[128,256]{1,0:T(8,128)(2,1)S(1)}, bf16[128,256]{1,0:T(8,128)(2,1)S(1)}, u32[]{:S(2)}, u32[]{:S(2)}) collective-permute-start(bf16[128,256]{1,0:T(8,128)(2,1)S(1)} %get-tuple-element.19), channel_id=1, source_target_pairs={{0,1},{1,0},{2,3},{3,2},{4,5},{5,4},{6,7},{7,6},{8,9},{9,8},{10,11... | collective-permute-start | bytes 196616 | tf_op jit(solution)/shard_map/ppermute | solution.py:328
  99.5 7.1 %collective-permute-start.1 = (bf16[512,128]{1,0:T(8,128)(2,1)S(1)}, bf16[512,128]{1,0:T(8,128)(2,1)}, u32[]{:S(2)}, u32[]{:S(2)}) collective-permute-start(bf16[512,128]{1,0:T(8,128)(2,1)S(1)} %get-tuple-element.17), channel_id=1, source_target_pairs={{64,0},{65,1},{66,2},{67,3},{68,4},{69,5},{70,6},{71,7},{72,8},{73... | collective-permute-start | bytes 393224 | tf_op jit(solution)/shard_map/ppermute | solution.py:299
  108.3 11.5 %all-to-all-start.2 = ((bf16[8,64,256]{2,1,0:T(8,128)(2,1)}), bf16[8,64,256]{2,1,0:T(8,128)(2,1)S(1)}, u32[]{:S(2)}, u32[]{:S(2)}) async-start(bf16[8,64,256]{2,1,0:T(8,128)(2,1)} %pad_maximum_fusion.1), calls=%async_computation.2 | async-start | bytes 524288 | tf_op jit(solution)/shard_map/all_to_all | solution.py:231
  121.1 35.5 %all-to-all-start.4 = ((f32[512,1,128]{2,1,0:T(1,128)}), f32[512,1,128]{2,1,0:T(1,128)S(1)}, u32[]{:S(2)}, u32[]{:S(2)}) async-start(f32[512,1,128]{2,1,0:T(1,128)} %bitcast.22), calls=%async_computation.4 | async-start | bytes 524288 | tf_op jit(solution)/shard_map/all_to_all | solution.py:355
  136.1 8.3 %collective-permute-start.5 = (bf16[512,128]{1,0:T(8,128)(2,1)S(1)}, bf16[512,128]{1,0:T(8,128)(2,1)S(1)}, u32[]{:S(2)}, u32[]{:S(2)}) collective-permute-start(bf16[512,128]{1,0:T(8,128)(2,1)S(1)} %slice.31), channel_id=1, source_target_pairs={{0,64},{1,65},{2,66},{3,67},{4,68},{5,69},{6,70},{7,71},{8,72},{9,... | collective-permute-start | bytes 393224 | tf_op jit(solution)/shard_map/ppermute | solution.py:335
  156.6 16.6 %all-to-all-start.3 = ((bf16[8,64,1280]{2,1,0:T(8,128)(2,1)}), bf16[8,64,1280]{2,1,0:T(8,128)(2,1)S(1)}, u32[]{:S(2)}, u32[]{:S(2)}) async-start(bf16[8,64,1280]{2,1,0:T(8,128)(2,1)} %bitcast.13), calls=%async_computation.3 | async-start | bytes 2621440 | tf_op jit(solution)/shard_map/all_to_all | solution.py:231
  174.1 41.0 %all-to-all-start.5 = ((f32[512,1,128]{2,1,0:T(1,128)}), f32[512,1,128]{2,1,0:T(1,128)S(1)}, u32[]{:S(2)}, u32[]{:S(2)}) async-start(f32[512,1,128]{2,1,0:T(1,128)} %reshape.139), calls=%async_computation.5 | async-start | bytes 524288 | tf_op jit(solution)/shard_map/all_to_all | solution.py:359
  198.5 20.6 %collective-permute-start.6 = (bf16[2,1,64,512]{3,2,1,0:T(8,128)(2,1)S(1)}, bf16[2,1,64,512]{3,2,1,0:T(8,128)(2,1)S(1)}, u32[]{:S(2)}, u32[]{:S(2)}) collective-permute-start(bf16[2,1,64,512]{3,2,1,0:T(8,128)(2,1)S(1)} %reshape.137), channel_id=1, source_target_pairs={{64,0},{65,1},{66,2},{67,3},{68,4},{69,5},{70,6},{71,7},{72,8},{73... | collective-permute-start | bytes 393224 | tf_op jit(solution)/shard_map/ppermute | solution.py:405
Sparse Core Ops, SparseCore 0:
  24.8 56.6 all-gather.1

commit v3 on v2

v3 whole, which is shorter than its diff:
```python
import functools
import math

import jax
import jax.numpy as jnp
from jax import lax
from jax.experimental import pallas as pl
from jax.experimental.pallas import tpu as pltpu
from jax.sharding import PartitionSpec as P

HEAD = 128
HALF = 512
TILE = 256
RATIO = 8
KV = 4
RANK = 8
UNITS = 8
PLANES = 8
SHARD = 512
ROWS = 64
SCALE = 1.0 / math.sqrt(HEAD)
ADAPTER_SCALE = 2.0
VMEM = 48 * 1024 * 1024
F32 = jnp.float32
BF16 = jnp.bfloat16


def dot_nt(a, b):
    return lax.dot_general(a, b, (((1,), (1,)), ((), ())), preferred_element_type=F32)


def dot_nn(a, b):
    return lax.dot_general(a, b, (((1,), (0,)), ((), ())), preferred_element_type=F32)


def weights_kernel(
    flags, q_ref, k_ref, kp_ref, do_ref, own_ref, prev_ref, dv_ref, dvp_ref, acc
):
    head = pl.program_id(0)
    factor = SCALE * math.log2(math.e)

    @pl.when(head == 0)
    def _():
        acc[...] = jnp.zeros_like(acc)

    def tiles(full):
        for r in range(HALF // TILE):
            cols = pl.ds(r * TILE, TILE)
            q = q_ref[cols, :]
            key_place = lax.broadcasted_iota(jnp.int32, (TILE, TILE), 0)
            query_place = lax.broadcasted_iota(jnp.int32, (TILE, TILE), 1)
            scores = dot_nt(k_ref[cols, :], q)
            scores = jnp.where(key_place <= query_place, scores, -jnp.inf)
            parts = [(own_ref, r * TILE, scores)]
            sources = [(own_ref, k_ref, t) for t in range(r)]
            if full:
                sources += [(prev_ref, kp_ref, t) for t in range(HALF // TILE)]
            for place, keys, t in sources:
                parts.append((place, t * TILE, dot_nt(keys[pl.ds(t * TILE, TILE), :], q)))
            top = functools.reduce(
                jnp.maximum, [jnp.max(scores, axis=0, keepdims=True) for _, _, scores in parts]
            )
            raised = [
                (place, at, jnp.exp2((scores - top) * factor)) for place, at, scores in parts
            ]
            total = sum(jnp.sum(e, axis=0, keepdims=True) for _, _, e in raised)
            inverse = 1.0 / total
            for place, at, e in raised:
                place[0, pl.ds(at, TILE), cols] = (e * inverse).astype(BF16)

    @pl.when(flags[head] > 0)
    def _():
        tiles(True)

    @pl.when(flags[head] == 0)
    def _():
        tiles(False)

    acc[pl.ds(HALF, TILE), :] += dot_nn(own_ref[0, pl.ds(0, TILE), :], do_ref[...])
    acc[pl.ds(HALF + TILE, TILE), :] += dot_nn(
        own_ref[0, pl.ds(TILE, TILE), pl.ds(TILE, TILE)], do_ref[pl.ds(TILE, TILE), :]
    )

    @pl.when(flags[head] > 0)
    def _():
        acc[pl.ds(0, HALF), :] += dot_nn(prev_ref[0], do_ref[...])

    @pl.when(head == RATIO - 1)
    def _():
        dv_ref[...] = acc[pl.ds(HALF, HALF), :]
        dvp_ref[...] = acc[pl.ds(0, HALF), :].astype(BF16)


def score_grad_kernel(
    flags,
    own_ref,
    prev_ref,
    q_ref,
    k_ref,
    kp_ref,
    do_ref,
    v_ref,
    vp_ref,
    dq_ref,
    dk_ref,
    dkp_ref,
    acc,
    kt,
):
    head = pl.program_id(0)

    @pl.when(head == 0)
    def _():
        acc[...] = jnp.zeros_like(acc)
        kt[:, pl.ds(0, HALF)] = kp_ref[...].astype(F32).T.astype(BF16)
        kt[:, pl.ds(HALF, HALF)] = k_ref[...].astype(F32).T.astype(BF16)

    def tiles(full):
        for r in range(HALF // TILE):
            cols = pl.ds(r * TILE, TILE)
            q = q_ref[cols, :]
            do = do_ref[cols, :]
            sources = [(own_ref, v_ref, t * TILE, HALF) for t in range(r + 1)]
            if full:
                sources += [(prev_ref, vp_ref, t * TILE, 0) for t in range(HALF // TILE)]
            parts = []
            for place, values, at, base in sources:
                p = place[0, pl.ds(at, TILE), cols].astype(F32)
                parts.append((p, dot_nt(values[pl.ds(at, TILE), :], do), at + base))
            delta = sum(jnp.sum(p * d, axis=0, keepdims=True) for p, d, _ in parts)
            dq = jnp.zeros((HEAD, TILE), F32)
            for p, d, at in parts:
                score_grad = (p * (d - delta)).astype(BF16)
                dq = dq + dot_nn(kt[:, pl.ds(at, TILE)], score_grad)
                acc[pl.ds(at, TILE), :] += dot_nn(score_grad, q)
            dq_ref[cols, :] = (dq * SCALE).T.astype(BF16)

    @pl.when(flags[head] > 0)
    def _():
        tiles(True)

    @pl.when(flags[head] == 0)
    def _():
        tiles(False)

    @pl.when(head == RATIO - 1)
    def _():
        dk_ref[...] = acc[pl.ds(HALF, HALF), :] * SCALE
        dkp_ref[...] = (acc[pl.ds(0, HALF), :] * SCALE).astype(BF16)


def pack_kernel(q_ref, do_ref, k_ref, kb_ref, out_ref):
    wide = RATIO * HEAD
    out_ref[0, :, pl.ds(0, wide)] = q_ref[0, 0]
    out_ref[0, :, pl.ds(wide, wide)] = do_ref[0, 0]
    out_ref[0, :, pl.ds(2 * wide, HEAD)] = k_ref[0, 0]
    out_ref[0, :, pl.ds(2 * wide + HEAD, HEAD)] = kb_ref[0, 0]


def unpack_kernel(in_ref, dq_ref, dk_ref, sums_ref):
    wide = RATIO * HEAD
    dq_ref[0, 0] = in_ref[0, :, pl.ds(0, wide)]
    dk_ref[0, 0] = in_ref[0, :, pl.ds(wide, HEAD)]
    high = in_ref[0, :, pl.ds(wide + HEAD, HEAD)].astype(F32)
    sums_ref[...] = high + in_ref[0, :, pl.ds(wide + 2 * HEAD, HEAD)].astype(F32)


def values_kernel(odd, x_ref, mine_ref, other_ref, down_ref, up_ref, out_ref):
    up = up_ref[...].astype(F32)
    half = SHARD // 2
    for s in range(2):
        low = dot_nn(x_ref[:, pl.ds(s * SHARD, SHARD)], down_ref[...])
        values = ADAPTER_SCALE * lax.dot_general(
            low,
            up,
            (((1,), (0,)), ((), ())),
            preferred_element_type=F32,
            precision=lax.Precision.HIGHEST,
        )
        for part, first in ((mine_ref, odd[0]), (other_ref, 1 - odd[0])):
            columns = pl.ds(pl.multiple_of(s * SHARD + first * half, half), half)
            values = values + dot_nn(x_ref[:, columns], part[...])
        values = values.astype(BF16)
        for g in range(KV):
            for c in range(UNITS):
                out_ref[s * KV + g, :, pl.ds((1 + c) * HEAD, HEAD)] = values[
                    c * ROWS : (c + 1) * ROWS, g * HEAD : (g + 1) * HEAD
                ]


def merge_kernel(parts_ref, own_ref, next_ref, out_ref):
    del parts_ref
    for c in range(UNITS):
        rows = pl.ds(c * ROWS, ROWS)
        out_ref[c] = (own_ref[rows, :] + next_ref[rows, :].astype(F32)).astype(BF16)


def values_sum_kernel(parts_ref, out_ref):
    for c in range(UNITS):
        total = jnp.zeros((ROWS, HEAD), F32)
        for j in range(UNITS):
            total = total + parts_ref[j, :, pl.ds((1 + c) * HEAD, HEAD)].astype(F32)
        out_ref[pl.ds(c * ROWS, ROWS), :] = total.astype(BF16)


def adapter_kernel(dv_ref, x_ref, low_ref, up_ref, out_ref):
    width = x_ref.shape[1]
    part = x_ref.shape[0] // 2
    down = jnp.zeros((RANK, width), F32)
    for s in range(2):
        pulled = jnp.zeros((RANK, part), F32)
        for g in range(KV):
            pulled = pulled + dot_nt(up_ref[:, pl.ds(g * HEAD, HEAD)], dv_ref[s * KV + g])
        down = down + dot_nn(pulled.astype(BF16), x_ref[pl.ds(s * part, part), :])
    pieces = [down[:, c * HEAD : (c + 1) * HEAD] for c in range(width // HEAD)]
    for g in range(KV):
        up = jnp.zeros((RANK, HEAD), F32)
        for s in range(2):
            up = up + lax.dot_general(
                low_ref[s],
                dv_ref[s * KV + g].astype(F32),
                (((1,), (0,)), ((), ())),
                preferred_element_type=F32,
                precision=lax.Precision.HIGHEST,
            )
        pieces.append(up)
    out_ref[...] = jnp.zeros_like(out_ref)
    for c, piece in enumerate(pieces):
        spot = (c % PLANES) * UNITS + c // PLANES
        out_ref[pl.ds(spot * RANK, RANK), :] = piece


def call(kernel, flops, nbytes, **keywords):
    return pl.pallas_call(
        kernel,
        compiler_params=pltpu.CompilerParams(vmem_limit_bytes=VMEM),
        cost_estimate=pl.CostEstimate(flops=flops, bytes_accessed=nbytes, transcendentals=0),
        **keywords,
    )


def body(x, queries, keys, frozen, down_weight, up_weight, grads, mask):
    seq_devices = lax.axis_size("seq")
    weight_devices = lax.axis_size("wt")
    devices = seq_devices * weight_devices
    sequences, _, rows, width = x.shape
    tokens = sequences * rows
    y_planes = PLANES
    both = ("seq", "wt")
    groups = [[UNITS * y + j for j in range(UNITS)] for y in range(y_planes)]
    smem = pl.BlockSpec(memory_space=pltpu.SMEM)

    def flat(y, j, w):
        return (y * UNITS + j) * weight_devices + w

    everywhere = [
        (y, j, w) for y in range(y_planes) for j in range(UNITS) for w in range(weight_devices)
    ]
    from_before = [
        (
            flat(y, j, w),
            flat(y + 1, j, w) if y + 1 < y_planes else flat(0, j, (w + 1) % weight_devices),
        )
        for y, j, w in everywhere
    ]
    to_before = [(b, a) for a, b in from_before]
    turned = [(flat(y, w, j), flat(y, j, w)) for y, j, w in everywhere]
    next_plane = [(i, i ^ UNITS) for i in range(seq_devices)]
    same_unit = [
        [flat(y, j, w) for y in range(PLANES) for w in range(weight_devices)] for j in range(UNITS)
    ]

    def swap(block):
        return lax.all_to_all(
            block, "seq", split_axis=0, concat_axis=0, axis_index_groups=groups, tiled=True
        )

    place = lax.axis_index("seq")
    parity = (place // UNITS) % 2
    kv_head = place % KV
    my_mask = lax.dynamic_slice_in_dim(mask, kv_head * RATIO, RATIO, 0)
    flags = jnp.where(parity == 1, 1 - my_mask, my_mask).astype(jnp.int32)

    x_rows = x.reshape(tokens, width)
    wide = RATIO * HEAD

    low = jnp.dot(x_rows, down_weight, preferred_element_type=F32)
    low_parts = jnp.transpose(low.reshape(sequences, rows, RANK), (0, 2, 1))

    piece = lax.dynamic_slice_in_dim(frozen, parity * (SHARD // 2), SHARD // 2, 0)
    piece = lax.ppermute(piece, both, turned)
    keys_before = lax.ppermute(keys, both, from_before)
    token_wide = pl.BlockSpec((1, 1, rows, wide), lambda i: (i // KV, 0, 0, i % KV))
    token_head = pl.BlockSpec((1, 1, rows, HEAD), lambda i: (i // KV, 0, 0, i % KV))
    packed = 2 * (wide + HEAD)
    outgoing = call(
        pack_kernel,
        0,
        5 << 20,
        grid=(UNITS,),
        in_specs=[token_wide, token_wide, token_head, token_head],
        out_specs=pl.BlockSpec((1, rows, packed), lambda i: (i, 0, 0)),
        out_shape=pltpu.HBM((UNITS, rows, packed), BF16),
        name="pack",
    )(queries, grads, keys, keys_before)
    outgoing, piece = lax.optimization_barrier((outgoing, piece))
    first = swap(outgoing).reshape(HALF, packed)
    piece_other = lax.ppermute(piece, "seq", next_plane)
    down_part = lax.dynamic_slice_in_dim(down_weight, place % UNITS * SHARD, SHARD, 0)
    first, piece_other = lax.optimization_barrier((first, piece_other))
    features = jnp.transpose(x.reshape(sequences, rows, UNITS, SHARD), (2, 1, 0, 3))
    features = features.reshape(UNITS, rows, sequences * SHARD)
    features, first = lax.optimization_barrier((features, first))
    x_parts = swap(features).reshape(HALF, sequences * SHARD)

    head_block = pl.BlockSpec((HALF, HEAD), lambda h: (0, h))
    grad_block = pl.BlockSpec((HALF, HEAD), lambda h: (0, RATIO + h))
    key_block = pl.BlockSpec((HALF, HEAD), lambda h: (0, 2 * RATIO))
    key_prev_block = pl.BlockSpec((HALF, HEAD), lambda h: (0, 2 * RATIO + 1))
    prev_block = pl.BlockSpec((HALF, HEAD), lambda h: (0, 0))
    p_block = pl.BlockSpec((1, HALF, HALF), lambda h: (h, 0, 0))
    p_shape = pltpu.HBM((RATIO, HALF, HALF), BF16)

    product = 2 * RATIO * HALF * HALF * 3 // 2 * HEAD

    def whole(*shape):
        return pl.BlockSpec(shape, lambda i: (0,) * len(shape))

    x_block = whole(tokens, width)
    prev_one = whole(HALF, HEAD)
    weights_own, weights_prev, dv_own, dv_prev = call(
        weights_kernel,
        2 * product,
        10 << 20,
        grid=(RATIO,),
        in_specs=[smem, head_block, key_block, key_prev_block, grad_block],
        out_specs=(p_block, p_block, prev_block, prev_block),
        out_shape=(p_shape, p_shape, pltpu.HBM((HALF, HEAD), F32), pltpu.HBM((HALF, HEAD), BF16)),
        scratch_shapes=[pltpu.VMEM((2 * HALF, HEAD), F32)],
        name="weights",
    )(flags, first, first, first, first)
    weights_own = pltpu.with_memory_space_constraint(weights_own, pltpu.HBM)
    weights_prev = pltpu.with_memory_space_constraint(weights_prev, pltpu.HBM)

    dv_next = lax.ppermute(dv_prev, both, to_before)
    parts_shape = pltpu.HBM((UNITS, rows, (1 + UNITS) * HEAD), BF16)
    parts = call(
        values_kernel,
        2 * tokens * width * KV * HEAD,
        4 << 20,
        grid=(1,),
        in_specs=[
            smem,
            whole(HALF, sequences * SHARD),
            whole(SHARD // 2, KV * HEAD),
            whole(SHARD // 2, KV * HEAD),
            whole(SHARD, RANK),
            whole(RANK, KV * HEAD),
        ],
        out_specs=whole(UNITS, rows, (1 + UNITS) * HEAD),
        out_shape=parts_shape,
        name="values",
    )(parity.astype(jnp.int32).reshape(1), x_parts, piece, piece_other, down_part, up_weight)
    merged = call(
        merge_kernel,
        0,
        1 << 19,
        grid=(1,),
        in_specs=[pl.BlockSpec(memory_space=pl.ANY), prev_one, prev_one],
        out_specs=whole(UNITS, rows, HEAD),
        out_shape=parts_shape,
        input_output_aliases={0: 0},
        name="merge",
    )(parts, dv_own, dv_next)
    third = swap(merged)
    v_unit = call(
        values_sum_kernel,
        1 << 20,
        1 << 20,
        grid=(1,),
        in_specs=[whole(UNITS, rows, (1 + UNITS) * HEAD)],
        out_specs=whole(HALF, HEAD),
        out_shape=pltpu.HBM((HALF, HEAD), BF16),
        name="values_sum",
    )(third)
    v_prev = lax.ppermute(v_unit, both, from_before)

    pieces = width // HEAD + KV
    sums = call(
        adapter_kernel,
        4 * tokens * width * RANK,
        3 << 20,
        grid=(1,),
        in_specs=[
            whole(UNITS, rows, HEAD),
            x_block,
            whole(sequences, RANK, rows),
            whole(RANK, KV * HEAD),
        ],
        out_specs=whole(devices, HEAD),
        out_shape=pltpu.HBM((devices, HEAD), F32),
        name="adapter",
    )(third, x_rows, low_parts, up_weight)
    sums, v_prev = lax.optimization_barrier((sums, v_prev))
    scattered = lax.all_to_all(sums, both, split_axis=0, concat_axis=0, tiled=True)
    mine = jnp.sum(scattered, axis=0) * (ADAPTER_SCALE / math.sqrt(tokens * devices))
    peers = PLANES * weight_devices
    gathered = lax.all_to_all(
        jnp.broadcast_to(mine[None], (peers, HEAD)),
        both,
        split_axis=0,
        concat_axis=0,
        axis_index_groups=same_unit,
        tiled=True,
    )
    high = gathered.astype(BF16)
    rest = (gathered - high.astype(F32)).astype(BF16)

    dq_unit, dk_own, dk_prev = call(
        score_grad_kernel,
        3 * product,
        12 << 20,
        grid=(RATIO,),
        in_specs=[
            smem,
            p_block,
            p_block,
            head_block,
            key_block,
            key_prev_block,
            grad_block,
            prev_block,
            prev_block,
        ],
        out_specs=(head_block, prev_block, prev_block),
        out_shape=(
            pltpu.HBM((HALF, wide), BF16),
            pltpu.HBM((HALF, HEAD), F32),
            pltpu.HBM((HALF, HEAD), BF16),
        ),
        scratch_shapes=[pltpu.VMEM((2 * HALF, HEAD), F32), pltpu.VMEM((HEAD, 2 * HALF), BF16)],
        name="score_grad",
    )(
        flags,
        weights_own,
        weights_prev,
        first,
        first,
        first,
        first,
        v_unit,
        v_prev,
    )
    dk_next = lax.ppermute(dk_prev, both, to_before)
    dk_unit = (dk_own + dk_next.astype(F32)).astype(BF16)

    returning = jnp.concatenate(
        [
            dq_unit.reshape(UNITS, rows, wide),
            dk_unit.reshape(UNITS, rows, HEAD),
            jnp.broadcast_to(high[None], (UNITS, peers, HEAD)),
            jnp.broadcast_to(rest[None], (UNITS, peers, HEAD)),
        ],
        axis=2,
    )
    returned = swap(returning)

    query_grad, key_grad, totals = call(
        unpack_kernel,
        0,
        4 << 20,
        grid=(UNITS,),
        in_specs=[pl.BlockSpec((1, rows, wide + 3 * HEAD), lambda i: (i, 0, 0))],
        out_specs=(token_wide, token_head, pl.BlockSpec((peers, HEAD), lambda i: (i, 0))),
        out_shape=(
            jax.ShapeDtypeStruct((sequences, 1, rows, KV * wide), BF16),
            jax.ShapeDtypeStruct((sequences, 1, rows, KV * HEAD), BF16),
            jax.ShapeDtypeStruct((devices, HEAD), F32),
        ),
        name="unpack",
    )(returned)
    totals = totals.reshape(devices // RANK, RANK, HEAD)[:pieces]
    down_grad = jnp.transpose(totals[: width // HEAD], (0, 2, 1)).reshape(width, RANK)
    up_grad = jnp.transpose(totals[width // HEAD :], (1, 0, 2)).reshape(RANK, KV * HEAD)
    return (query_grad, key_grad, down_grad, up_grad)


def solution(mesh):
    tokens = P(None, "wt", "seq", None)
    return jax.shard_map(
        body,
        mesh=mesh,
        in_specs=(tokens, tokens, tokens, P("wt", None), P(), P(), tokens, P()),
        out_specs=(tokens, tokens, P(), P()),
        check_vma=False,
    )
```

time: 228 us -> 209 us (0.917)
  blocking collectives: 0 us -> 46.4 us
  waiting for transfers between devices: 71 us -> 39.8 us
  starting transfers between devices: 88.2 us -> 64 us
  between operations: 14.4 us -> 0.92 us
  Pallas kernels: 31.5 us -> 38.2 us
    all_to_all x0 -> x2, blocking collectives: none -> 46.4 us  [swap(): lax.all_to_all(block, 'seq', split_axis=0, concat_axis=0, axis_index_grou...]
    all_to_all x4 -> x2, waiting for transfers between devices: 38.7 us -> 19.2 us  [swap(): lax.all_to_all(block, 'seq', split_axis=0, concat_axis=0, axis_index_grou...]
    all_to_all x1, starting transfers between devices: 24.1 us -> 12.3 us  [body(): lax.all_to_all(jnp.broadcast_to(mine[None], (peers, HEAD)), both, split_a...]
    ppermute x6 -> x5, starting transfers between devices: 23.5 us -> 16.8 us  [the longest x1 5.15 us: body(): dk_next = lax.ppermute(dk_prev, both, to_before)]
    pallas_call x3 -> x6, Pallas kernels: 17.9 us -> 24.4 us  [the longest x1 10.8 us: body(): call(weights_kernel, 2 * product, 10 << 20, grid=(RATIO,), in_specs=[smem...]
    all_gather x1 -> x0, waiting for transfers between devices: 6.23 us -> none  [body(): lax.all_gather(shard, 'seq', axis=0, axis_index_groups=columns_of_y, tile...]
    reshape x12 -> x3, local copies, waits for them, and re-layouts: 8.7 us -> 3.86 us  [the longest x1 2.59 us: body(): features = features.reshape(UNITS, rows, sequences * SHARD)]
    unnamed x16 -> x22, local copies, waits for them, and re-layouts: 3.32 us -> 6.86 us
  transfers between devices with their start and end apart: 14 -> 10, of which waited for: 8 -> 5; matrix products, arithmetic and copies ran while one was open for 7% -> 5% of each run, Pallas kernels for 13% -> 16%
where the time goes in v3:
time: 209 us; the launch traced here: 208 us
  starting transfers between devices  64 us (31%)
  blocking collectives  46.4 us (22%)
  waiting for transfers between devices  39.8 us (19%)
  Pallas kernels  38.2 us (18%)
  local copies, waits for them, and re-layouts  14.8 us (7%)
  other arithmetic  3 us (1%)
    all_to_all x2, blocking collectives, swap(): lax.all_to_all(block, 'seq', split_axis=0, concat_axis=0, axis_index_grou...  46.4 us
    all_to_all x2, waiting for transfers between devices, swap(): lax.all_to_all(block, 'seq', split_axis=0, concat_axis=0, axis_index_grou...  19.2 us
    all_to_all x2, starting transfers between devices, swap(): lax.all_to_all(block, 'seq', split_axis=0, concat_axis=0, axis_index_grou...  18.7 us
    all_to_all x1, starting transfers between devices, body(): lax.all_to_all(sums, both, split_axis=0, concat_axis=0, tiled=True)  12.6 us
    pallas_call x1, Pallas kernels, body(): call(score_grad_kernel, 3 * product, 12 << 20, grid=(RATIO,), in_specs=[s...  12.4 us
    all_to_all x1, starting transfers between devices, body(): lax.all_to_all(jnp.broadcast_to(mine[None], (peers, HEAD)), both, split_a...  12.3 us
    pallas_call x1, Pallas kernels, body(): call(weights_kernel, 2 * product, 10 << 20, grid=(RATIO,), in_specs=[smem...  10.8 us
    all_to_all x1, waiting for transfers between devices, body(): lax.all_to_all(jnp.broadcast_to(mine[None], (peers, HEAD)), both, split_a...  10.7 us
  transfers between devices with their start and end apart: 10, of which 5 were waited for; matrix products, arithmetic and copies ran while one was open for 5% of the time, Pallas kernels for 16%

profile of v3, /device:TPU:1, one launch (start us, length us, event | category | flops | bytes accessed | tf_op | source)
XLA Modules:
  0.0 207.6 jit_solution(5321904018953950313)
XLA Ops:
  0.7 1.0 copy-done
  1.7 4.5 %collective-permute-start.1 = (bf16[256,512]{1,0:T(8,128)(2,1)S(1)}, bf16[256,512]{1,0:T(8,128)(2,1)S(1)}, u32[]{:S(2)}, u32[]{:S(2)}) collective-permute-start(bf16[256,512]{1,0:T(8,128)(2,1)S(1)} %constant_dynamic-slice_fusion.1), channel_id=1, source_target_pairs={{0,0},{8,1},{16,2},{24,3},{32,4},{40,5},{48,6},{56,7},{1,8},{9,9},... | collective-permute-start | bytes 786440 | tf_op jit(solution)/shard_map/ppermute | solution.py:291
  6.2 3.2 %collective-permute-start = (bf16[2,1,64,512]{3,2,1,0:T(8,128)(2,1)}, bf16[2,1,64,512]{3,2,1,0:T(8,128)(2,1)S(1)}, u32[]{:S(2)}, u32[]{:S(2)}) collective-permute-start(bf16[2,1,64,512]{3,2,1,0:T(8,128)(2,1)} %k_ref.1), channel_id=1, source_target_pairs={{0,64},{1,65},{2,66},{3,67},{4,68},{5,69},{6,70},{7,71},{8,72},{9,... | collective-permute-start | bytes 393224 | tf_op jit(solution)/shard_map/ppermute | solution.py:292
  9.4 4.5 %collective-permute-done.kb_ref = bf16[2,1,64,512]{3,2,1,0:T(8,128)(2,1)S(1)} collective-permute-done((bf16[2,1,64,512]{3,2,1,0:T(8,128)(2,1)}, bf16[2,1,64,512]{3,2,1,0:T(8,128)(2,1)S(1)}, u32[]{:S(2)}, u32[]{:S(2)}) %collective-permute-start) | collective-permute-done | bytes 131104 | tf_op jit(solution)/shard_map/ppermute | solution.py:292
  13.9 1.2 copy-done.2
  15.2 1.2 copy-done.3
  17.3 3.2 %pack.1 = bf16[8,64,2304]{2,1,0:T(8,128)(2,1)} custom-call(bf16[2,1,64,4096]{3,2,1,0:T(8,128)(2,1)S(1)} %copy-done.2, bf16[2,1,64,4096]{3,2,1,0:T(8,128)(2,1)S(1)} %copy-done.3, bf16[2,1,64,512]{3,2,1,0:T(8,128)(2,1)S(1)} %copy-done.6, bf16[2,1,64,512]{3,2,1,0:T(8,128)(2,1)S(1)} %collective-permute-done.kb_ref), custom_call_target="tpu_custom_call" | custom-call | bytes 5242880 | tf_op jit(solution)/shard_map/pack/pallas_call | solution.py:296
  20.5 14.5 %all-to-all-start = ((bf16[8,64,2304]{2,1,0:T(8,128)(2,1)}), bf16[8,64,2304]{2,1,0:T(8,128)(2,1)S(1)}, u32[]{:S(2)}, u32[]{:S(2)}) async-start(bf16[8,64,2304]{2,1,0:T(8,128)(2,1)} %pack.1), calls=%async_computation | async-start | bytes 4718592 | tf_op jit(solution)/shard_map/all_to_all | solution.py:274
  35.0 1.6 copy.19
  36.6 1.9 collective-permute-start.2
  38.6 2.0 copy.15
  40.7 2.6 %reshape.71 = bf16[8,64,1024]{2,1,0:T(8,128)(2,1)} reshape(bf16[8,64,2,512]{3,2,1,0:T(2,128)(2,1)} %copy.15) | data formatting | bytes 2097152 | tf_op jit(solution)/shard_map/reshape | solution.py:312
  43.3 1.4 collective-permute-done.2.other_ref
  44.7 19.2 %all-to-all-done = bf16[8,64,2304]{2,1,0:T(8,128)(2,1)S(1)} async-done(((bf16[8,64,2304]{2,1,0:T(8,128)(2,1)}), bf16[8,64,2304]{2,1,0:T(8,128)(2,1)S(1)}, u32[]{:S(2)}, u32[]{:S(2)}) %all-to-all-start) | async-done | bytes 2359328 | tf_op jit(solution)/shard_map/all_to_all | solution.py:274
  64.0 4.2 %all-to-all-start.1 = ((bf16[8,64,1024]{2,1,0:T(8,128)(2,1)}), bf16[8,64,1024]{2,1,0:T(8,128)(2,1)}, u32[]{:S(2)}, u32[]{:S(2)}) async-start(bf16[8,64,1024]{2,1,0:T(8,128)(2,1)} %reshape.71), calls=%async_computation.1 | async-start | bytes 2097152 | tf_op jit(solution)/shard_map/all_to_all | solution.py:274
  68.3 10.8 %weights.1 = (bf16[8,512,512]{2,1,0:T(8,128)(2,1)}, bf16[8,512,512]{2,1,0:T(8,128)(2,1)}, f32[512,128]{1,0:T(8,128)}, bf16[512,128]{1,0:T(8,128)(2,1)}) custom-call(s32[8]{0:T(128)S(1)} %broadcast_select_fusion.flags, bf16[512,2304]{1,0:T(8,128)(2,1)S(1)} %bitcast.39, bf16[512,2304]{1,0:T(8,128)(2,1)S(1)} %bitcast.40, bf16[512,2304]{1,0:T(8,128)(2,1)S(1)} %bitcast.41, ...), custom_call_target="tpu_custom_call" | custom-call | flops 1610612736 | bytes 10485760 | tf_op jit(solution)/shard_map/weights/pallas_call | solution.py:331
  79.1 3.6 %collective-permute-start.3 = (bf16[512,128]{1,0:T(8,128)(2,1)}, bf16[512,128]{1,0:T(8,128)(2,1)}, u32[]{:S(2)}, u32[]{:S(2)}) collective-permute-start(bf16[512,128]{1,0:T(8,128)(2,1)} %get-tuple-element.31), channel_id=1, source_target_pairs={{64,0},{65,1},{66,2},{67,3},{68,4},{69,5},{70,6},{71,7},{72,8},{73... | collective-permute-start | bytes 393224 | tf_op jit(solution)/shard_map/ppermute | solution.py:345
  82.7 1.3 constant_dynamic-slice_fusion
  84.9 5.2 %values.1.parts_ref = bf16[8,64,1152]{2,1,0:T(8,128)(2,1)} custom-call(s32[1]{0:T(128)} %bitcast.2.odd, bf16[512,1024]{1,0:T(8,128)(2,1)} %bitcast.3.x_ref, bf16[256,512]{1,0:T(8,128)(2,1)S(1)} %collective-permute-done.1.mine_ref, bf16[256,512]{1,0:T(8,128)(2,1)S(1)} %collective-permute-done.2.other_ref, bf16[512,8]{1,0:T(8,128)(2,1)S(1)} %copy.18.down_ref, ...), custom_call_target="tpu_custom_call" | custom-call | flops 536870912 | bytes 4194304 | tf_op jit(solution)/shard_map/values/pallas_call | solution.py:347
  90.1 1.6 merge.1
  91.7 23.3 %all_to_all.38.parts_ref.dv_ref = bf16[8,64,1152]{2,1,0:T(8,128)(2,1)S(1)} all-to-all(bf16[8,64,1152]{2,1,0:T(8,128)(2,1)} %merge.1), channel_id=1, replica_groups={{0,8,16,24,32,40,48,56},{64,72,80,88,96,104,112,120},{128,136,144,152,1..., dimensions={0} | all-to-all | bytes 2359296 | tf_op jit(solution)/shard_map/all_to_all | solution.py:274
  115.8 2.0 collective-permute-start.4
  118.4 1.4 adapter.1
  119.7 3.9 %collective-permute-done.4.vp_ref = bf16[512,128]{1,0:T(8,128)(2,1)S(1)} collective-permute-done((bf16[512,128]{1,0:T(8,128)(2,1)}, bf16[512,128]{1,0:T(8,128)(2,1)S(1)}, u32[]{:S(2)}, u32[]{:S(2)}) %collective-permute-start.4) | collective-permute-done | bytes 131104 | tf_op jit(solution)/shard_map/ppermute | solution.py:386
  123.6 12.6 %all-to-all-start.3 = ((f32[512,1,128]{2,1,0:T(1,128)}), f32[512,1,128]{2,1,0:T(1,128)S(1)}, u32[]{:S(2)}, u32[]{:S(2)}) async-start(f32[512,1,128]{2,1,0:T(1,128)} %bitcast.50), calls=%async_computation.3 | async-start | bytes 524288 | tf_op jit(solution)/shard_map/all_to_all | solution.py:405
  136.2 12.4 %score_grad.1 = (bf16[512,1024]{1,0:T(8,128)(2,1)}, f32[512,128]{1,0:T(8,128)}, bf16[512,128]{1,0:T(8,128)(2,1)}) custom-call(s32[8]{0:T(128)S(1)} %broadcast_select_fusion.flags, bf16[8,512,512]{2,1,0:T(8,128)(2,1)} %get-tuple-element.26.own_ref, bf16[8,512,512]{2,1,0:T(8,128)(2,1)} %get-tuple-element.27.prev_ref, bf16[512,2304]{1,0:T(8,128)(2,1)S(1)} %bitcast.43, ...), custom_call_target="tpu_custom_call" | custom-call | flops 2415919104 | bytes 12582912 | tf_op jit(solution)/shard_map/score_grad/pallas_call | solution.py:419
  148.7 5.2 %collective-permute-start.5 = (bf16[512,128]{1,0:T(8,128)(2,1)}, bf16[512,128]{1,0:T(8,128)(2,1)S(1)}, u32[]{:S(2)}, u32[]{:S(2)}) collective-permute-start(bf16[512,128]{1,0:T(8,128)(2,1)} %get-tuple-element.35), channel_id=1, source_target_pairs={{64,0},{65,1},{66,2},{67,3},{68,4},{69,5},{70,6},{71,7},{72,8},{73... | collective-permute-start | bytes 393224 | tf_op jit(solution)/shard_map/ppermute | solution.py:454
  155.0 12.3 %all-to-all-start.4 = ((f32[64,1,128]{2,1,0:T(1,128)}), f32[64,1,128]{2,1,0:T(1,128)S(1)}, u32[]{:S(2)}, u32[]{:S(2)}) async-start(f32[64,1,128]{2,1,0:T(1,128)} %broadcast_in_dim.6), calls=%async_computation.4 | async-start | bytes 65536 | tf_op jit(solution)/shard_map/all_to_all | solution.py:408
  168.3 10.7 %all-to-all-done.4 = f32[64,1,128]{2,1,0:T(1,128)S(1)} async-done(((f32[64,1,128]{2,1,0:T(1,128)}), f32[64,1,128]{2,1,0:T(1,128)S(1)}, u32[]{:S(2)}, u32[]{:S(2)}) %all-to-all-start.4) | async-done | bytes 32800 | tf_op jit(solution)/shard_map/all_to_all | solution.py:408
  179.1 1.4 pad_maximum_fusion
  180.5 23.1 %all_to_all.39.in_ref = bf16[8,64,1408]{2,1,0:T(8,128)(2,1)S(1)} all-to-all(bf16[8,64,1408]{2,1,0:T(8,128)(2,1)S(1)} %pad_maximum_fusion), channel_id=1, replica_groups={{0,8,16,24,32,40,48,56},{64,72,80,88,96,104,112,120},{128,136,144,152,1..., dimensions={0} | all-to-all | bytes 2883584 | tf_op jit(solution)/shard_map/all_to_all | solution.py:274
  203.6 2.7 %unpack.1 = (bf16[2,1,64,4096]{3,2,1,0:T(8,128)(2,1)}, bf16[2,1,64,512]{3,2,1,0:T(8,128)(2,1)}, f32[512,128]{1,0:T(8,128)S(1)}) custom-call(bf16[8,64,1408]{2,1,0:T(8,128)(2,1)S(1)} %all_to_all.39.in_ref), custom_call_target="tpu_custom_call" | custom-call | bytes 4194304 | tf_op jit(solution)/shard_map/unpack/pallas_call | solution.py:468
  (37 shorter events, 6.8 us)
Async XLA Ops:
  0.6 1.0 copy-start
  1.7 18.8 %collective-permute-start.1 = (bf16[256,512]{1,0:T(8,128)(2,1)S(1)}, bf16[256,512]{1,0:T(8,128)(2,1)S(1)}, u32[]{:S(2)}, u32[]{:S(2)}) collective-permute-start(bf16[256,512]{1,0:T(8,128)(2,1)S(1)} %constant_dynamic-slice_fusion.1), channel_id=1, source_target_pairs={{0,0},{8,1},{16,2},{24,3},{32,4},{40,5},{48,6},{56,7},{1,8},{9,9},... | collective-permute-start | bytes 786440 | tf_op jit(solution)/shard_map/ppermute | solution.py:291
  6.2 7.7 %collective-permute-start = (bf16[2,1,64,512]{3,2,1,0:T(8,128)(2,1)}, bf16[2,1,64,512]{3,2,1,0:T(8,128)(2,1)S(1)}, u32[]{:S(2)}, u32[]{:S(2)}) collective-permute-start(bf16[2,1,64,512]{3,2,1,0:T(8,128)(2,1)} %k_ref.1), channel_id=1, source_target_pairs={{0,64},{1,65},{2,66},{3,67},{4,68},{5,69},{6,70},{7,71},{8,72},{9,... | collective-permute-start | bytes 393224 | tf_op jit(solution)/shard_map/ppermute | solution.py:292
  13.9 1.2 copy-start.2
  15.2 1.2 copy-start.3
  16.4 0.9 copy-start.6
  20.5 43.4 %all-to-all-start = ((bf16[8,64,2304]{2,1,0:T(8,128)(2,1)}), bf16[8,64,2304]{2,1,0:T(8,128)(2,1)S(1)}, u32[]{:S(2)}, u32[]{:S(2)}) async-start(bf16[8,64,2304]{2,1,0:T(8,128)(2,1)} %pack.1), calls=%async_computation | async-start | bytes 4718592 | tf_op jit(solution)/shard_map/all_to_all | solution.py:274
  36.6 8.1 %collective-permute-start.2 = (bf16[256,512]{1,0:T(8,128)(2,1)S(1)}, bf16[256,512]{1,0:T(8,128)(2,1)S(1)}, u32[]{:S(2)}, u32[]{:S(2)}) collective-permute-start(bf16[256,512]{1,0:T(8,128)(2,1)S(1)} %collective-permute-done.1.mine_ref), channel_id=1, source_target_pairs={{0,64},{8,72},{16,80},{24,88},{32,96},{40,104},{48,112},{56,120},{... | collective-permute-start | bytes 786440 | tf_op jit(solution)/shard_map/ppermute | solution.py:308
  40.7 27.6 %copy-start.9 = (s32[32]{0:T(128)S(1)}, s32[32]{0:T(128)}, u32[]{:S(2)}) copy-start(s32[32]{0:T(128)} %param.15) | copy-start | bytes 388
  64.0 20.9 %all-to-all-start.1 = ((bf16[8,64,1024]{2,1,0:T(8,128)(2,1)}), bf16[8,64,1024]{2,1,0:T(8,128)(2,1)}, u32[]{:S(2)}, u32[]{:S(2)}) async-start(bf16[8,64,1024]{2,1,0:T(8,128)(2,1)} %reshape.71), calls=%async_computation.1 | async-start | bytes 2097152 | tf_op jit(solution)/shard_map/all_to_all | solution.py:274
  68.3 16.6 %copy-start.7 = (bf16[8,512]{1,0:T(8,128)(2,1)S(1)}, bf16[8,512]{1,0:T(8,128)(2,1)}, u32[]{:S(2)}) copy-start(bf16[8,512]{1,0:T(8,128)(2,1)} %up_ref.3) | copy-start | bytes 24580
  79.1 11.0 %collective-permute-start.3 = (bf16[512,128]{1,0:T(8,128)(2,1)}, bf16[512,128]{1,0:T(8,128)(2,1)}, u32[]{:S(2)}, u32[]{:S(2)}) collective-permute-start(bf16[512,128]{1,0:T(8,128)(2,1)} %get-tuple-element.31), channel_id=1, source_target_pairs={{64,0},{65,1},{66,2},{67,3},{68,4},{69,5},{70,6},{71,7},{72,8},{73... | collective-permute-start | bytes 393224 | tf_op jit(solution)/shard_map/ppermute | solution.py:345
  84.9 5.3 %copy-start.5 = (f32[512,128]{1,0:T(8,128)S(1)}, f32[512,128]{1,0:T(8,128)}, u32[]{:S(2)}) copy-start(f32[512,128]{1,0:T(8,128)} %get-tuple-element.30.own_ref) | copy-start | bytes 786436
  91.7 26.1 %copy-start.1 = (bf16[2,1,64,4096]{3,2,1,0:T(8,128)(2,1)S(1)}, bf16[2,1,64,4096]{3,2,1,0:T(8,128)(2,1)}, u32[]{:S(2)}) copy-start(bf16[2,1,64,4096]{3,2,1,0:T(8,128)(2,1)} %param.8) | copy-start | bytes 3145732
  91.7 26.1 %copy-start.8 = (bf16[4096,8]{0,1:T(8,128)(2,1)S(1)}, bf16[4096,8]{0,1:T(8,128)(2,1)}, u32[]{:S(2)}) copy-start(bf16[4096,8]{0,1:T(8,128)(2,1)} %param.12) | copy-start | bytes 196612
  115.8 20.4 %copy-start.4 = (bf16[512,128]{1,0:T(8,128)(2,1)S(1)}, bf16[512,128]{1,0:T(8,128)(2,1)}, u32[]{:S(2)}) copy-start(bf16[512,128]{1,0:T(8,128)(2,1)} %values_sum.1.v_ref) | copy-start | bytes 393220
  115.8 7.8 %collective-permute-start.4 = (bf16[512,128]{1,0:T(8,128)(2,1)}, bf16[512,128]{1,0:T(8,128)(2,1)S(1)}, u32[]{:S(2)}, u32[]{:S(2)}) collective-permute-start(bf16[512,128]{1,0:T(8,128)(2,1)} %values_sum.1.v_ref), channel_id=1, source_target_pairs={{0,64},{1,65},{2,66},{3,67},{4,68},{5,69},{6,70},{7,71},{8,72},{9,... | collective-permute-start | bytes 393224 | tf_op jit(solution)/shard_map/ppermute | solution.py:386
  123.6 30.2 %all-to-all-start.3 = ((f32[512,1,128]{2,1,0:T(1,128)}), f32[512,1,128]{2,1,0:T(1,128)S(1)}, u32[]{:S(2)}, u32[]{:S(2)}) async-start(f32[512,1,128]{2,1,0:T(1,128)} %bitcast.50), calls=%async_computation.3 | async-start | bytes 524288 | tf_op jit(solution)/shard_map/all_to_all | solution.py:405
  148.7 18.7 %collective-permute-start.5 = (bf16[512,128]{1,0:T(8,128)(2,1)}, bf16[512,128]{1,0:T(8,128)(2,1)S(1)}, u32[]{:S(2)}, u32[]{:S(2)}) collective-permute-start(bf16[512,128]{1,0:T(8,128)(2,1)} %get-tuple-element.35), channel_id=1, source_target_pairs={{64,0},{65,1},{66,2},{67,3},{68,4},{69,5},{70,6},{71,7},{72,8},{73... | collective-permute-start | bytes 393224 | tf_op jit(solution)/shard_map/ppermute | solution.py:454
  155.0 24.0 %all-to-all-start.4 = ((f32[64,1,128]{2,1,0:T(1,128)}), f32[64,1,128]{2,1,0:T(1,128)S(1)}, u32[]{:S(2)}, u32[]{:S(2)}) async-start(f32[64,1,128]{2,1,0:T(1,128)} %broadcast_in_dim.6), calls=%async_computation.4 | async-start | bytes 65536 | tf_op jit(solution)/shard_map/all_to_all | solution.py:408

commit v4 on v3

v4 whole, which is shorter than its diff:
```python
import functools
import math

import jax
import jax.numpy as jnp
from jax import lax
from jax.experimental import pallas as pl
from jax.experimental.pallas import tpu as pltpu
from jax.sharding import PartitionSpec as P

HEAD = 128
HALF = 512
TILE = 256
RATIO = 8
KV = 4
RANK = 8
UNITS = 8
PLANES = 8
SHARD = 512
ROWS = 64
BATCH = 2
SCALE = 1.0 / math.sqrt(HEAD)
ADAPTER_SCALE = 2.0
VMEM = 48 * 1024 * 1024
F32 = jnp.float32
BF16 = jnp.bfloat16


def dot_nt(a, b):
    return lax.dot_general(a, b, (((1,), (1,)), ((), ())), preferred_element_type=F32)


def dot_nn(a, b):
    return lax.dot_general(a, b, (((1,), (0,)), ((), ())), preferred_element_type=F32)


def weights_kernel(
    flags, q_ref, k_ref, kp_ref, do_ref, own_ref, prev_ref, dv_ref, dvp_ref, acc
):
    step = pl.program_id(0)
    factor = SCALE * math.log2(math.e)

    @pl.when(step == 0)
    def _():
        acc[...] = jnp.zeros_like(acc)

    def tiles(i, full):
        head = pl.ds(i * HEAD, HEAD)
        for r in range(HALF // TILE):
            cols = pl.ds(r * TILE, TILE)
            q = q_ref[cols, head]
            key_place = lax.broadcasted_iota(jnp.int32, (TILE, TILE), 0)
            query_place = lax.broadcasted_iota(jnp.int32, (TILE, TILE), 1)
            scores = dot_nt(k_ref[cols, :], q)
            scores = jnp.where(key_place <= query_place, scores, -jnp.inf)
            parts = [(own_ref, r * TILE, scores)]
            sources = [(own_ref, k_ref, t) for t in range(r)]
            if full:
                sources += [(prev_ref, kp_ref, t) for t in range(HALF // TILE)]
            for place, keys, t in sources:
                parts.append((place, t * TILE, dot_nt(keys[pl.ds(t * TILE, TILE), :], q)))
            top = functools.reduce(
                jnp.maximum, [jnp.max(scores, axis=0, keepdims=True) for _, _, scores in parts]
            )
            raised = [
                (place, at, jnp.exp2((scores - top) * factor)) for place, at, scores in parts
            ]
            total = sum(jnp.sum(e, axis=0, keepdims=True) for _, _, e in raised)
            inverse = 1.0 / total
            for place, at, e in raised:
                place[i, pl.ds(at, TILE), cols] = (e * inverse).astype(BF16)
        do = do_ref[:, head]
        acc[pl.ds(HALF, TILE), :] += dot_nn(own_ref[i, pl.ds(0, TILE), :], do)
        acc[pl.ds(HALF + TILE, TILE), :] += dot_nn(
            own_ref[i, pl.ds(TILE, TILE), pl.ds(TILE, TILE)], do[TILE:]
        )
        if full:
            acc[pl.ds(0, HALF), :] += dot_nn(prev_ref[i], do)

    for i in range(BATCH):

        @pl.when(flags[step * BATCH + i] > 0)
        def _(i=i):
            tiles(i, True)

        @pl.when(flags[step * BATCH + i] == 0)
        def _(i=i):
            tiles(i, False)

    @pl.when(step == RATIO // BATCH - 1)
    def _():
        dv_ref[...] = acc[pl.ds(HALF, HALF), :]
        dvp_ref[...] = acc[pl.ds(0, HALF), :].astype(BF16)


def score_grad_kernel(
    flags,
    own_ref,
    prev_ref,
    q_ref,
    k_ref,
    kp_ref,
    do_ref,
    v_ref,
    vp_ref,
    dq_ref,
    dk_ref,
    dkp_ref,
    acc,
    kt,
):
    step = pl.program_id(0)

    @pl.when(step == 0)
    def _():
        acc[...] = jnp.zeros_like(acc)
        kt[:, pl.ds(0, HALF)] = kp_ref[...].astype(F32).T.astype(BF16)
        kt[:, pl.ds(HALF, HALF)] = k_ref[...].astype(F32).T.astype(BF16)

    def tiles(i, full):
        head = pl.ds(i * HEAD, HEAD)
        for r in range(HALF // TILE):
            cols = pl.ds(r * TILE, TILE)
            q = q_ref[cols, head]
            do = do_ref[cols, head]
            sources = [(own_ref, v_ref, t * TILE, HALF) for t in range(r + 1)]
            if full:
                sources += [(prev_ref, vp_ref, t * TILE, 0) for t in range(HALF // TILE)]
            parts = []
            for place, values, at, base in sources:
                p = place[i, pl.ds(at, TILE), cols].astype(F32)
                parts.append((p, dot_nt(values[pl.ds(at, TILE), :], do), at + base))
            delta = sum(jnp.sum(p * d, axis=0, keepdims=True) for p, d, _ in parts)
            dq = jnp.zeros((HEAD, TILE), F32)
            for p, d, at in parts:
                score_grad = (p * (d - delta)).astype(BF16)
                dq = dq + dot_nn(kt[:, pl.ds(at, TILE)], score_grad)
                acc[pl.ds(at, TILE), :] += dot_nn(score_grad, q)
            dq_ref[cols, head] = (dq * SCALE).T.astype(BF16)

    for i in range(BATCH):

        @pl.when(flags[step * BATCH + i] > 0)
        def _(i=i):
            tiles(i, True)

        @pl.when(flags[step * BATCH + i] == 0)
        def _(i=i):
            tiles(i, False)

    @pl.when(step == RATIO // BATCH - 1)
    def _():
        dk_ref[...] = (acc[pl.ds(HALF, HALF), :] * SCALE).astype(BF16)
        dkp_ref[...] = (acc[pl.ds(0, HALF), :] * SCALE).astype(BF16)


def features_kernel(x_ref, out_ref):
    for j in range(UNITS):
        for s in range(2):
            out_ref[j, :, pl.ds(s * SHARD, SHARD)] = x_ref[s, 0, :, pl.ds(j * SHARD, SHARD)]


def pack_kernel(q_ref, do_ref, out_ref):
    wide = RATIO * HEAD
    for g in range(KV):
        heads = pl.ds(g * wide, wide)
        out_ref[g, :, pl.ds(0, wide)] = q_ref[0, 0, :, heads]
        out_ref[g, :, pl.ds(wide, wide)] = do_ref[0, 0, :, heads]


def pack_keys_kernel(packed_ref, k_ref, kb_ref, out_ref):
    del packed_ref
    for s in range(2):
        for g in range(KV):
            heads = pl.ds(g * HEAD, HEAD)
            out_ref[s * KV + g, :, pl.ds(0, HEAD)] = k_ref[s, 0, :, heads]
            out_ref[s * KV + g, :, pl.ds(HEAD, HEAD)] = kb_ref[s, 0, :, heads]


def unpack_kernel(in_ref, dq_ref, dk_ref):
    wide = RATIO * HEAD
    for g in range(KV):
        dq_ref[0, 0, :, pl.ds(g * wide, wide)] = in_ref[g, :, pl.ds(0, wide)]
        dk_ref[0, 0, :, pl.ds(g * HEAD, HEAD)] = in_ref[g, :, pl.ds(wide, HEAD)]


def split_float(x):
    high = x.astype(BF16)
    return high, (x - high.astype(F32)).astype(BF16)


def values_kernel(odd, x_ref, mine_ref, other_ref, down_ref, up_ref, out_ref):
    half = SHARD // 2
    high, rest = split_float(ADAPTER_SCALE * dot_nn(x_ref[...], down_ref[...]))
    values = dot_nn(high, up_ref[...]) + dot_nn(rest, up_ref[...])
    for part, first in ((mine_ref, odd[0]), (other_ref, 1 - odd[0])):
        columns = pl.ds(pl.multiple_of(first * half, half), half)
        values = values + dot_nn(x_ref[:, columns], part[...])
    values = values.astype(BF16)
    for g in range(KV):
        for c in range(UNITS):
            out_ref[g, :, pl.ds((1 + c) * HEAD, HEAD)] = values[
                c * ROWS : (c + 1) * ROWS, g * HEAD : (g + 1) * HEAD
            ]


def merge_kernel(parts_ref, own_ref, next_ref, out_ref):
    del parts_ref
    for c in range(UNITS):
        rows = pl.ds(c * ROWS, ROWS)
        out_ref[c] = (own_ref[rows, :] + next_ref[rows, :].astype(F32)).astype(BF16)


def values_sum_kernel(parts_ref, out_ref):
    for c in range(UNITS):
        total = jnp.zeros((ROWS, HEAD), F32)
        for j in range(UNITS):
            total = total + parts_ref[j, :, pl.ds((1 + c) * HEAD, HEAD)].astype(F32)
        out_ref[pl.ds(c * ROWS, ROWS), :] = total.astype(BF16)


def adapter_kernel(dv_ref, x_ref, low_ref, up_ref, out_ref):
    width = x_ref.shape[1]
    part = x_ref.shape[0] // 2
    down = jnp.zeros((RANK, width), F32)
    for s in range(2):
        pulled = jnp.zeros((RANK, part), F32)
        for g in range(KV):
            pulled = pulled + dot_nt(up_ref[:, pl.ds(g * HEAD, HEAD)], dv_ref[s * KV + g])
        down = down + dot_nn(pulled.astype(BF16), x_ref[pl.ds(s * part, part), :])
    pieces = [down[:, c * HEAD : (c + 1) * HEAD] for c in range(width // HEAD)]
    lows = [split_float(low_ref[s]) for s in range(2)]
    for g in range(KV):
        up = jnp.zeros((RANK, HEAD), F32)
        for s in range(2):
            for low in lows[s]:
                up = up + dot_nn(low, dv_ref[s * KV + g])
        pieces.append(up)
    for c, piece in enumerate(pieces):
        out_ref[pl.ds(c * RANK, RANK), :] = piece
    used = len(pieces) * RANK
    out_ref[pl.ds(used, out_ref.shape[0] - used), :] = jnp.zeros(
        (out_ref.shape[0] - used, HEAD), F32
    )


def call(kernel, flops, nbytes, **keywords):
    return pl.pallas_call(
        kernel,
        compiler_params=pltpu.CompilerParams(vmem_limit_bytes=VMEM),
        cost_estimate=pl.CostEstimate(flops=flops, bytes_accessed=nbytes, transcendentals=0),
        **keywords,
    )


def body(x, queries, keys, frozen, down_weight, up_weight, grads, mask):
    seq_devices = lax.axis_size("seq")
    weight_devices = lax.axis_size("wt")
    devices = seq_devices * weight_devices
    sequences, _, rows, width = x.shape
    tokens = sequences * rows
    y_planes = PLANES
    both = ("seq", "wt")
    groups = [[UNITS * y + j for j in range(UNITS)] for y in range(y_planes)]
    smem = pl.BlockSpec(memory_space=pltpu.SMEM)

    def flat(y, j, w):
        return (y * UNITS + j) * weight_devices + w

    everywhere = [
        (y, j, w) for y in range(y_planes) for j in range(UNITS) for w in range(weight_devices)
    ]
    from_before = [
        (
            flat(y, j, w),
            flat(y + 1, j, w) if y + 1 < y_planes else flat(0, j, (w + 1) % weight_devices),
        )
        for y, j, w in everywhere
    ]
    to_before = [(b, a) for a, b in from_before]
    turned = [(flat(y, w, j), flat(y, j, w)) for y, j, w in everywhere]
    next_plane = [(i, i ^ UNITS) for i in range(seq_devices)]
    same_unit = [
        [flat(y, j, w) for y in range(PLANES) for w in range(weight_devices)] for j in range(UNITS)
    ]

    def swap(block):
        return lax.all_to_all(
            block, "seq", split_axis=0, concat_axis=0, axis_index_groups=groups, tiled=True
        )

    place = lax.axis_index("seq")
    parity = (place // UNITS) % 2
    kv_head = place % KV
    my_mask = lax.dynamic_slice_in_dim(mask, kv_head * RATIO, RATIO, 0)
    flags = jnp.where(parity == 1, 1 - my_mask, my_mask).astype(jnp.int32)

    x_rows = x.reshape(tokens, width)
    wide = RATIO * HEAD

    low = jnp.dot(x_rows, down_weight, preferred_element_type=F32)
    low_parts = jnp.transpose(low.reshape(sequences, rows, RANK), (0, 2, 1))

    def whole(*shape):
        return pl.BlockSpec(shape, lambda i: (0,) * len(shape))

    features = call(
        features_kernel,
        0,
        2 << 20,
        grid=(1,),
        in_specs=[whole(sequences, 1, rows, width)],
        out_specs=whole(UNITS, rows, sequences * SHARD),
        out_shape=pltpu.HBM((UNITS, rows, sequences * SHARD), BF16),
        name="features",
    )(pltpu.with_memory_space_constraint(x, pltpu.HBM))
    x_parts = swap(features).reshape(HALF, sequences * SHARD)
    piece = lax.dynamic_slice_in_dim(frozen, parity * (SHARD // 2), SHARD // 2, 0)
    piece = lax.ppermute(piece, both, turned)
    keys_before = lax.ppermute(keys, both, from_before)
    token_wide = pl.BlockSpec((1, 1, rows, KV * wide), lambda i: (i, 0, 0, 0))
    token_head = pl.BlockSpec((1, 1, rows, KV * HEAD), lambda i: (i, 0, 0, 0))
    packed = 2 * (wide + HEAD)
    packed_shape = pltpu.HBM((UNITS, rows, packed), BF16)
    outgoing = call(
        pack_kernel,
        0,
        4 << 20,
        grid=(sequences,),
        in_specs=[token_wide, token_wide],
        out_specs=pl.BlockSpec((KV, rows, 2 * wide), lambda i: (i, 0, 0)),
        out_shape=packed_shape,
        name="pack",
    )(
        pltpu.with_memory_space_constraint(queries, pltpu.HBM),
        pltpu.with_memory_space_constraint(grads, pltpu.HBM),
    )
    all_keys = whole(sequences, 1, rows, KV * HEAD)
    outgoing = call(
        pack_keys_kernel,
        0,
        1 << 19,
        grid=(1,),
        in_specs=[pl.BlockSpec(memory_space=pl.ANY), all_keys, all_keys],
        out_specs=pl.BlockSpec((UNITS, rows, 2 * HEAD), lambda i: (0, 0, RATIO)),
        out_shape=packed_shape,
        input_output_aliases={0: 0},
        name="pack_keys",
    )(outgoing, keys, keys_before)
    outgoing, piece, x_parts = lax.optimization_barrier((outgoing, piece, x_parts))
    first = swap(outgoing).reshape(HALF, packed)
    piece_other = lax.ppermute(piece, "seq", next_plane)
    down_part = lax.dynamic_slice_in_dim(down_weight, place % UNITS * SHARD, SHARD, 0)
    first, piece_other, down_part, low_parts = lax.optimization_barrier(
        (first, piece_other, down_part, low_parts)
    )

    steps = RATIO // BATCH
    head_block = pl.BlockSpec((HALF, BATCH * HEAD), lambda h: (0, h))
    grad_block = pl.BlockSpec((HALF, BATCH * HEAD), lambda h: (0, steps + h))
    key_block = pl.BlockSpec((HALF, HEAD), lambda h: (0, 2 * RATIO))
    key_prev_block = pl.BlockSpec((HALF, HEAD), lambda h: (0, 2 * RATIO + 1))
    prev_block = pl.BlockSpec((HALF, HEAD), lambda h: (0, 0))
    p_block = pl.BlockSpec((BATCH, HALF, HALF), lambda h: (h, 0, 0))
    p_shape = pltpu.HBM((RATIO, HALF, HALF), BF16)

    product = 2 * RATIO * HALF * HALF * 3 // 2 * HEAD

    x_block = whole(tokens, width)
    prev_one = whole(HALF, HEAD)
    weights_own, weights_prev, dv_own, dv_prev = call(
        weights_kernel,
        2 * product,
        10 << 20,
        grid=(steps,),
        in_specs=[smem, head_block, key_block, key_prev_block, grad_block],
        out_specs=(p_block, p_block, prev_block, prev_block),
        out_shape=(p_shape, p_shape, pltpu.HBM((HALF, HEAD), F32), pltpu.HBM((HALF, HEAD), BF16)),
        scratch_shapes=[pltpu.VMEM((2 * HALF, HEAD), F32)],
        name="weights",
    )(flags, first, first, first, first)
    weights_own = pltpu.with_memory_space_constraint(weights_own, pltpu.HBM)
    weights_prev = pltpu.with_memory_space_constraint(weights_prev, pltpu.HBM)

    dv_next = lax.ppermute(dv_prev, both, to_before)
    parts_shape = pltpu.HBM((UNITS, rows, (1 + UNITS) * HEAD), BF16)
    parts = call(
        values_kernel,
        2 * tokens * width * KV * HEAD,
        4 << 20,
        grid=(sequences,),
        in_specs=[
            smem,
            pl.BlockSpec((HALF, SHARD), lambda i: (0, i)),
            whole(SHARD // 2, KV * HEAD),
            whole(SHARD // 2, KV * HEAD),
            whole(SHARD, RANK),
            whole(RANK, KV * HEAD),
        ],
        out_specs=pl.BlockSpec((KV, rows, (1 + UNITS) * HEAD), lambda i: (i, 0, 0)),
        out_shape=parts_shape,
        name="values",
    )(parity.astype(jnp.int32).reshape(1), x_parts, piece, piece_other, down_part, up_weight)
    merged = call(
        merge_kernel,
        0,
        1 << 19,
        grid=(1,),
        in_specs=[pl.BlockSpec(memory_space=pl.ANY), prev_one, prev_one],
        out_specs=whole(UNITS, rows, HEAD),
        out_shape=parts_shape,
        input_output_aliases={0: 0},
        name="merge",
    )(parts, dv_own, dv_next)
    third = swap(merged)
    v_unit = call(
        values_sum_kernel,
        1 << 20,
        1 << 20,
        grid=(1,),
        in_specs=[whole(UNITS, rows, (1 + UNITS) * HEAD)],
        out_specs=whole(HALF, HEAD),
        out_shape=pltpu.HBM((HALF, HEAD), BF16),
        name="values_sum",
    )(third)
    v_prev = lax.ppermute(v_unit, both, from_before)

    pieces = width // HEAD + KV
    peers = PLANES * weight_devices
    share = RANK
    sums = call(
        adapter_kernel,
        4 * tokens * width * RANK,
        3 << 20,
        grid=(1,),
        in_specs=[
            whole(UNITS, rows, HEAD),
            x_block,
            whole(sequences, RANK, rows),
            whole(RANK, KV * HEAD),
        ],
        out_specs=whole(peers * share, HEAD),
        out_shape=pltpu.HBM((peers * share, HEAD), F32),
        name="adapter",
    )(third, x_rows, low_parts, up_weight)
    v_prev, sums = lax.optimization_barrier((v_prev, sums))

    def among_peers(block):
        return lax.all_to_all(
            block, both, split_axis=0, concat_axis=0, axis_index_groups=same_unit, tiled=True
        ).reshape(peers, share, HEAD)

    mine = jnp.sum(among_peers(sums), axis=0) * (ADAPTER_SCALE / math.sqrt(tokens * devices))
    blank = jnp.zeros((rows // 2 - share, HEAD), BF16)
    high, rest = split_float(mine)
    mine_parts = jnp.concatenate([high, blank, rest, blank], axis=0)

    dq_unit, dk_own, dk_prev = call(
        score_grad_kernel,
        3 * product,
        12 << 20,
        grid=(steps,),
        in_specs=[
            smem,
            p_block,
            p_block,
            head_block,
            key_block,
            key_prev_block,
            grad_block,
            prev_block,
            prev_block,
        ],
        out_specs=(head_block, prev_block, prev_block),
        out_shape=(
            pltpu.HBM((HALF, wide), BF16),
            pltpu.HBM((HALF, HEAD), BF16),
            pltpu.HBM((HALF, HEAD), BF16),
        ),
        scratch_shapes=[pltpu.VMEM((2 * HALF, HEAD), F32), pltpu.VMEM((HEAD, 2 * HALF), BF16)],
        name="score_grad",
    )(
        flags,
        weights_own,
        weights_prev,
        first,
        first,
        first,
        first,
        v_unit,
        v_prev,
    )
    returning = jnp.concatenate(
        [
            dq_unit.reshape(UNITS, rows, wide),
            dk_own.reshape(UNITS, rows, HEAD),
            dk_prev.reshape(UNITS, rows, HEAD),
            jnp.broadcast_to(mine_parts[None], (UNITS, rows, HEAD)),
        ],
        axis=2,
    )
    returned = swap(returning)

    sum_parts = returned[:, :, wide + 2 * HEAD :].reshape(UNITS * 2, rows // 2, HEAD)
    total = jnp.sum(sum_parts[:, :share].astype(F32), axis=0)
    spread = jnp.broadcast_to(total[None], (peers, share, HEAD)).reshape(peers * share, HEAD)
    key_prev = returned[:, :, wide + HEAD : wide + 2 * HEAD]
    key_prev, spread = lax.optimization_barrier((key_prev, spread))
    totals = among_peers(spread).reshape(peers * share, HEAD)[: pieces * RANK]
    totals = totals.reshape(pieces, RANK, HEAD)

    key_shape = jax.ShapeDtypeStruct((sequences, 1, rows, KV * HEAD), BF16)
    query_grad, key_own = call(
        unpack_kernel,
        0,
        4 << 20,
        grid=(sequences,),
        in_specs=[pl.BlockSpec((KV, rows, wide + HEAD), lambda i: (i, 0, 0))],
        out_specs=(token_wide, token_head),
        out_shape=(
            jax.ShapeDtypeStruct((sequences, 1, rows, KV * wide), BF16),
            jax.ShapeDtypeStruct((sequences, 1, rows, KV * HEAD), BF16),
        ),
        name="unpack",
    )(returned)
    key_next = lax.ppermute(key_prev, both, to_before)
    key_next = jnp.transpose(key_next.reshape(sequences, KV, rows, HEAD), (0, 2, 1, 3))
    key_next = key_next.reshape(sequences, 1, rows, KV * HEAD)
    key_grad = (key_own.astype(F32) + key_next.astype(F32)).astype(BF16)
    down_grad = jnp.transpose(totals[: width // HEAD], (0, 2, 1)).reshape(width, RANK)
    up_grad = jnp.transpose(totals[width // HEAD :], (1, 0, 2)).reshape(RANK, KV * HEAD)
    return (query_grad, key_grad, down_grad, up_grad)


def solution(mesh):
    tokens = P(None, "wt", "seq", None)
    return jax.shard_map(
        body,
        mesh=mesh,
        in_specs=(tokens, tokens, tokens, P("wt", None), P(), P(), tokens, P()),
        out_specs=(tokens, tokens, P(), P()),
        check_vma=False,
    )
```

time: 209 us -> 201 us (0.962)
  waiting for transfers between devices: 39.8 us -> 56.7 us
  local copies, waits for them, and re-layouts: 14.8 us -> 4.22 us
  blocking collectives: 46.4 us -> 40.6 us
  starting transfers between devices: 64 us -> 58.2 us
  Pallas kernels: 38.2 us -> 36 us
    all_to_all x2, starting transfers between devices: 24.9 us -> 17.1 us  [among_peers(): lax.all_to_all(block, both, split_axis=0, concat_axis=0, axis_index_group...]
    all_to_all x2, waiting for transfers between devices: 10.7 us -> 16.7 us  [among_peers(): lax.all_to_all(block, both, split_axis=0, concat_axis=0, axis_index_group...]
    unnamed x22 -> x18, local copies, waits for them, and re-layouts: 6.86 us -> 1.01 us
    all_to_all x2, blocking collectives: 46.4 us -> 40.6 us  [swap(): lax.all_to_all(block, 'seq', split_axis=0, concat_axis=0, axis_index_grou...]
    ppermute x1, waiting for transfers between devices: 0.01 us -> 4.25 us  [body(): piece = lax.ppermute(piece, both, turned)]
    ppermute x1, waiting for transfers between devices: 1.45 us -> 5.13 us  [body(): piece_other = lax.ppermute(piece, 'seq', next_plane)]
    ppermute x1, waiting for transfers between devices: 3.87 us -> 7.3 us  [body(): v_prev = lax.ppermute(v_unit, both, from_before)]
    all_to_all x2, starting transfers between devices: 18.7 us -> 21.7 us  [swap(): lax.all_to_all(block, 'seq', split_axis=0, concat_axis=0, axis_index_grou...]
  transfers between devices with their start and end apart: 10 -> 10, of which waited for: 5 -> 8; matrix products, arithmetic and copies ran while one was open for 5% -> 2% of each run, Pallas kernels for 16% -> 11%
where the time goes in v4:
time: 201 us
  starting transfers between devices  58.2 us (29%)
  waiting for transfers between devices  56.7 us (28%)
  blocking collectives  40.6 us (20%)
  Pallas kernels  36 us (18%)
  local copies, waits for them, and re-layouts  4.22 us (2%)
  other arithmetic  2.4 us (1%)
    all_to_all x2, blocking collectives, swap(): lax.all_to_all(block, 'seq', split_axis=0, concat_axis=0, axis_index_grou...  40.6 us
    all_to_all x2, starting transfers between devices, swap(): lax.all_to_all(block, 'seq', split_axis=0, concat_axis=0, axis_index_grou...  21.7 us
    all_to_all x2, waiting for transfers between devices, swap(): lax.all_to_all(block, 'seq', split_axis=0, concat_axis=0, axis_index_grou...  19.3 us
    all_to_all x2, starting transfers between devices, among_peers(): lax.all_to_all(block, both, split_axis=0, concat_axis=0, axis_index_group...  17.1 us
    all_to_all x2, waiting for transfers between devices, among_peers(): lax.all_to_all(block, both, split_axis=0, concat_axis=0, axis_index_group...  16.7 us
    pallas_call x1, Pallas kernels, body(): call(score_grad_kernel, 3 * product, 12 << 20, grid=(steps,), in_specs=[s...  12.4 us
    pallas_call x1, Pallas kernels, body(): call(weights_kernel, 2 * product, 10 << 20, grid=(steps,), in_specs=[smem...  10.5 us
    ppermute x1, waiting for transfers between devices, body(): v_prev = lax.ppermute(v_unit, both, from_before)  7.3 us
  transfers between devices with their start and end apart: 10, of which 8 were waited for; matrix products, arithmetic and copies ran while one was open for 2% of the time, Pallas kernels for 11%

profile of v4, /device:TPU:1, one launch (start us, length us, event | category | flops | bytes accessed | tf_op | source)
XLA Modules:
  0.0 200.7 jit_solution(1637724550982743097)
XLA Ops:
  0.7 2.3 %features.1 = bf16[8,64,1024]{2,1,0:T(8,128)(2,1)} custom-call(bf16[2,1,64,4096]{3,2,1,0:T(8,128)(2,1)} %x_ref.1), custom_call_target="tpu_custom_call" | custom-call | bytes 2097152 | tf_op jit(solution)/shard_map/features/pallas_call | solution.py:307
  3.0 6.7 %all-to-all-start = ((bf16[8,64,1024]{2,1,0:T(8,128)(2,1)}), bf16[8,64,1024]{2,1,0:T(8,128)(2,1)S(1)}, u32[]{:S(2)}, u32[]{:S(2)}) async-start(bf16[8,64,1024]{2,1,0:T(8,128)(2,1)} %features.1), calls=%async_computation | async-start | bytes 2097152 | tf_op jit(solution)/shard_map/all_to_all | solution.py:288
  9.7 7.2 %collective-permute-start.1 = (bf16[256,512]{1,0:T(8,128)(2,1)S(1)}, bf16[256,512]{1,0:T(8,128)(2,1)S(1)}, u32[]{:S(2)}, u32[]{:S(2)}) collective-permute-start(bf16[256,512]{1,0:T(8,128)(2,1)S(1)} %constant_dynamic-slice_fusion.1), channel_id=1, source_target_pairs={{0,0},{8,1},{16,2},{24,3},{32,4},{40,5},{48,6},{56,7},{1,8},{9,9},... | collective-permute-start | bytes 786440 | tf_op jit(solution)/shard_map/ppermute | solution.py:319
  16.9 1.9 collective-permute-start
  18.8 2.7 %pack.1.packed_ref = bf16[8,64,2304]{2,1,0:T(8,128)(2,1)} custom-call(bf16[2,1,64,4096]{3,2,1,0:T(8,128)(2,1)} %q_ref.1, bf16[2,1,64,4096]{3,2,1,0:T(8,128)(2,1)} %do_ref.1), custom_call_target="tpu_custom_call" | custom-call | bytes 4194304 | tf_op jit(solution)/shard_map/pack/pallas_call | solution.py:325
  21.5 3.2 %collective-permute-done.kb_ref = bf16[2,1,64,512]{3,2,1,0:T(8,128)(2,1)S(1)} collective-permute-done((bf16[2,1,64,512]{3,2,1,0:T(8,128)(2,1)S(1)}, bf16[2,1,64,512]{3,2,1,0:T(8,128)(2,1)S(1)}, u32[]{:S(2)}, u32[]{:S(2)}) %collective-permute-start) | collective-permute-done | bytes 131104 | tf_op jit(solution)/shard_map/ppermute | solution.py:320
  24.7 0.8 pack_keys.1
  25.5 4.3 %collective-permute-done.1.mine_ref = bf16[256,512]{1,0:T(8,128)(2,1)S(1)} collective-permute-done((bf16[256,512]{1,0:T(8,128)(2,1)S(1)}, bf16[256,512]{1,0:T(8,128)(2,1)S(1)}, u32[]{:S(2)}, u32[]{:S(2)}) %collective-permute-start.1) | collective-permute-done | bytes 262176 | tf_op jit(solution)/shard_map/ppermute | solution.py:319
  29.7 1.0 copy-done.2
  30.7 15.1 %all-to-all-start.1 = ((bf16[8,64,2304]{2,1,0:T(8,128)(2,1)}), bf16[8,64,2304]{2,1,0:T(8,128)(2,1)S(1)}, u32[]{:S(2)}, u32[]{:S(2)}) async-start(bf16[8,64,2304]{2,1,0:T(8,128)(2,1)} %pack_keys.1), calls=%async_computation.1 | async-start | bytes 4718592 | tf_op jit(solution)/shard_map/all_to_all | solution.py:288
  46.5 1.9 collective-permute-start.2
  48.6 1.7 convolution_bitcast_fusion.low_ref
  50.4 5.1 %collective-permute-done.2.other_ref = bf16[256,512]{1,0:T(8,128)(2,1)S(1)} collective-permute-done((bf16[256,512]{1,0:T(8,128)(2,1)S(1)}, bf16[256,512]{1,0:T(8,128)(2,1)S(1)}, u32[]{:S(2)}, u32[]{:S(2)}) %collective-permute-start.2) | collective-permute-done | bytes 262176 | tf_op jit(solution)/shard_map/ppermute | solution.py:352
  55.5 19.3 %all-to-all-done.1 = bf16[8,64,2304]{2,1,0:T(8,128)(2,1)S(1)} async-done(((bf16[8,64,2304]{2,1,0:T(8,128)(2,1)}), bf16[8,64,2304]{2,1,0:T(8,128)(2,1)S(1)}, u32[]{:S(2)}, u32[]{:S(2)}) %all-to-all-start.1) | async-done | bytes 2359328 | tf_op jit(solution)/shard_map/all_to_all | solution.py:288
  74.8 10.5 %weights.1 = (bf16[8,512,512]{2,1,0:T(8,128)(2,1)}, bf16[8,512,512]{2,1,0:T(8,128)(2,1)}, f32[512,128]{1,0:T(8,128)}, bf16[512,128]{1,0:T(8,128)(2,1)}) custom-call(s32[8]{0:T(128)S(1)} %broadcast_select_fusion.flags, bf16[512,2304]{1,0:T(8,128)(2,1)S(1)} %bitcast.32, bf16[512,2304]{1,0:T(8,128)(2,1)S(1)} %bitcast.33, bf16[512,2304]{1,0:T(8,128)(2,1)S(1)} %bitcast.34, ...), custom_call_target="tpu_custom_call" | custom-call | flops 1610612736 | bytes 10485760 | tf_op jit(solution)/shard_map/weights/pallas_call | solution.py:371
  85.3 2.1 %collective-permute-start.3 = (bf16[512,128]{1,0:T(8,128)(2,1)}, bf16[512,128]{1,0:T(8,128)(2,1)S(1)}, u32[]{:S(2)}, u32[]{:S(2)}) collective-permute-start(bf16[512,128]{1,0:T(8,128)(2,1)} %get-tuple-element.33), channel_id=1, source_target_pairs={{64,0},{65,1},{66,2},{67,3},{68,4},{69,5},{70,6},{71,7},{72,8},{73... | collective-permute-start | bytes 393224 | tf_op jit(solution)/shard_map/ppermute | solution.py:385
  87.4 3.4 %values.1.parts_ref = bf16[8,64,1152]{2,1,0:T(8,128)(2,1)} custom-call(s32[1]{0:T(128)} %bitcast.5.odd, bf16[512,1024]{1,0:T(8,128)(2,1)S(1)} %bitcast.41, bf16[256,512]{1,0:T(8,128)(2,1)S(1)} %collective-permute-done.1.mine_ref, bf16[256,512]{1,0:T(8,128)(2,1)S(1)} %collective-permute-done.2.other_ref, bf16[512,8]{1,0:T(8,128)(2,1)S(1)} %copy.16.down_ref, ...), custom_call_target="tpu_custom_call" | custom-call | flops 536870912 | bytes 4194304 | tf_op jit(solution)/shard_map/values/pallas_call | solution.py:387
  90.8 0.9 collective-permute-done.3.next_ref
  92.5 18.6 %all_to_all.38.parts_ref.dv_ref = bf16[8,64,1152]{2,1,0:T(8,128)(2,1)S(1)} all-to-all(bf16[8,64,1152]{2,1,0:T(8,128)(2,1)} %merge.1), channel_id=1, replica_groups={{0,8,16,24,32,40,48,56},{64,72,80,88,96,104,112,120},{128,136,144,152,1..., dimensions={0} | all-to-all | bytes 2359296 | tf_op jit(solution)/shard_map/all_to_all | solution.py:288
  111.1 0.8 values_sum.1.v_ref
  111.9 3.0 %collective-permute-start.4 = (bf16[512,128]{1,0:T(8,128)(2,1)}, bf16[512,128]{1,0:T(8,128)(2,1)S(1)}, u32[]{:S(2)}, u32[]{:S(2)}) collective-permute-start(bf16[512,128]{1,0:T(8,128)(2,1)} %values_sum.1.v_ref), channel_id=1, source_target_pairs={{0,64},{1,65},{2,66},{3,67},{4,68},{5,69},{6,70},{7,71},{8,72},{9,... | collective-permute-start | bytes 393224 | tf_op jit(solution)/shard_map/ppermute | solution.py:426
  114.9 1.2 adapter.1
  116.1 7.3 %collective-permute-done.4.vp_ref = bf16[512,128]{1,0:T(8,128)(2,1)S(1)} collective-permute-done((bf16[512,128]{1,0:T(8,128)(2,1)}, bf16[512,128]{1,0:T(8,128)(2,1)S(1)}, u32[]{:S(2)}, u32[]{:S(2)}) %collective-permute-start.4) | collective-permute-done | bytes 131104 | tf_op jit(solution)/shard_map/ppermute | solution.py:426
  123.4 7.0 %all-to-all-start.3 = ((f32[64,8,128]{2,1,0:T(8,128)}), f32[64,8,128]{2,1,0:T(8,128)S(1)}, u32[]{:S(2)}, u32[]{:S(2)}) async-start(f32[64,8,128]{2,1,0:T(8,128)} %bitcast.42), calls=%async_computation.3 | async-start | bytes 524288 | tf_op jit(solution)/shard_map/all_to_all | solution.py:449
  130.4 12.4 %score_grad.1 = (bf16[512,1024]{1,0:T(8,128)(2,1)}, bf16[512,128]{1,0:T(8,128)(2,1)}, bf16[512,128]{1,0:T(8,128)(2,1)}) custom-call(s32[8]{0:T(128)S(1)} %broadcast_select_fusion.flags, bf16[8,512,512]{2,1,0:T(8,128)(2,1)} %get-tuple-element.27.own_ref, bf16[8,512,512]{2,1,0:T(8,128)(2,1)} %get-tuple-element.28.prev_ref, bf16[512,2304]{1,0:T(8,128)(2,1)S(1)} %bitcast.36, ...), custom_call_target="tpu_custom_call" | custom-call | flops 2415919104 | bytes 12582912 | tf_op jit(solution)/shard_map/score_grad/pallas_call | solution.py:458
  142.9 3.2 %all-to-all-done.3 = f32[64,8,128]{2,1,0:T(8,128)S(1)} async-done(((f32[64,8,128]{2,1,0:T(8,128)}), f32[64,8,128]{2,1,0:T(8,128)S(1)}, u32[]{:S(2)}, u32[]{:S(2)}) %all-to-all-start.3) | async-done | bytes 262176 | tf_op jit(solution)/shard_map/all_to_all | solution.py:449
  146.2 1.5 pad_maximum_fusion
  147.7 22.0 %all_to_all.39.in_ref = bf16[8,64,1408]{2,1,0:T(8,128)(2,1)S(1)} all-to-all(bf16[8,64,1408]{2,1,0:T(8,128)(2,1)S(1)} %pad_maximum_fusion), channel_id=1, replica_groups={{0,8,16,24,32,40,48,56},{64,72,80,88,96,104,112,120},{128,136,144,152,1..., dimensions={0} | all-to-all | bytes 2883584 | tf_op jit(solution)/shard_map/all_to_all | solution.py:288
  170.5 3.2 %collective-permute-start.5 = (bf16[8,64,128]{2,1,0:T(8,128)(2,1)S(1)}, bf16[8,64,128]{2,1,0:T(8,128)(2,1)S(1)}, u32[]{:S(2)}, u32[]{:S(2)}) collective-permute-start(bf16[8,64,128]{2,1,0:T(8,128)(2,1)S(1)} %get-tuple-element.42), channel_id=1, source_target_pairs={{64,0},{65,1},{66,2},{67,3},{68,4},{69,5},{70,6},{71,7},{72,8},{73... | collective-permute-start | bytes 393224 | tf_op jit(solution)/shard_map/ppermute | solution.py:526
  173.8 10.1 %all-to-all-start.5 = ((f32[64,8,128]{2,1,0:T(8,128)}), f32[64,8,128]{2,1,0:T(8,128)S(1)}, u32[]{:S(2)}, u32[]{:S(2)}) async-start(f32[64,8,128]{2,1,0:T(8,128)} %bitcast.15), calls=%async_computation.5 | async-start | bytes 524288 | tf_op jit(solution)/shard_map/all_to_all | solution.py:449
  183.9 1.1 unpack.1
  186.0 13.4 %all-to-all-done.5 = f32[64,8,128]{2,1,0:T(8,128)S(1)} async-done(((f32[64,8,128]{2,1,0:T(8,128)}), f32[64,8,128]{2,1,0:T(8,128)S(1)}, u32[]{:S(2)}, u32[]{:S(2)}) %all-to-all-start.5) | async-done | bytes 262176 | tf_op jit(solution)/shard_map/all_to_all | solution.py:449
  (38 shorter events, 4.8 us)
Async XLA Ops:
  0.6 9.0 %copy-start = (bf16[512,512]{1,0:T(8,128)(2,1)S(1)}, bf16[512,512]{1,0:T(8,128)(2,1)}, u32[]{:S(2)}) copy-start(bf16[512,512]{1,0:T(8,128)(2,1)} %param.11) | copy-start | bytes 1572868
  0.6 16.3 %copy-start.6 = (bf16[2,1,64,512]{3,2,1,0:T(8,128)(2,1)S(1)}, bf16[2,1,64,512]{3,2,1,0:T(8,128)(2,1)}, u32[]{:S(2)}) copy-start(bf16[2,1,64,512]{3,2,1,0:T(8,128)(2,1)} %k_ref.1) | copy-start | bytes 393220
  3.0 26.8 %all-to-all-start = ((bf16[8,64,1024]{2,1,0:T(8,128)(2,1)}), bf16[8,64,1024]{2,1,0:T(8,128)(2,1)S(1)}, u32[]{:S(2)}, u32[]{:S(2)}) async-start(bf16[8,64,1024]{2,1,0:T(8,128)(2,1)} %features.1), calls=%async_computation | async-start | bytes 2097152 | tf_op jit(solution)/shard_map/all_to_all | solution.py:288
  9.7 20.1 %collective-permute-start.1 = (bf16[256,512]{1,0:T(8,128)(2,1)S(1)}, bf16[256,512]{1,0:T(8,128)(2,1)S(1)}, u32[]{:S(2)}, u32[]{:S(2)}) collective-permute-start(bf16[256,512]{1,0:T(8,128)(2,1)S(1)} %constant_dynamic-slice_fusion.1), channel_id=1, source_target_pairs={{0,0},{8,1},{16,2},{24,3},{32,4},{40,5},{48,6},{56,7},{1,8},{9,9},... | collective-permute-start | bytes 786440 | tf_op jit(solution)/shard_map/ppermute | solution.py:319
  16.9 7.8 %collective-permute-start = (bf16[2,1,64,512]{3,2,1,0:T(8,128)(2,1)S(1)}, bf16[2,1,64,512]{3,2,1,0:T(8,128)(2,1)S(1)}, u32[]{:S(2)}, u32[]{:S(2)}) collective-permute-start(bf16[2,1,64,512]{3,2,1,0:T(8,128)(2,1)S(1)} %copy-done.6), channel_id=1, source_target_pairs={{0,64},{1,65},{2,66},{3,67},{4,68},{5,69},{6,70},{7,71},{8,72},{9,... | collective-permute-start | bytes 393224 | tf_op jit(solution)/shard_map/ppermute | solution.py:320
  29.7 1.0 copy-start.2
  30.7 17.7 %copy-start.8 = (s32[32]{0:T(128)S(1)}, s32[32]{0:T(128)}, u32[]{:S(2)}) copy-start(s32[32]{0:T(128)} %param.15) | copy-start | bytes 388
  30.7 44.1 %all-to-all-start.1 = ((bf16[8,64,2304]{2,1,0:T(8,128)(2,1)}), bf16[8,64,2304]{2,1,0:T(8,128)(2,1)S(1)}, u32[]{:S(2)}, u32[]{:S(2)}) async-start(bf16[8,64,2304]{2,1,0:T(8,128)(2,1)} %pack_keys.1), calls=%async_computation.1 | async-start | bytes 4718592 | tf_op jit(solution)/shard_map/all_to_all | solution.py:288
  46.5 9.0 %collective-permute-start.2 = (bf16[256,512]{1,0:T(8,128)(2,1)S(1)}, bf16[256,512]{1,0:T(8,128)(2,1)S(1)}, u32[]{:S(2)}, u32[]{:S(2)}) collective-permute-start(bf16[256,512]{1,0:T(8,128)(2,1)S(1)} %collective-permute-done.1.mine_ref), channel_id=1, source_target_pairs={{0,64},{8,72},{16,80},{24,88},{32,96},{40,104},{48,112},{56,120},{... | collective-permute-start | bytes 786440 | tf_op jit(solution)/shard_map/ppermute | solution.py:352
  74.8 12.6 %copy-start.3 = (bf16[8,64,1024]{2,1,0:T(8,128)(2,1)S(1)}, bf16[8,64,1024]{2,1,0:T(8,128)(2,1)}, u32[]{:S(2)}) copy-start(bf16[8,64,1024]{2,1,0:T(8,128)(2,1)} %copy-done.2) | copy-start | bytes 3145732
  74.8 12.6 %copy-start.7 = (bf16[8,512]{1,0:T(8,128)(2,1)S(1)}, bf16[8,512]{1,0:T(8,128)(2,1)}, u32[]{:S(2)}) copy-start(bf16[8,512]{1,0:T(8,128)(2,1)} %up_ref.3) | copy-start | bytes 24580
  85.3 6.5 %copy-start.5 = (f32[512,128]{1,0:T(8,128)S(1)}, f32[512,128]{1,0:T(8,128)}, u32[]{:S(2)}) copy-start(f32[512,128]{1,0:T(8,128)} %get-tuple-element.32.own_ref) | copy-start | bytes 786436
  85.3 6.4 %collective-permute-start.3 = (bf16[512,128]{1,0:T(8,128)(2,1)}, bf16[512,128]{1,0:T(8,128)(2,1)S(1)}, u32[]{:S(2)}, u32[]{:S(2)}) collective-permute-start(bf16[512,128]{1,0:T(8,128)(2,1)} %get-tuple-element.33), channel_id=1, source_target_pairs={{64,0},{65,1},{66,2},{67,3},{68,4},{69,5},{70,6},{71,7},{72,8},{73... | collective-permute-start | bytes 393224 | tf_op jit(solution)/shard_map/ppermute | solution.py:385
  92.5 22.5 %copy-start.1 = (bf16[2,1,64,4096]{3,2,1,0:T(8,128)(2,1)S(1)}, bf16[2,1,64,4096]{3,2,1,0:T(8,128)(2,1)}, u32[]{:S(2)}) copy-start(bf16[2,1,64,4096]{3,2,1,0:T(8,128)(2,1)} %x_ref.1) | copy-start | bytes 3145732
  111.9 18.5 %copy-start.4 = (bf16[512,128]{1,0:T(8,128)(2,1)S(1)}, bf16[512,128]{1,0:T(8,128)(2,1)}, u32[]{:S(2)}) copy-start(bf16[512,128]{1,0:T(8,128)(2,1)} %values_sum.1.v_ref) | copy-start | bytes 393220
  111.9 11.5 %collective-permute-start.4 = (bf16[512,128]{1,0:T(8,128)(2,1)}, bf16[512,128]{1,0:T(8,128)(2,1)S(1)}, u32[]{:S(2)}, u32[]{:S(2)}) collective-permute-start(bf16[512,128]{1,0:T(8,128)(2,1)} %values_sum.1.v_ref), channel_id=1, source_target_pairs={{0,64},{1,65},{2,66},{3,67},{4,68},{5,69},{6,70},{7,71},{8,72},{9,... | collective-permute-start | bytes 393224 | tf_op jit(solution)/shard_map/ppermute | solution.py:426
  123.4 22.6 %all-to-all-start.3 = ((f32[64,8,128]{2,1,0:T(8,128)}), f32[64,8,128]{2,1,0:T(8,128)S(1)}, u32[]{:S(2)}, u32[]{:S(2)}) async-start(f32[64,8,128]{2,1,0:T(8,128)} %bitcast.42), calls=%async_computation.3 | async-start | bytes 524288 | tf_op jit(solution)/shard_map/all_to_all | solution.py:449
  170.5 14.5 %collective-permute-start.5 = (bf16[8,64,128]{2,1,0:T(8,128)(2,1)S(1)}, bf16[8,64,128]{2,1,0:T(8,128)(2,1)S(1)}, u32[]{:S(2)}, u32[]{:S(2)}) collective-permute-start(bf16[8,64,128]{2,1,0:T(8,128)(2,1)S(1)} %get-tuple-element.42), channel_id=1, source_target_pairs={{64,0},{65,1},{66,2},{67,3},{68,4},{69,5},{70,6},{71,7},{72,8},{73... | collective-permute-start | bytes 393224 | tf_op jit(solution)/shard_map/ppermute | solution.py:526
  173.8 25.7 %all-to-all-start.5 = ((f32[64,8,128]{2,1,0:T(8,128)}), f32[64,8,128]{2,1,0:T(8,128)S(1)}, u32[]{:S(2)}, u32[]{:S(2)}) async-start(f32[64,8,128]{2,1,0:T(8,128)} %bitcast.15), calls=%async_computation.5 | async-start | bytes 524288 | tf_op jit(solution)/shard_map/all_to_all | solution.py:449

commit v5 on v4

--- a/solution.py
+++ b/solution.py
@@ -154,12 +154,6 @@
         dkp_ref[...] = (acc[pl.ds(0, HALF), :] * SCALE).astype(BF16)
 
 
-def features_kernel(x_ref, out_ref):
-    for j in range(UNITS):
-        for s in range(2):
-            out_ref[j, :, pl.ds(s * SHARD, SHARD)] = x_ref[s, 0, :, pl.ds(j * SHARD, SHARD)]
-
-
 def pack_kernel(q_ref, do_ref, out_ref):
     wide = RATIO * HEAD
     for g in range(KV):
@@ -304,17 +298,6 @@
     def whole(*shape):
         return pl.BlockSpec(shape, lambda i: (0,) * len(shape))
 
-    features = call(
-        features_kernel,
-        0,
-        2 << 20,
-        grid=(1,),
-        in_specs=[whole(sequences, 1, rows, width)],
-        out_specs=whole(UNITS, rows, sequences * SHARD),
-        out_shape=pltpu.HBM((UNITS, rows, sequences * SHARD), BF16),
-        name="features",
-    )(pltpu.with_memory_space_constraint(x, pltpu.HBM))
-    x_parts = swap(features).reshape(HALF, sequences * SHARD)
     piece = lax.dynamic_slice_in_dim(frozen, parity * (SHARD // 2), SHARD // 2, 0)
     piece = lax.ppermute(piece, both, turned)
     keys_before = lax.ppermute(keys, both, from_before)
@@ -347,13 +330,17 @@
         input_output_aliases={0: 0},
         name="pack_keys",
     )(outgoing, keys, keys_before)
-    outgoing, piece, x_parts = lax.optimization_barrier((outgoing, piece, x_parts))
+    outgoing, piece = lax.optimization_barrier((outgoing, piece))
     first = swap(outgoing).reshape(HALF, packed)
     piece_other = lax.ppermute(piece, "seq", next_plane)
     down_part = lax.dynamic_slice_in_dim(down_weight, place % UNITS * SHARD, SHARD, 0)
     first, piece_other, down_part, low_parts = lax.optimization_barrier(
         (first, piece_other, down_part, low_parts)
     )
+    features = jnp.transpose(x.reshape(sequences, rows, UNITS, SHARD), (2, 1, 0, 3))
+    features = features.reshape(UNITS, rows, sequences * SHARD)
+    features, first = lax.optimization_barrier((features, first))
+    x_parts = swap(features).reshape(HALF, sequences * SHARD)
 
     steps = RATIO // BATCH
     head_block = pl.BlockSpec((HALF, BATCH * HEAD), lambda h: (0, h))
@@ -427,7 +414,7 @@
 
     pieces = width // HEAD + KV
     peers = PLANES * weight_devices
-    share = RANK
+    share = -(-pieces * RANK // peers)
     sums = call(
         adapter_kernel,
         4 * tokens * width * RANK,
@@ -443,7 +430,7 @@
         out_shape=pltpu.HBM((peers * share, HEAD), F32),
         name="adapter",
     )(third, x_rows, low_parts, up_weight)
-    v_prev, sums = lax.optimization_barrier((v_prev, sums))
+    v_late, sums = lax.optimization_barrier((v_unit, sums))
 
     def among_peers(block):
         return lax.all_to_all(
@@ -487,7 +474,7 @@
         first,
         first,
         first,
-        v_unit,
+        v_late,
         v_prev,
     )
     returning = jnp.concatenate(

time: 201 us -> 196 us (0.975)
  waiting for transfers between devices: 56.7 us -> 33.7 us
  local copies, waits for them, and re-layouts: 4.22 us -> 16.7 us
  starting transfers between devices: 58.2 us -> 67.4 us
  blocking collectives: 40.6 us -> 37.7 us
    all_to_all x2, starting transfers between devices: 17.1 us -> 26.9 us  [among_peers(): lax.all_to_all(block, both, split_axis=0, concat_axis=0, axis_index_group...]
    ppermute x1, waiting for transfers between devices: 7.3 us -> 0.01 us  [body(): v_prev = lax.ppermute(v_unit, both, from_before)]
    transpose x0 -> x2, local copies, waits for them, and re-layouts: none -> 5.55 us  [body(): jnp.transpose(x.reshape(sequences, rows, UNITS, SHARD), (2, 1, 0, 3))]
    ppermute x1, waiting for transfers between devices: 5.13 us -> 0.01 us  [body(): piece_other = lax.ppermute(piece, 'seq', next_plane)]
    all_to_all x2, waiting for transfers between devices: 19.3 us -> 14.9 us  [swap(): lax.all_to_all(block, 'seq', split_axis=0, concat_axis=0, axis_index_grou...]
    ppermute x1, waiting for transfers between devices: 4.25 us -> 0.01 us  [body(): piece = lax.ppermute(piece, both, turned)]
    all_to_all x2, starting transfers between devices: 21.7 us -> 18.7 us  [swap(): lax.all_to_all(block, 'seq', split_axis=0, concat_axis=0, axis_index_grou...]
    all_to_all x2, blocking collectives: 40.6 us -> 37.7 us  [swap(): lax.all_to_all(block, 'seq', split_axis=0, concat_axis=0, axis_index_grou...]
  transfers between devices with their start and end apart: 10 -> 10, of which waited for: 8 -> 5; matrix products, arithmetic and copies ran while one was open for 2% -> 7% of each run, Pallas kernels for 11% -> 16%
where the time goes in v5:
time: 196 us; the launch traced here: 195 us
  starting transfers between devices  67.4 us (34%)
  blocking collectives  37.7 us (19%)
  Pallas kernels  34.5 us (18%)
  waiting for transfers between devices  33.7 us (17%)
  local copies, waits for them, and re-layouts  16.7 us (9%)
  other arithmetic  2.41 us (1%)
    all_to_all x2, blocking collectives, swap(): lax.all_to_all(block, 'seq', split_axis=0, concat_axis=0, axis_index_grou...  37.7 us
    all_to_all x2, starting transfers between devices, among_peers(): lax.all_to_all(block, both, split_axis=0, concat_axis=0, axis_index_group...  26.9 us
    all_to_all x2, starting transfers between devices, swap(): lax.all_to_all(block, 'seq', split_axis=0, concat_axis=0, axis_index_grou...  18.7 us
    all_to_all x2, waiting for transfers between devices, among_peers(): lax.all_to_all(block, both, split_axis=0, concat_axis=0, axis_index_group...  16.9 us
    all_to_all x2, waiting for transfers between devices, swap(): lax.all_to_all(block, 'seq', split_axis=0, concat_axis=0, axis_index_grou...  14.9 us
    pallas_call x1, Pallas kernels, body(): call(score_grad_kernel, 3 * product, 12 << 20, grid=(steps,), in_specs=[s...  12.1 us
    pallas_call x1, Pallas kernels, body(): call(weights_kernel, 2 * product, 10 << 20, grid=(steps,), in_specs=[smem...  9.94 us
    transpose x2, local copies, waits for them, and re-layouts, body(): jnp.transpose(x.reshape(sequences, rows, UNITS, SHARD), (2, 1, 0, 3))  5.55 us
  transfers between devices with their start and end apart: 10, of which 5 were waited for; matrix products, arithmetic and copies ran while one was open for 7% of the time, Pallas kernels for 16%

profile of v5, /device:TPU:1, one launch (start us, length us, event | category | flops | bytes accessed | tf_op | source)
XLA Modules:
  0.0 195.1 jit_solution(14225699190555093775)
XLA Ops:
  0.7 1.0 copy-done
  1.7 4.6 %collective-permute-start.1 = (bf16[256,512]{1,0:T(8,128)(2,1)S(1)}, bf16[256,512]{1,0:T(8,128)(2,1)S(1)}, u32[]{:S(2)}, u32[]{:S(2)}) collective-permute-start(bf16[256,512]{1,0:T(8,128)(2,1)S(1)} %constant_dynamic-slice_fusion.1), channel_id=1, source_target_pairs={{0,0},{8,1},{16,2},{24,3},{32,4},{40,5},{48,6},{56,7},{1,8},{9,9},... | collective-permute-start | bytes 786440 | tf_op jit(solution)/shard_map/ppermute | solution.py:302
  6.4 3.2 %collective-permute-start = (bf16[2,1,64,512]{3,2,1,0:T(8,128)(2,1)}, bf16[2,1,64,512]{3,2,1,0:T(8,128)(2,1)S(1)}, u32[]{:S(2)}, u32[]{:S(2)}) collective-permute-start(bf16[2,1,64,512]{3,2,1,0:T(8,128)(2,1)} %k_ref.1), channel_id=1, source_target_pairs={{0,64},{1,65},{2,66},{3,67},{4,68},{5,69},{6,70},{7,71},{8,72},{9,... | collective-permute-start | bytes 393224 | tf_op jit(solution)/shard_map/ppermute | solution.py:303
  9.6 2.7 %pack.1.packed_ref = bf16[8,64,2304]{2,1,0:T(8,128)(2,1)} custom-call(bf16[2,1,64,4096]{3,2,1,0:T(8,128)(2,1)} %q_ref.1, bf16[2,1,64,4096]{3,2,1,0:T(8,128)(2,1)} %do_ref.1), custom_call_target="tpu_custom_call" | custom-call | bytes 4194304 | tf_op jit(solution)/shard_map/pack/pallas_call | solution.py:308
  12.3 1.8 collective-permute-done.kb_ref
  14.9 14.5 %all-to-all-start = ((bf16[8,64,2304]{2,1,0:T(8,128)(2,1)}), bf16[8,64,2304]{2,1,0:T(8,128)(2,1)S(1)}, u32[]{:S(2)}, u32[]{:S(2)}) async-start(bf16[8,64,2304]{2,1,0:T(8,128)(2,1)} %pack_keys.1), calls=%async_computation | async-start | bytes 4718592 | tf_op jit(solution)/shard_map/all_to_all | solution.py:282
  29.3 2.6 %copy.21 = bf16[16,8,8,512]{3,2,1,0:T(8,128)(2,1)} copy(bf16[16,8,8,512]{3,1,2,0:T(8,128)(2,1)} %bitcast.49) | data formatting | bytes 2097152
  31.9 2.3 %bitcast_bitcast_fusion = bf16[8,64,2,512]{3,0,1,2:T(8,128)(2,1)} fusion(bf16[2,64,8,512]{3,2,1,0:T(8,128)(2,1)} %bitcast.51), kind=kLoop, calls=%fused_computation.2 | loop fusion | bytes 2097152 | tf_op jit(solution)/shard_map/transpose | solution.py:340
  34.2 1.9 collective-permute-start.2
  37.0 3.3 %copy.17 = bf16[8,64,2,512]{3,2,1,0:T(2,128)(2,1)} copy(bf16[8,64,2,512]{3,0,1,2:T(8,128)(2,1)} %bitcast_bitcast_fusion) | data formatting | bytes 2097152 | tf_op jit(solution)/shard_map/transpose | solution.py:340
  40.3 2.6 %reshape.80 = bf16[8,64,1024]{2,1,0:T(8,128)(2,1)} reshape(bf16[8,64,2,512]{3,2,1,0:T(2,128)(2,1)} %copy.17) | data formatting | bytes 2097152 | tf_op jit(solution)/shard_map/reshape | solution.py:341
  42.9 1.7 convolution_bitcast_fusion.low_ref
  44.6 13.7 %all-to-all-done = bf16[8,64,2304]{2,1,0:T(8,128)(2,1)S(1)} async-done(((bf16[8,64,2304]{2,1,0:T(8,128)(2,1)}), bf16[8,64,2304]{2,1,0:T(8,128)(2,1)S(1)}, u32[]{:S(2)}, u32[]{:S(2)}) %all-to-all-start) | async-done | bytes 2359328 | tf_op jit(solution)/shard_map/all_to_all | solution.py:282
  58.3 4.2 %all-to-all-start.1 = ((bf16[8,64,1024]{2,1,0:T(8,128)(2,1)}), bf16[8,64,1024]{2,1,0:T(8,128)(2,1)}, u32[]{:S(2)}, u32[]{:S(2)}) async-start(bf16[8,64,1024]{2,1,0:T(8,128)(2,1)} %reshape.80), calls=%async_computation.1 | async-start | bytes 2097152 | tf_op jit(solution)/shard_map/all_to_all | solution.py:282
  62.7 9.9 %weights.1 = (bf16[8,512,512]{2,1,0:T(8,128)(2,1)}, bf16[8,512,512]{2,1,0:T(8,128)(2,1)}, f32[512,128]{1,0:T(8,128)}, bf16[512,128]{1,0:T(8,128)(2,1)}) custom-call(s32[8]{0:T(128)S(1)} %broadcast_select_fusion.flags, bf16[512,2304]{1,0:T(8,128)(2,1)S(1)} %bitcast.41, bf16[512,2304]{1,0:T(8,128)(2,1)S(1)} %bitcast.42, bf16[512,2304]{1,0:T(8,128)(2,1)S(1)} %bitcast.43, ...), custom_call_target="tpu_custom_call" | custom-call | flops 1610612736 | bytes 10485760 | tf_op jit(solution)/shard_map/weights/pallas_call | solution.py:358
  72.6 3.6 %collective-permute-start.3 = (bf16[512,128]{1,0:T(8,128)(2,1)}, bf16[512,128]{1,0:T(8,128)(2,1)}, u32[]{:S(2)}, u32[]{:S(2)}) collective-permute-start(bf16[512,128]{1,0:T(8,128)(2,1)} %get-tuple-element.35), channel_id=1, source_target_pairs={{64,0},{65,1},{66,2},{67,3},{68,4},{69,5},{70,6},{71,7},{72,8},{73... | collective-permute-start | bytes 393224 | tf_op jit(solution)/shard_map/ppermute | solution.py:372
  76.2 1.2 all-to-all-done.1
  77.5 4.4 %values.1.parts_ref = bf16[8,64,1152]{2,1,0:T(8,128)(2,1)} custom-call(s32[1]{0:T(128)} %bitcast.5.odd, bf16[512,1024]{1,0:T(8,128)(2,1)} %bitcast.6.x_ref, bf16[256,512]{1,0:T(8,128)(2,1)S(1)} %collective-permute-done.1.mine_ref, bf16[256,512]{1,0:T(8,128)(2,1)S(1)} %collective-permute-done.2.other_ref, bf16[512,8]{1,0:T(8,128)(2,1)S(1)} %copy.20.down_ref, ...), custom_call_target="tpu_custom_call" | custom-call | flops 536870912 | bytes 4194304 | tf_op jit(solution)/shard_map/values/pallas_call | solution.py:374
  81.8 1.6 merge.1
  83.4 16.1 %all_to_all.41.parts_ref.dv_ref = bf16[8,64,1152]{2,1,0:T(8,128)(2,1)S(1)} all-to-all(bf16[8,64,1152]{2,1,0:T(8,128)(2,1)} %merge.1), channel_id=1, replica_groups={{0,8,16,24,32,40,48,56},{64,72,80,88,96,104,112,120},{128,136,144,152,1..., dimensions={0} | all-to-all | bytes 2359296 | tf_op jit(solution)/shard_map/all_to_all | solution.py:282
  100.3 4.7 %collective-permute-start.4 = (bf16[512,128]{1,0:T(8,128)(2,1)}, bf16[512,128]{1,0:T(8,128)(2,1)S(1)}, u32[]{:S(2)}, u32[]{:S(2)}) collective-permute-start(bf16[512,128]{1,0:T(8,128)(2,1)} %values_sum.1.v_ref), channel_id=1, source_target_pairs={{0,64},{1,65},{2,66},{3,67},{4,68},{5,69},{6,70},{7,71},{8,72},{9,... | collective-permute-start | bytes 393224 | tf_op jit(solution)/shard_map/ppermute | solution.py:413
  105.0 1.2 adapter.1
  106.2 1.7 all_to_all.29
  107.9 16.8 %all-to-all-start.3 = ((f32[64,5,128]{2,1,0:T(8,128)}), f32[64,5,128]{2,1,0:T(8,128)S(1)}, u32[]{:S(2)}, u32[]{:S(2)}) async-start(f32[64,5,128]{2,1,0:T(8,128)} %all_to_all.29), calls=%async_computation.3 | async-start | bytes 524288 | tf_op jit(solution)/shard_map/all_to_all | solution.py:436
  124.7 12.1 %score_grad.1 = (bf16[512,1024]{1,0:T(8,128)(2,1)}, bf16[512,128]{1,0:T(8,128)(2,1)}, bf16[512,128]{1,0:T(8,128)(2,1)}) custom-call(s32[8]{0:T(128)S(1)} %copy-done.7, bf16[8,512,512]{2,1,0:T(8,128)(2,1)} %get-tuple-element.29.own_ref, bf16[8,512,512]{2,1,0:T(8,128)(2,1)} %get-tuple-element.30.prev_ref, bf16[512,2304]{1,0:T(8,128)(2,1)S(1)} %bitcast.45, ...), custom_call_target="tpu_custom_call" | custom-call | flops 2415919104 | bytes 12582912 | tf_op jit(solution)/shard_map/score_grad/pallas_call | solution.py:445
  136.8 3.5 %all-to-all-done.3 = f32[64,5,128]{2,1,0:T(8,128)S(1)} async-done(((f32[64,5,128]{2,1,0:T(8,128)}), f32[64,5,128]{2,1,0:T(8,128)S(1)}, u32[]{:S(2)}, u32[]{:S(2)}) %all-to-all-start.3) | async-done | bytes 163872 | tf_op jit(solution)/shard_map/all_to_all | solution.py:436
  140.4 1.5 pad_maximum_fusion
  141.9 21.6 %all_to_all.42.in_ref = bf16[8,64,1408]{2,1,0:T(8,128)(2,1)S(1)} all-to-all(bf16[8,64,1408]{2,1,0:T(8,128)(2,1)S(1)} %pad_maximum_fusion), channel_id=1, replica_groups={{0,8,16,24,32,40,48,56},{64,72,80,88,96,104,112,120},{128,136,144,152,1..., dimensions={0} | all-to-all | bytes 2883584 | tf_op jit(solution)/shard_map/all_to_all | solution.py:282
  163.7 3.8 %collective-permute-start.5 = (bf16[8,64,128]{2,1,0:T(8,128)(2,1)S(1)}, bf16[8,64,128]{2,1,0:T(8,128)(2,1)S(1)}, u32[]{:S(2)}, u32[]{:S(2)}) collective-permute-start(bf16[8,64,128]{2,1,0:T(8,128)(2,1)S(1)} %get-tuple-element.44), channel_id=1, source_target_pairs={{64,0},{65,1},{66,2},{67,3},{68,4},{69,5},{70,6},{71,7},{72,8},{73... | collective-permute-start | bytes 393224 | tf_op jit(solution)/shard_map/ppermute | solution.py:513
  168.2 10.0 %all-to-all-start.5 = ((f32[64,5,128]{2,1,0:T(8,128)}), f32[64,5,128]{2,1,0:T(8,128)S(1)}, u32[]{:S(2)}, u32[]{:S(2)}) async-start(f32[64,5,128]{2,1,0:T(8,128)} %all_to_all.32), calls=%async_computation.5 | async-start | bytes 524288 | tf_op jit(solution)/shard_map/all_to_all | solution.py:436
  178.2 1.1 unpack.1
  180.4 13.4 %all-to-all-done.5 = f32[64,5,128]{2,1,0:T(8,128)S(1)} async-done(((f32[64,5,128]{2,1,0:T(8,128)}), f32[64,5,128]{2,1,0:T(8,128)S(1)}, u32[]{:S(2)}, u32[]{:S(2)}) %all-to-all-start.5) | async-done | bytes 163872 | tf_op jit(solution)/shard_map/all_to_all | solution.py:436
  (45 shorter events, 5.8 us)
Async XLA Ops:
  0.6 1.0 copy-start
  1.7 12.4 %copy-start.4 = (bf16[2,1,64,512]{3,2,1,0:T(8,128)(2,1)S(1)}, bf16[2,1,64,512]{3,2,1,0:T(8,128)(2,1)}, u32[]{:S(2)}) copy-start(bf16[2,1,64,512]{3,2,1,0:T(8,128)(2,1)} %k_ref.1) | copy-start | bytes 393220
  1.7 13.1 %collective-permute-start.1 = (bf16[256,512]{1,0:T(8,128)(2,1)S(1)}, bf16[256,512]{1,0:T(8,128)(2,1)S(1)}, u32[]{:S(2)}, u32[]{:S(2)}) collective-permute-start(bf16[256,512]{1,0:T(8,128)(2,1)S(1)} %constant_dynamic-slice_fusion.1), channel_id=1, source_target_pairs={{0,0},{8,1},{16,2},{24,3},{32,4},{40,5},{48,6},{56,7},{1,8},{9,9},... | collective-permute-start | bytes 786440 | tf_op jit(solution)/shard_map/ppermute | solution.py:302
  6.4 7.7 %collective-permute-start = (bf16[2,1,64,512]{3,2,1,0:T(8,128)(2,1)}, bf16[2,1,64,512]{3,2,1,0:T(8,128)(2,1)S(1)}, u32[]{:S(2)}, u32[]{:S(2)}) collective-permute-start(bf16[2,1,64,512]{3,2,1,0:T(8,128)(2,1)} %k_ref.1), channel_id=1, source_target_pairs={{0,64},{1,65},{2,66},{3,67},{4,68},{5,69},{6,70},{7,71},{8,72},{9,... | collective-permute-start | bytes 393224 | tf_op jit(solution)/shard_map/ppermute | solution.py:303
  14.9 43.4 %all-to-all-start = ((bf16[8,64,2304]{2,1,0:T(8,128)(2,1)}), bf16[8,64,2304]{2,1,0:T(8,128)(2,1)S(1)}, u32[]{:S(2)}, u32[]{:S(2)}) async-start(bf16[8,64,2304]{2,1,0:T(8,128)(2,1)} %pack_keys.1), calls=%async_computation | async-start | bytes 4718592 | tf_op jit(solution)/shard_map/all_to_all | solution.py:282
  34.2 10.4 %collective-permute-start.2 = (bf16[256,512]{1,0:T(8,128)(2,1)S(1)}, bf16[256,512]{1,0:T(8,128)(2,1)S(1)}, u32[]{:S(2)}, u32[]{:S(2)}) collective-permute-start(bf16[256,512]{1,0:T(8,128)(2,1)S(1)} %collective-permute-done.1.mine_ref), channel_id=1, source_target_pairs={{0,64},{8,72},{16,80},{24,88},{32,96},{40,104},{48,112},{56,120},{... | collective-permute-start | bytes 786440 | tf_op jit(solution)/shard_map/ppermute | solution.py:335
  40.3 22.3 %copy-start.8 = (s32[32]{0:T(128)S(1)}, s32[32]{0:T(128)}, u32[]{:S(2)}) copy-start(s32[32]{0:T(128)} %param.15) | copy-start | bytes 388
  58.3 19.2 %all-to-all-start.1 = ((bf16[8,64,1024]{2,1,0:T(8,128)(2,1)}), bf16[8,64,1024]{2,1,0:T(8,128)(2,1)}, u32[]{:S(2)}, u32[]{:S(2)}) async-start(bf16[8,64,1024]{2,1,0:T(8,128)(2,1)} %reshape.80), calls=%async_computation.1 | async-start | bytes 2097152 | tf_op jit(solution)/shard_map/all_to_all | solution.py:282
  62.7 9.9 %copy-start.6 = (s32[8]{0:T(128)}, s32[8]{0:T(128)S(1)}, u32[]{:S(2)}) copy-start(s32[8]{0:T(128)S(1)} %broadcast_select_fusion.flags) | copy-start | bytes 100
  62.7 14.8 %copy-start.5 = (bf16[8,512]{1,0:T(8,128)(2,1)S(1)}, bf16[8,512]{1,0:T(8,128)(2,1)}, u32[]{:S(2)}) copy-start(bf16[8,512]{1,0:T(8,128)(2,1)} %up_ref.3) | copy-start | bytes 24580
  72.6 9.2 %collective-permute-start.3 = (bf16[512,128]{1,0:T(8,128)(2,1)}, bf16[512,128]{1,0:T(8,128)(2,1)}, u32[]{:S(2)}, u32[]{:S(2)}) collective-permute-start(bf16[512,128]{1,0:T(8,128)(2,1)} %get-tuple-element.35), channel_id=1, source_target_pairs={{64,0},{65,1},{66,2},{67,3},{68,4},{69,5},{70,6},{71,7},{72,8},{73... | collective-permute-start | bytes 393224 | tf_op jit(solution)/shard_map/ppermute | solution.py:372
  77.5 4.4 %copy-start.3 = (f32[512,128]{1,0:T(8,128)S(1)}, f32[512,128]{1,0:T(8,128)}, u32[]{:S(2)}) copy-start(f32[512,128]{1,0:T(8,128)} %get-tuple-element.34.own_ref) | copy-start | bytes 786436
  83.4 21.6 %copy-start.1 = (bf16[2,1,64,4096]{3,2,1,0:T(8,128)(2,1)S(1)}, bf16[2,1,64,4096]{3,2,1,0:T(8,128)(2,1)}, u32[]{:S(2)}) copy-start(bf16[2,1,64,4096]{3,2,1,0:T(8,128)(2,1)} %param.8) | copy-start | bytes 3145732
  99.5 25.2 %copy-start.7 = (s32[8]{0:T(128)S(1)}, s32[8]{0:T(128)}, u32[]{:S(2)}) copy-start(s32[8]{0:T(128)} %copy-done.6) | copy-start | bytes 100
  100.3 24.4 %copy-start.2 = (bf16[512,128]{1,0:T(8,128)(2,1)S(1)}, bf16[512,128]{1,0:T(8,128)(2,1)}, u32[]{:S(2)}) copy-start(bf16[512,128]{1,0:T(8,128)(2,1)} %values_sum.1.v_ref) | copy-start | bytes 393220
  100.3 24.4 %collective-permute-start.4 = (bf16[512,128]{1,0:T(8,128)(2,1)}, bf16[512,128]{1,0:T(8,128)(2,1)S(1)}, u32[]{:S(2)}, u32[]{:S(2)}) collective-permute-start(bf16[512,128]{1,0:T(8,128)(2,1)} %values_sum.1.v_ref), channel_id=1, source_target_pairs={{0,64},{1,65},{2,66},{3,67},{4,68},{5,69},{6,70},{7,71},{8,72},{9,... | collective-permute-start | bytes 393224 | tf_op jit(solution)/shard_map/ppermute | solution.py:413
  107.9 32.4 %all-to-all-start.3 = ((f32[64,5,128]{2,1,0:T(8,128)}), f32[64,5,128]{2,1,0:T(8,128)S(1)}, u32[]{:S(2)}, u32[]{:S(2)}) async-start(f32[64,5,128]{2,1,0:T(8,128)} %all_to_all.29), calls=%async_computation.3 | async-start | bytes 524288 | tf_op jit(solution)/shard_map/all_to_all | solution.py:436
  163.7 15.7 %collective-permute-start.5 = (bf16[8,64,128]{2,1,0:T(8,128)(2,1)S(1)}, bf16[8,64,128]{2,1,0:T(8,128)(2,1)S(1)}, u32[]{:S(2)}, u32[]{:S(2)}) collective-permute-start(bf16[8,64,128]{2,1,0:T(8,128)(2,1)S(1)} %get-tuple-element.44), channel_id=1, source_target_pairs={{64,0},{65,1},{66,2},{67,3},{68,4},{69,5},{70,6},{71,7},{72,8},{73... | collective-permute-start | bytes 393224 | tf_op jit(solution)/shard_map/ppermute | solution.py:513
  168.2 25.6 %all-to-all-start.5 = ((f32[64,5,128]{2,1,0:T(8,128)}), f32[64,5,128]{2,1,0:T(8,128)S(1)}, u32[]{:S(2)}, u32[]{:S(2)}) async-start(f32[64,5,128]{2,1,0:T(8,128)} %all_to_all.32), calls=%async_computation.5 | async-start | bytes 524288 | tf_op jit(solution)/shard_map/all_to_all | solution.py:436
